TPU v7x, 32 devices: a whole 2x2x4 slice. The times are simulated.
32 devices in a mesh: dp: 4 (over z), expert: 4 (over x, core), mp: 2 (over y).
Axes of the slice: x: 2, y: 2, z: 4, core: 2. Of those that a mesh axis runs over, the one named last changes fastest.
Arguments:
- x_rows: bfloat16 [256, 3072], P(('dp', 'expert')), may hold values from -6 to 6, as said below
- dy_rows: bfloat16 [256, 3072], P(('dp', 'expert')), may hold values from -1.5 to 1.5, as said below
- w_in: bfloat16 [4, 3072, 2, 672], P('expert', None, None, 'mp'), may hold values from -0.109375 to 0.109375
- w_out: bfloat16 [4, 3072, 672], P('expert', None, 'mp'), may hold values from -0.25 to 0.25
- counts: int32 [16, 4], P(('dp', 'expert')), may hold values from 0 to 4, as said below
- assign: int32 [64, 2], P(('dp', 'expert')), may hold values from 0 to 3, as said below
Outputs:
- grad_w_in: bfloat16 [4, 3072, 2, 672], P('expert', 'dp', None, 'mp')
- grad_w_out: bfloat16 [4, 3072, 672], P('expert', 'dp', 'mp')
- grad_tokens: bfloat16 [64, 3072], P(('dp', 'expert'), 'mp')
Inputs may be any that keep to these rules, and one draw needn't show every extreme that they name: counts[(g, u), s] is the number of tokens of owner s of group g that name expert e = u // 1 in assign, equal for the slices of one expert; it is at most 4, and 4 is reached in every group. `assign`: each token names 2 different experts; no owner names one expert for more than 4 of its tokens. `x_rows`: the 1 slices of one expert in one group keep equal copies of the same rows. `dy_rows`: the 1 slices of one expert in one group keep equal copies of the same rows.
All inputs are finite; a program needn't handle non-finite values.
Results may differ from a plain program's by a relative error of at most 0.018.
Values may be sent and summed in bfloat16 or wider, within the bound.
No kernel may reach another device: no remote copies, remote signals or barrier semaphores. Data moves between devices by JAX's collectives and lax.ppermute only.
A program may use at most 64 MiB of HBM per device.

v0:
```python
import jax
import jax.numpy as jnp
from jax import lax
from jax.sharding import PartitionSpec as P

LAYER_EXPERTS = 16


def block_grads(x_block, dy_block, w_flat, w_down, live_mask):
    hidden_units = w_down.shape[1]
    preact = jnp.dot(x_block, w_flat, preferred_element_type=jnp.float32)
    gate_pre = preact[:, :hidden_units]
    up_pre = preact[:, hidden_units:]
    sigmoid_gate = jax.nn.sigmoid(gate_pre)
    hidden = (live_mask * gate_pre * sigmoid_gate * up_pre).astype(jnp.bfloat16)
    grad_hidden = jnp.dot(dy_block, w_down, preferred_element_type=jnp.float32)
    grad_gate = (
        live_mask * grad_hidden * up_pre * sigmoid_gate * (1.0 + gate_pre * (1.0 - sigmoid_gate))
    )
    grad_up = live_mask * grad_hidden * gate_pre * sigmoid_gate
    grad_pre = jnp.concatenate([grad_gate, grad_up], axis=1).astype(jnp.bfloat16)
    dx_partial = lax.dot_general(
        grad_pre, w_flat, (((1,), (1,)), ((), ())), preferred_element_type=jnp.float32
    )
    return (jnp.concatenate([grad_pre, hidden], axis=1), dx_partial)


def per_device(x_rows, dy_rows, w_in, w_out, counts, assign):
    slot_total, model_width = x_rows.shape
    hidden_units = w_out.shape[2]
    w_flat = w_in[0].reshape(model_width, 2 * hidden_units)
    w_down = w_out[0]
    per_source = counts[0]
    live_rows = jnp.sum(per_source)
    slot_index = jnp.arange(slot_total, dtype=jnp.int32)
    live_mask = (slot_index < live_rows).astype(jnp.float32)[:, None]
    block_acts, block_partial = block_grads(x_rows, dy_rows, w_flat, w_down, live_mask)
    summed_rows = lax.psum_scatter(
        block_partial.astype(jnp.bfloat16), "mp", scatter_dimension=1, tiled=True
    )
    owners = per_source.shape[0]
    capacity = slot_total // owners
    offsets = jnp.cumsum(per_source) - per_source
    lane_index = jnp.arange(capacity, dtype=jnp.int32)
    wanted = jnp.clip(offsets[:, None] + lane_index[None, :], 0, slot_total - 1).reshape(-1)
    present = lane_index[None, :] < per_source[:, None]
    source_rows = jnp.take(summed_rows, wanted, axis=0).reshape(owners, capacity, -1)
    outgoing = jnp.where(present[:, :, None], source_rows, jnp.zeros((), jnp.bfloat16))
    incoming = lax.all_to_all(outgoing, "expert", split_axis=0, concat_axis=0, tiled=True)
    units = lax.axis_size("expert")
    slices = units // min(LAYER_EXPERTS, units)
    tokens, route_width = assign.shape
    flat_routes = assign.reshape(-1)
    route_count = flat_routes.shape[0]
    token_of = jnp.arange(route_count, dtype=jnp.int32) // route_width
    same_expert = flat_routes[:, None] == flat_routes[None, :]
    earlier = token_of[None, :] < token_of[:, None]
    route_rank = jnp.sum((same_expert & earlier).astype(jnp.int32), axis=1)
    columns = jnp.arange(units * capacity, dtype=jnp.int32)
    column_expert = columns // capacity // slices
    column_rank = columns % capacity
    hits = (column_expert[None, :] == flat_routes[:, None]) & (
        column_rank[None, :] == route_rank[:, None]
    )
    selector = jnp.sum(hits.astype(jnp.float32).reshape(tokens, route_width, -1), axis=1).astype(
        jnp.bfloat16
    )
    grad_tokens = jnp.dot(
        selector, incoming.reshape(units * capacity, -1), preferred_element_type=jnp.float32
    ).astype(jnp.bfloat16)
    quarter = model_width // lax.axis_size("dp")
    act_column = jnp.arange(3 * hidden_units, dtype=jnp.int32)[None, :]
    zero_value = jnp.zeros((), jnp.bfloat16)
    stacked_acts = jnp.concatenate(
        [
            jnp.where(act_column < 2 * hidden_units, block_acts, zero_value),
            jnp.where(act_column >= 2 * hidden_units, block_acts, zero_value),
        ],
        axis=0,
    )
    stacked_cols = jnp.concatenate([x_rows, dy_rows], axis=0)
    summed_terms = lax.psum_scatter(
        lax.dot_general(
            stacked_cols, stacked_acts, (((0,), (0,)), ((), ())), preferred_element_type=jnp.float32
        ).astype(jnp.bfloat16),
        "dp",
        scatter_dimension=0,
        tiled=True,
    ).astype(jnp.float32)
    grad_w_in = (
        summed_terms[:, : 2 * hidden_units]
        .astype(jnp.bfloat16)
        .reshape(1, quarter, 2, hidden_units)
    )
    grad_w_out = (
        summed_terms[:, 2 * hidden_units :].astype(jnp.bfloat16).reshape(1, quarter, hidden_units)
    )
    return (grad_w_in, grad_w_out, grad_tokens)


def solution(mesh):
    return jax.shard_map(
        per_device,
        mesh=mesh,
        in_specs=(
            P(("dp", "expert"), None),
            P(("dp", "expert"), None),
            P("expert", None, None, "mp"),
            P("expert", None, "mp"),
            P(("dp", "expert"), None),
            P(("dp", "expert"), None),
        ),
        out_specs=(
            P("expert", "dp", None, "mp"),
            P("expert", "dp", "mp"),
            P(("dp", "expert"), "mp"),
        ),
        check_vma=False,
    )
```

profile of v0, /device:TPU:0, one launch (start us, length us, event | category | flops | bytes accessed | tf_op | source)
XLA Modules:
  0.0 150.3 jit_solution(2793947535895062636)
XLA Ops:
  7.2 0.0 copy-start
  7.2 0.0 copy-start.2
  7.2 0.0 reduce-scatter.5.cloned.1.call-start
  7.2 1.4 reduce_sum.27
  8.7 0.0 copy-start.1
  8.7 0.8 compare_convert_fusion
  9.5 3.5 %fusion.18 = f32[16,672]{1,0:T(8,128)S(1)} fusion(bf16[16,3072]{1,0:T(8,128)(2,1)} %param.6, bf16[3072,672]{0,1:T(8,128)(2,1)} %bitcast.24), kind=kOutput, calls=%fused_computation.50 | convolution fusion | flops 66060288 | bytes 4270080 | tf_op jit(solution)/shard_map/dot_general | solution.py:11
  13.0 0.0 copy-done
  13.0 0.0 copy-done.2
  13.0 0.0 copy-start.3
  13.0 0.7 multiply_convert_fusion.2
  13.7 0.0 copy-done.1
  13.7 1.3 convolution_convert_fusion.1
  15.0 0.0 reduce-scatter.5.cloned.1.call-update
  15.0 0.0 reduce-scatter.3.cloned.1.call-start
  15.1 0.1 broadcast_select_fusion.1
  15.2 0.0 copy-done.3
  15.2 4.4 %convolution_convert_fusion = bf16[3072,1008]{0,1:T(8,128)(2,1)} fusion(bf16[16,3072]{1,0:T(8,128)(2,1)S(1)} %copy-done.2, bf16[16,3072]{1,0:T(8,128)(2,1)S(1)} %copy-done.3, bf16[16,1008]{1,0:T(8,128)(2,1)S(1)} %get-tuple-element.7, bf16[16,1008]{1,0:T(8,128)(2,1)S(1)} %get-tuple-element.6), kind=kOutput, calls=%fused_computation.1 | convolution fusion | flops 201799680 | bytes 6454272 | tf_op jit(solution)/shard_map/dot_general | solution.py:83
  19.6 0.0 copy-start.5
  19.6 0.0 copy-start.4
  19.6 0.0 reduce-scatter.3.cloned.1.call-update
  19.6 0.6 copy-done.5
  20.3 0.2 reduce-window.8
  20.5 0.1 add_clamp_fusion
  20.5 0.1 min.12
  20.6 0.0 copy-done.4
  20.6 0.1 copy.13
  20.7 0.1 eq.51
  20.8 0.2 convert_reduce_fusion.1
  21.0 0.1 eq.55
  21.1 0.1 copy.14
  21.2 0.1 iota_compare_fusion.2
  21.3 6.6 %reduce-scatter.5.cloned.1.call-done = bf16[16,1536]{1,0:T(8,128)(2,1)} async-done(((bf16[16,3072]{1,0:T(8,128)(2,1)}), bf16[16,1536]{1,0:T(8,128)(2,1)}) %reduce-scatter.5.cloned.1.call-update) | async-done | bytes 49168 | tf_op jit(solution)/shard_map/reduce_scatter | solution.py:38
  27.9 1.4 gather_fusion
  29.3 0.7 select_select_fusion
  30.1 3.3 %all-to-all-start = ((bf16[4,4,1536]{2,1,0:T(4,128)(2,1)}), bf16[4,4,1536]{2,1,0:T(4,128)(2,1)S(1)}, u32[]{:S(2)}, u32[]{:S(2)}) async-start(bf16[4,4,1536]{2,1,0:T(4,128)(2,1)} %select_select_fusion), calls=%async_computation.2 | async-start | bytes 98304 | tf_op jit(solution)/shard_map/all_to_all | solution.py:49
  33.3 0.1 convert_reduce_fusion
  33.4 3.9 %all-to-all-done = bf16[4,4,1536]{2,1,0:T(4,128)(2,1)S(1)} async-done(((bf16[4,4,1536]{2,1,0:T(4,128)(2,1)}), bf16[4,4,1536]{2,1,0:T(4,128)(2,1)S(1)}, u32[]{:S(2)}, u32[]{:S(2)}) %all-to-all-start) | async-done | bytes 49184 | tf_op jit(solution)/shard_map/all_to_all | solution.py:49
  37.4 0.7 convolution_convert_fusion.2
  38.1 101.3 %reduce-scatter.3.cloned.1.call-done = bf16[768,1008]{0,1:T(8,128)(2,1)} async-done(((bf16[3072,1008]{0,1:T(8,128)(2,1)}), bf16[768,1008]{0,1:T(8,128)(2,1)}) %reduce-scatter.3.cloned.1.call-update) | async-done | bytes 1548304 | tf_op jit(solution)/shard_map/reduce_scatter | solution.py:82
  139.4 1.9 %slice_bitcast_fusion = bf16[1,768,336]{1,2,0:T(8,128)(2,1)} fusion(bf16[768,1008]{0,1:T(8,128)(2,1)} %reduce-scatter.3.cloned.1.call-done), kind=kLoop, calls=%fused_computation.7 | loop fusion | bytes 1032192 | tf_op jit(solution)/shard_map/reshape | solution.py:96
  141.2 2.2 %slice.22 = bf16[768,672]{0,1:T(8,128)(2,1)} slice(bf16[768,1008]{0,1:T(8,128)(2,1)} %reduce-scatter.3.cloned.1.call-done), slice={[0:768], [0:672]} | slice | bytes 2064384 | tf_op jit(solution)/shard_map/slice | solution.py:91
  (8 shorter events, 0.1 us)
Async XLA Ops:
  7.2 5.8 %copy-start = (bf16[1,3072,336]{1,2,0:T(8,128)(2,1)S(1)}, bf16[1,3072,336]{1,2,0:T(8,128)(2,1)}, u32[]{:S(2)}) copy-start(bf16[1,3072,336]{1,2,0:T(8,128)(2,1)} %param.9) | copy-start | bytes 6193156
  7.2 5.8 %copy-start.2 = (bf16[16,3072]{1,0:T(8,128)(2,1)S(1)}, bf16[16,3072]{1,0:T(8,128)(2,1)}, u32[]{:S(2)}) copy-start(bf16[16,3072]{1,0:T(8,128)(2,1)} %param.7) | copy-start | bytes 294916
  7.2 20.7 %reduce-scatter.5.cloned.1.call-start = ((), (), s32[]{:S(2)}) async-start(), calls=%async_computation.4 | async-start | bytes 147456 | tf_op jit(solution)/shard_map/reduce_scatter | solution.py:38
  8.7 5.0 %copy-start.1 = (bf16[1,3072,2,336]{1,3,2,0:T(8,128)(2,1)S(1)}, bf16[1,3072,2,336]{1,3,2,0:T(8,128)(2,1)}, u32[]{:S(2)}) copy-start(bf16[1,3072,2,336]{1,3,2,0:T(8,128)(2,1)} %param.8) | copy-start | bytes 12386308
  13.0 2.2 %copy-start.3 = (bf16[16,3072]{1,0:T(8,128)(2,1)S(1)}, bf16[16,3072]{1,0:T(8,128)(2,1)}, u32[]{:S(2)}) copy-start(bf16[16,3072]{1,0:T(8,128)(2,1)} %param.6) | copy-start | bytes 294916
  15.0 124.3 %reduce-scatter.3.cloned.1.call-start = ((), (), s32[]{:S(2)}) async-start(), calls=%async_computation.3 | async-start | bytes 7741440 | tf_op jit(solution)/shard_map/reduce_scatter | solution.py:82
  19.6 0.7 copy-start.5
  19.6 1.0 copy-start.4
  30.1 7.3 %all-to-all-start = ((bf16[4,4,1536]{2,1,0:T(4,128)(2,1)}), bf16[4,4,1536]{2,1,0:T(4,128)(2,1)S(1)}, u32[]{:S(2)}, u32[]{:S(2)}) async-start(bf16[4,4,1536]{2,1,0:T(4,128)(2,1)} %select_select_fusion), calls=%async_computation.2 | async-start | bytes 98304 | tf_op jit(solution)/shard_map/all_to_all | solution.py:49
Sparse Core Ops, SparseCore 0:
  15.2 12.6 reduce-scatter.4
  30.2 109.1 reduce-scatter.2
where the time goes:
time: 151 us; the launch traced here: 150 us
  waiting for transfers between devices  112 us (74%)
  between operations  14.2 us (9%)
  matrix products  10.6 us (7%)
  local copies, waits for them, and re-layouts  6.69 us (4%)
  other arithmetic  3.67 us (2%)
  starting transfers between devices  3.35 us (2%)
    reduce_scatter x1, waiting for transfers between devices, per_device(): lax.psum_scatter(lax.dot_general(stacked_cols, stacked_acts, (((0,), (0,)...  101 us
    reduce_scatter x1, waiting for transfers between devices, per_device(): lax.psum_scatter(block_partial.astype(jnp.bfloat16), 'mp', scatter_dimens...  6.6 us
    dot_general x1, matrix products, per_device(): lax.dot_general(stacked_cols, stacked_acts, (((0,), (0,)), ((), ())), pre...  4.42 us
    all_to_all x1, waiting for transfers between devices, per_device(): lax.all_to_all(outgoing, 'expert', split_axis=0, concat_axis=0, tiled=True)  3.91 us
    dot_general x1, matrix products, block_grads(): preact = jnp.dot(x_block, w_flat, preferred_element_type=jnp.float32)  3.5 us
    all_to_all x1, starting transfers between devices, per_device(): lax.all_to_all(outgoing, 'expert', split_axis=0, concat_axis=0, tiled=True)  3.27 us
  transfers between devices with their start and end apart: 3, of which 3 were waited for; matrix products, arithmetic and copies ran while one was open for 6% of the time, Pallas kernels for 0%

commit v1 on v0

v1 whole, which is shorter than its diff:
```python
import jax
import jax.numpy as jnp
from jax import lax
from jax.sharding import PartitionSpec as P

LAYER_EXPERTS = 16
BF16 = jnp.bfloat16
F32 = jnp.float32


def local_grads(x_rows, dy_rows, w_flat, w_down, live_mask, pick):
    hidden_units = w_down.shape[0]
    contract_last = (((1,), (1,)), ((), ()))
    preact = lax.dot_general(x_rows, w_flat, contract_last, preferred_element_type=F32)
    gate_pre = preact[:, :hidden_units]
    up_pre = preact[:, hidden_units:]
    sigmoid_gate = jax.nn.sigmoid(gate_pre)
    hidden = (live_mask * gate_pre * sigmoid_gate * up_pre).astype(BF16)
    grad_hidden = lax.dot_general(dy_rows, w_down, contract_last, preferred_element_type=F32)
    grad_gate = (
        live_mask * grad_hidden * up_pre * sigmoid_gate * (1.0 + gate_pre * (1.0 - sigmoid_gate))
    )
    grad_up = live_mask * grad_hidden * gate_pre * sigmoid_gate
    grad_pre = jnp.concatenate([grad_gate, grad_up], axis=1).astype(BF16)
    picked = jnp.dot(pick, grad_pre, preferred_element_type=F32).astype(BF16)
    row_parts = jnp.dot(picked, w_flat, preferred_element_type=F32).astype(BF16)
    return jnp.concatenate([grad_pre, hidden], axis=1), row_parts


def pick_matrix(per_source, slot_total):
    owners = per_source.shape[0]
    capacity = slot_total // owners
    offsets = jnp.cumsum(per_source) - per_source
    lane = jnp.arange(capacity, dtype=jnp.int32)
    wanted = jnp.where(lane[None, :] < per_source[:, None], offsets[:, None] + lane[None, :], -1)
    slots = jnp.arange(slot_total, dtype=jnp.int32)
    return (wanted.reshape(-1)[:, None] == slots[None, :]).astype(BF16)


def token_selector(assign, units, parts, capacity):
    slices = units // min(LAYER_EXPERTS, units)
    tokens, route_width = assign.shape
    flat_routes = assign.reshape(-1)
    token_of = jnp.arange(flat_routes.shape[0], dtype=jnp.int32) // route_width
    same_expert = flat_routes[:, None] == flat_routes[None, :]
    earlier = token_of[None, :] < token_of[:, None]
    route_rank = jnp.sum((same_expert & earlier).astype(jnp.int32), axis=1)
    columns = jnp.arange(units * parts * capacity, dtype=jnp.int32)
    column_expert = columns // (capacity * parts * slices)
    column_rank = columns % capacity
    hits = (column_expert[None, :] == flat_routes[:, None]) & (
        column_rank[None, :] == route_rank[:, None]
    )
    return jnp.sum(hits.astype(F32).reshape(tokens, route_width, -1), axis=1).astype(BF16)


def per_device(x_rows, dy_rows, w_in, w_out, counts, assign):
    slot_total, model_width = x_rows.shape
    hidden_units = w_out.shape[2]
    groups = lax.axis_size("dp")
    units = lax.axis_size("expert")
    parts = lax.axis_size("mp")
    owners = counts.shape[1]
    capacity = slot_total // owners
    quarter = model_width // groups
    share = model_width // parts

    both = jnp.concatenate([x_rows, dy_rows], axis=0)
    both_all = lax.all_to_all(both, "dp", split_axis=1, concat_axis=0, tiled=True)
    both_all = both_all.reshape(groups, 2, slot_total, quarter)

    w_flat = jnp.transpose(w_in[0], (1, 2, 0)).reshape(2 * hidden_units, model_width)
    w_down = jnp.transpose(w_out[0], (1, 0))
    per_source = counts[0]
    slot_index = jnp.arange(slot_total, dtype=jnp.int32)
    live_mask = (slot_index < jnp.sum(per_source)).astype(F32)[:, None]
    pick = pick_matrix(per_source, slot_total)
    acts, row_parts = local_grads(x_rows, dy_rows, w_flat, w_down, live_mask, pick)

    acts_all = lax.all_to_all(
        jnp.broadcast_to(acts[None], (groups,) + acts.shape), "dp", 0, 0, tiled=True
    ).reshape(groups * slot_total, 3 * hidden_units)

    outgoing = row_parts.reshape(units, capacity, parts, share).transpose(0, 2, 1, 3)
    incoming = lax.all_to_all(
        outgoing.reshape(units * parts, capacity, share), ("expert", "mp"), 0, 0, tiled=True
    )
    selector = token_selector(assign, units, parts, capacity)
    grad_tokens = jnp.dot(
        selector, incoming.reshape(units * parts * capacity, share), preferred_element_type=F32
    ).astype(BF16)

    contract_first = (((0,), (0,)), ((), ()))
    x_all = both_all[:, 0].reshape(groups * slot_total, quarter)
    dy_all = both_all[:, 1].reshape(groups * slot_total, quarter)
    grad_in = lax.dot_general(
        acts_all[:, : 2 * hidden_units], x_all, contract_first, preferred_element_type=F32
    ).astype(BF16)
    grad_out = lax.dot_general(
        acts_all[:, 2 * hidden_units :], dy_all, contract_first, preferred_element_type=F32
    ).astype(BF16)
    grad_w_in = grad_in.reshape(2, hidden_units, quarter).transpose(2, 0, 1)[None]
    grad_w_out = grad_out.transpose(1, 0)[None]
    return (grad_w_in, grad_w_out, grad_tokens)


def solution(mesh):
    return jax.shard_map(
        per_device,
        mesh=mesh,
        in_specs=(
            P(("dp", "expert"), None),
            P(("dp", "expert"), None),
            P("expert", None, None, "mp"),
            P("expert", None, "mp"),
            P(("dp", "expert"), None),
            P(("dp", "expert"), None),
        ),
        out_specs=(
            P("expert", "dp", None, "mp"),
            P("expert", "dp", "mp"),
            P(("dp", "expert"), "mp"),
        ),
        check_vma=False,
    )
```

time: 151 us -> 48.5 us (0.32)
  waiting for transfers between devices: 112 us -> 16.2 us
  between operations: 14.2 us -> 0.77 us
  starting transfers between devices: 3.35 us -> 13.4 us
  local copies, waits for them, and re-layouts: 6.69 us -> 2.62 us
    reduce_scatter x2 -> x0, waiting for transfers between devices: 108 us -> none  [the longest x1 101 us: per_device(): lax.psum_scatter(lax.dot_general(stacked_cols, stacked_acts, (((0,), (0,)...]
    all_to_all x1 -> x3, waiting for transfers between devices: 3.91 us -> 16.2 us  [the longest x1 6.96 us: per_device(): lax.all_to_all(both, 'dp', split_axis=1, concat_axis=0, tiled=True)]
    all_to_all x1 -> x3, starting transfers between devices: 3.27 us -> 13.4 us  [the longest x1 5.17 us: per_device(): lax.all_to_all(outgoing.reshape(units * parts, capacity, share), ('expert...]
    slice x1, local copies, waits for them, and re-layouts: 2.24 us -> 0.02 us  [per_device(): dy_all = both_all[:, 1].reshape(groups * slot_total, quarter)]
    dot_general x5 -> x6, matrix products: 10.6 us -> 10.4 us  [the longest x1 3.38 us: local_grads(): lax.dot_general(x_rows, w_flat, contract_last, preferred_element_type=F32)]
  transfers between devices with their start and end apart: 3 -> 3, of which waited for: 3 -> 3; matrix products, arithmetic and copies ran while one was open for 6% -> 5% of each run, Pallas kernels for 0% -> 0%
where the time goes in v1:
time: 48.5 us; the launch traced here: 48 us
  waiting for transfers between devices  16.2 us (33%)
  starting transfers between devices  13.4 us (28%)
  matrix products  10.4 us (21%)
  other arithmetic  4.67 us (10%)
  local copies, waits for them, and re-layouts  2.62 us (5%)
  between operations  0.77 us (2%)
    all_to_all x1, waiting for transfers between devices, per_device(): lax.all_to_all(both, 'dp', split_axis=1, concat_axis=0, tiled=True)  6.96 us
    all_to_all x1, waiting for transfers between devices, per_device(): lax.all_to_all(jnp.broadcast_to(acts[None], (groups,) + acts.shape), 'dp'...  5.86 us
    all_to_all x1, starting transfers between devices, per_device(): lax.all_to_all(outgoing.reshape(units * parts, capacity, share), ('expert...  5.17 us
    all_to_all x1, starting transfers between devices, per_device(): lax.all_to_all(both, 'dp', split_axis=1, concat_axis=0, tiled=True)  4.87 us
    all_to_all x1, waiting for transfers between devices, per_device(): lax.all_to_all(outgoing.reshape(units * parts, capacity, share), ('expert...  3.41 us
    dot_general x1, matrix products, local_grads(): lax.dot_general(x_rows, w_flat, contract_last, preferred_element_type=F32)  3.38 us
    all_to_all x1, starting transfers between devices, per_device(): lax.all_to_all(jnp.broadcast_to(acts[None], (groups,) + acts.shape), 'dp'...  3.33 us
    dot_general x1, matrix products, local_grads(): row_parts = jnp.dot(picked, w_flat, preferred_element_type=F32).astype(BF16)  2.97 us
  transfers between devices with their start and end apart: 3, of which 3 were waited for; matrix products, arithmetic and copies ran while one was open for 5% of the time, Pallas kernels for 0%

profile of v1, /device:TPU:0, one launch (start us, length us, event | category | flops | bytes accessed | tf_op | source)
XLA Modules:
  0.0 48.0 jit_solution(9146628835858242521)
XLA Ops:
  0.6 0.0 copy-start
  0.6 0.0 copy-start.1
  0.7 1.4 %reduce_sum.27 = s32[]{:T(128)} reduce(s32[1,4]{1,0:T(1,128)} %param.10, s32[]{:T(128)} %constant.48.clone.1), dimensions={0,1}, to_apply=%region_0.0 | reduce | flops 3 | bytes 24 | tf_op jit(solution)/shard_map/reduce_sum | solution.py:76
  2.1 0.6 %compare_convert_fusion = f32[16]{0:T(128)S(1)} fusion(s32[]{:T(128)} %reduce_sum.27), kind=kLoop, calls=%fused_computation.30 | loop fusion | flops 32 | bytes 68 | tf_op jit(solution)/shard_map/convert_element_type | solution.py:76
  2.8 0.8 %reduce-window.8 = s32[4,1]{0,1:T(1,128)S(1)} reduce-window(s32[4,1]{0,1:T(1,128)} %bitcast.54, s32[]{:T(128)} %constant.48.clone.1), window={size=4x1 pad=3_0x0_0}, to_apply=%region_3.4 | reduce-window | flops 12 | bytes 36 | tf_op jit(solution)/shard_map/reduce-window.3
  3.6 0.7 %bitcast_subtract_fusion = s32[4]{0:T(128)S(1)} fusion(s32[4,1]{0,1:T(1,128)S(1)} %reduce-window.8, s32[1,4]{1,0:T(1,128)} %param.10), kind=kLoop, calls=%fused_computation.38 | loop fusion | flops 4 | bytes 48 | tf_op jit(solution)/shard_map/sub | solution.py:33
  4.2 0.7 %add_select_fusion = s32[4,4]{1,0:T(4,128)S(1)} fusion(s32[4]{0:T(128)S(1)} %bitcast_subtract_fusion, s32[4]{0:T(128)} %bitcast.55), kind=kLoop, calls=%fused_computation.25 | loop fusion | flops 48 | bytes 96 | tf_op jit(solution)/shard_map/jit(_where)/select_n | solution.py:35
  5.0 0.1 select_n.48
  5.1 3.4 %fusion.20 = f32[16,672]{1,0:T(8,128)S(1)} fusion(bf16[16,3072]{1,0:T(8,128)(2,1)} %param.6, bf16[672,3072]{1,0:T(8,128)(2,1)} %bitcast.45), kind=kOutput, calls=%fused_computation.41 | convolution fusion | flops 66060288 | bytes 4270080 | tf_op jit(solution)/shard_map/dot_general | solution.py:14
  8.4 0.0 copy-done
  8.5 0.0 copy-done.1
  8.5 0.0 copy-start.2
  8.5 0.0 copy-start.3
  8.5 0.7 %multiply_convert_fusion.2 = (bf16[16,336]{1,0:T(8,128)(2,1)S(1)}, bf16[16,336]{1,0:T(8,128)(2,1)S(1)}, bf16[16,336]{1,0:T(8,128)(2,1)S(1)}) fusion(f32[16,672]{1,0:T(8,128)S(1)} %fusion.20, f32[16]{0:T(128)S(1)} %compare_convert_fusion, bf16[16,3072]{1,0:T(8,128)(2,1)S(1)} %copy-done.1, bf16[1,3072,336]{1,2,0:T(8,128)(2,1)S(1)} %copy-done), kind=kOutput, calls=%fused_computation.19 | convolution fusion | flops 33126912 | bytes 2238016 | tf_op jit(solution)/shard_map/dot_general | solution.py:19
  9.2 3.0 %convolution_convert_fusion = bf16[16,3072]{1,0:T(8,128)(2,1)S(1)} fusion(bf16[672,3072]{1,0:T(8,128)(2,1)} %bitcast.46, bf16[16,336]{1,0:T(8,128)(2,1)S(1)} %get-tuple-element.6, bf16[16,336]{1,0:T(8,128)(2,1)S(1)} %get-tuple-element.5, s32[16]{0:T(128)S(1)} %select_n.48), kind=kOutput, calls=%fused_computation | convolution fusion | flops 66507520 | bytes 4248640 | tf_op jit(solution)/shard_map/dot_general | solution.py:26
  12.1 0.1 reshape.176
  12.2 0.7 %copy.28 = bf16[4,4,2,1536]{3,1,2,0:T(4,128)(2,1)} copy(bf16[4,4,2,1536]{3,2,1,0:T(2,128)(2,1)S(1)} %reshape.176) | data formatting | bytes 196608 | tf_op jit(solution)/shard_map/reshape | solution.py:84
  12.9 5.2 %all-to-all-start.2 = ((bf16[8,4,1536]{2,1,0:T(4,128)(2,1)}), bf16[8,4,1536]{2,1,0:T(4,128)(2,1)S(1)}, u32[]{:S(2)}, u32[]{:S(2)}) async-start(bf16[8,4,1536]{2,1,0:T(4,128)(2,1)} %bitcast.20), calls=%async_computation.2 | async-start | bytes 196608 | tf_op jit(solution)/shard_map/all_to_all | solution.py:85
  18.1 0.0 copy-done.2
  18.1 0.0 copy-done.3
  18.1 0.1 copy.26
  18.2 0.1 eq.64
  18.3 0.2 convert_reduce_fusion.1
  18.5 0.1 eq.68
  18.6 0.1 copy.27
  18.7 0.7 %copy.31 = bf16[4,4,8,768]{3,2,0,1:T(8,128)(2,1)} copy(bf16[4,4,8,768]{3,2,1,0:T(8,128)(2,1)S(1)} %bitcast.49) | data formatting | bytes 393216 | tf_op jit(solution)/shard_map/all_to_all | solution.py:69
  19.4 0.1 convert_reduce_fusion
  19.4 3.4 %all-to-all-done.2 = bf16[8,4,1536]{2,1,0:T(4,128)(2,1)S(1)} async-done(((bf16[8,4,1536]{2,1,0:T(4,128)(2,1)}), bf16[8,4,1536]{2,1,0:T(4,128)(2,1)S(1)}, u32[]{:S(2)}, u32[]{:S(2)}) %all-to-all-start.2) | async-done | bytes 98336 | tf_op jit(solution)/shard_map/all_to_all | solution.py:85
  22.9 4.9 %all-to-all-start.1 = ((bf16[32,4,768]{2,0,1:T(8,128)(2,1)}), bf16[32,4,768]{2,0,1:T(8,128)(2,1)S(1)}, u32[]{:S(2)}, u32[]{:S(2)}) async-start(bf16[32,4,768]{2,0,1:T(8,128)(2,1)} %bitcast.44), calls=%async_computation.1 | async-start | bytes 393216 | tf_op jit(solution)/shard_map/all_to_all | solution.py:69
  27.7 0.1 pad_maximum_fusion.1
  27.8 0.7 %convolution_convert_fusion.1 = bf16[4,1536]{1,0:T(4,128)(2,1)} fusion(bf16[32,1536]{1,0:T(8,128)(2,1)S(1)} %reshape.178, bf16[4,32]{1,0:T(4,128)(2,1)S(1)} %convert_reduce_fusion), kind=kOutput, calls=%fused_computation.1 | convolution fusion | flops 399360 | bytes 110848 | tf_op jit(solution)/shard_map/dot_general | solution.py:89
  28.6 7.0 %all-to-all-done.1 = bf16[32,4,768]{2,0,1:T(8,128)(2,1)S(1)} async-done(((bf16[32,4,768]{2,0,1:T(8,128)(2,1)}), bf16[32,4,768]{2,0,1:T(8,128)(2,1)S(1)}, u32[]{:S(2)}, u32[]{:S(2)}) %all-to-all-start.1) | async-done | bytes 196640 | tf_op jit(solution)/shard_map/all_to_all | solution.py:69
  35.5 0.7 %broadcast_in_dim.10 = bf16[4,16,1008]{2,1,0:T(8,128)(2,1)} broadcast(bf16[16,1008]{1,0:T(8,128)(2,1)S(1)} %pad_maximum_fusion.1), dimensions={1,2} | broadcast | bytes 161280 | tf_op jit(solution)/shard_map/broadcast_in_dim | solution.py:81
  36.2 3.3 %all-to-all-start = ((bf16[4,16,1008]{2,1,0:T(8,128)(2,1)}), bf16[4,16,1008]{2,1,0:T(8,128)(2,1)S(1)}, u32[]{:S(2)}, u32[]{:S(2)}) async-start(bf16[4,16,1008]{2,1,0:T(8,128)(2,1)} %broadcast_in_dim.10), calls=%async_computation | async-start | bytes 262144 | tf_op jit(solution)/shard_map/all_to_all | solution.py:80
  39.5 5.9 %all-to-all-done = bf16[4,16,1008]{2,1,0:T(8,128)(2,1)S(1)} async-done(((bf16[4,16,1008]{2,1,0:T(8,128)(2,1)}), bf16[4,16,1008]{2,1,0:T(8,128)(2,1)S(1)}, u32[]{:S(2)}, u32[]{:S(2)}) %all-to-all-start) | async-done | bytes 129056 | tf_op jit(solution)/shard_map/all_to_all | solution.py:80
  45.4 1.2 %fusion.2 = bf16[1,768,336]{1,2,0:T(8,128)(2,1)} fusion(bf16[64,768]{1,0:T(8,128)(2,1)S(1)} %bitcast.53, bf16[64,1008]{1,0:T(8,128)(2,1)S(1)} %bitcast.50), kind=kOutput, calls=%fused_computation.6 | convolution fusion | flops 33288192 | bytes 663552 | tf_op jit(solution)/shard_map/dot_general | solution.py:99
  46.6 1.4 %convolution_convert_fusion.2 = bf16[672,768]{1,0:T(8,128)(2,1)} fusion(bf16[64,768]{1,0:T(8,128)(2,1)S(1)} %bitcast.52, bf16[64,1008]{1,0:T(8,128)(2,1)S(1)} %bitcast.51), kind=kOutput, calls=%fused_computation.4 | convolution fusion | flops 66576384 | bytes 1228800 | tf_op jit(solution)/shard_map/dot_general | solution.py:96
  (5 shorter events, 0.1 us)
Async XLA Ops:
  0.6 7.8 %copy-start = (bf16[1,3072,336]{1,2,0:T(8,128)(2,1)S(1)}, bf16[1,3072,336]{1,2,0:T(8,128)(2,1)}, u32[]{:S(2)}) copy-start(bf16[1,3072,336]{1,2,0:T(8,128)(2,1)} %param.9) | copy-start | bytes 6193156
  0.6 7.8 %copy-start.1 = (bf16[16,3072]{1,0:T(8,128)(2,1)S(1)}, bf16[16,3072]{1,0:T(8,128)(2,1)}, u32[]{:S(2)}) copy-start(bf16[16,3072]{1,0:T(8,128)(2,1)} %param.7) | copy-start | bytes 294916
  8.5 9.6 %copy-start.2 = (bf16[16,3072]{1,0:T(8,128)(2,1)S(1)}, bf16[16,3072]{1,0:T(8,128)(2,1)}, u32[]{:S(2)}) copy-start(bf16[16,3072]{1,0:T(8,128)(2,1)} %param.6) | copy-start | bytes 294916
  8.5 9.6 %copy-start.3 = (s32[4,2]{0,1:T(2,128)S(1)}, s32[4,2]{0,1:T(2,128)}, u32[]{:S(2)}) copy-start(s32[4,2]{0,1:T(2,128)} %param.11) | copy-start | bytes 100
  12.9 10.0 %all-to-all-start.2 = ((bf16[8,4,1536]{2,1,0:T(4,128)(2,1)}), bf16[8,4,1536]{2,1,0:T(4,128)(2,1)S(1)}, u32[]{:S(2)}, u32[]{:S(2)}) async-start(bf16[8,4,1536]{2,1,0:T(4,128)(2,1)} %bitcast.20), calls=%async_computation.2 | async-start | bytes 196608 | tf_op jit(solution)/shard_map/all_to_all | solution.py:85
  22.9 12.7 %all-to-all-start.1 = ((bf16[32,4,768]{2,0,1:T(8,128)(2,1)}), bf16[32,4,768]{2,0,1:T(8,128)(2,1)S(1)}, u32[]{:S(2)}, u32[]{:S(2)}) async-start(bf16[32,4,768]{2,0,1:T(8,128)(2,1)} %bitcast.44), calls=%async_computation.1 | async-start | bytes 393216 | tf_op jit(solution)/shard_map/all_to_all | solution.py:69
  36.2 9.2 %all-to-all-start = ((bf16[4,16,1008]{2,1,0:T(8,128)(2,1)}), bf16[4,16,1008]{2,1,0:T(8,128)(2,1)S(1)}, u32[]{:S(2)}, u32[]{:S(2)}) async-start(bf16[4,16,1008]{2,1,0:T(8,128)(2,1)} %broadcast_in_dim.10), calls=%async_computation | async-start | bytes 262144 | tf_op jit(solution)/shard_map/all_to_all | solution.py:80

commit v2 on v1

v2 whole, which is shorter than its diff:
```python
import functools

import jax
import jax.numpy as jnp
from jax import lax
from jax.experimental import pallas as pl
from jax.experimental.pallas import tpu as pltpu
from jax.sharding import PartitionSpec as P

LAYER_EXPERTS = 16
DIRECT_PEERS = 16
BF16 = jnp.bfloat16
F32 = jnp.float32
VMEM_BYTES = 48 * 1024 * 1024
CONTRACT_LAST = (((1,), (1,)), ((), ()))

ANY = pl.BlockSpec(memory_space=pl.ANY)
IN_VMEM = pl.BlockSpec(memory_space=pltpu.VMEM)
IN_SMEM = pl.BlockSpec(memory_space=pltpu.SMEM)


def cuts_of(rows, most=256, unit=16):
    pieces = -(-rows // most)
    size = -(-rows // pieces)
    size = -(-size // unit) * unit
    return [(at, min(size, rows - at)) for at in range(0, rows, size)]


def split_kernel(groups, x_ref, dy_ref, *rest):
    outs, sems = rest[:groups], rest[groups]
    rows, width = x_ref.shape
    quarter = width // groups
    me = lax.axis_index("dp")
    copies = []
    for step in range(groups):
        goal = lax.rem(me + step, groups)
        columns = pl.ds(pl.multiple_of(goal * quarter, quarter), quarter)
        for half, ref in enumerate((x_ref, dy_ref)):
            copy = pltpu.make_async_copy(
                ref.at[:, columns],
                outs[step].at[pl.ds(half * rows, rows), :],
                sems.at[2 * step + half],
            )
            copy.start()
            copies.append(copy)
    for copy in copies:
        copy.wait()


def acts_kernel(units, parts, direct, *refs):
    x_hbm, dy_hbm, w_in_hbm, w_out_hbm, counts_hbm = refs[:5]
    blocks = units * parts if direct else 1
    acts_ref, row_refs = refs[5], refs[6 : 6 + blocks]
    x_ref, dy_ref, w_in_ref, w_out_ref, counts_ref, rows_ref, sems = refs[6 + blocks :]

    in_cuts = cuts_of(w_in_ref.shape[0])
    out_cuts = cuts_of(w_out_ref.shape[0])
    plan = [(counts_hbm, counts_ref), (x_hbm, x_ref)]
    plan += [(w_in_hbm.at[pl.ds(a, n), :], w_in_ref.at[pl.ds(a, n), :]) for a, n in in_cuts]
    plan += [(dy_hbm, dy_ref)]
    plan += [(w_out_hbm.at[pl.ds(a, n), :], w_out_ref.at[pl.ds(a, n), :]) for a, n in out_cuts]
    copies = [pltpu.make_async_copy(s, d, sems.at[i]) for i, (s, d) in enumerate(plan)]
    for copy in copies:
        copy.start()
    copies = iter(copies)

    next(copies).wait()
    slots = x_ref.shape[0]
    owners = counts_ref.shape[1]
    capacity = slots // owners
    my_unit = lax.axis_index("expert") if direct else 0
    row_at = lax.broadcasted_iota(jnp.int32, (slots, slots), 0)
    slot_at = lax.broadcasted_iota(jnp.int32, (slots, slots), 1)
    pick = jnp.zeros((slots, slots), F32)
    total = jnp.int32(0)
    for owner in range(owners):
        held = counts_ref[0, owner]
        first = lax.rem(owner - my_unit + owners, owners) * capacity
        hit = (row_at >= first) & (row_at < first + held) & (slot_at - row_at == total - first)
        pick = jnp.where(hit, 1.0, pick)
        total = total + held

    next(copies).wait()
    x = x_ref[...]
    pre = []
    for at, size in in_cuts:
        next(copies).wait()
        pre.append(
            lax.dot_general(
                x, w_in_ref[pl.ds(at, size), :], CONTRACT_LAST, preferred_element_type=F32
            )
        )
    pre = jnp.concatenate(pre, axis=1)
    next(copies).wait()
    dy = dy_ref[...]
    grad_hidden = []
    for at, size in out_cuts:
        next(copies).wait()
        grad_hidden.append(
            lax.dot_general(
                dy, w_out_ref[pl.ds(at, size), :], CONTRACT_LAST, preferred_element_type=F32
            )
        )
    grad_hidden = jnp.concatenate(grad_hidden, axis=1)

    units_here = w_out_ref.shape[0]
    gate_pre, up_pre = pre[:, :units_here], pre[:, units_here:]
    live = lax.broadcasted_iota(jnp.int32, gate_pre.shape, 0) < total
    live_mask = jnp.where(live, 1.0, 0.0)
    sigmoid_gate = jax.nn.sigmoid(gate_pre)
    hidden = live_mask * gate_pre * sigmoid_gate * up_pre
    grad_gate = (
        live_mask * grad_hidden * up_pre * sigmoid_gate * (1.0 + gate_pre * (1.0 - sigmoid_gate))
    )
    grad_up = live_mask * grad_hidden * gate_pre * sigmoid_gate
    grad_pre = jnp.concatenate([grad_gate, grad_up], axis=1).astype(BF16)
    acts_ref[...] = jnp.concatenate([grad_gate, grad_up, hidden], axis=1).astype(BF16)

    picked = jnp.dot(pick.astype(BF16), grad_pre, preferred_element_type=F32).astype(BF16)
    width = w_in_ref.shape[1]
    for at, size in cuts_of(width, 512, 128):
        rows_ref[:, pl.ds(at, size)] = jnp.dot(
            picked, w_in_ref[:, pl.ds(at, size)], preferred_element_type=F32
        )
    share = width // parts
    my_part = lax.axis_index("mp") if direct else 0
    for other in range(parts):
        goal = lax.rem(my_part + other, parts)
        half = rows_ref[:, pl.ds(pl.multiple_of(goal * share, share), share)].astype(BF16)
        for unit in range(units):
            piece = half[unit * capacity : (unit + 1) * capacity]
            index = unit * parts + other
            if direct:
                row_refs[index][...] = piece
            else:
                row_refs[0][index] = piece


def weights_kernel(groups, *refs):
    sent, acts = refs[:groups], refs[groups : 2 * groups]
    in_hbm, out_hbm, in_ref, out_ref, sems = refs[2 * groups :]
    slots = acts[0].shape[0]
    x = jnp.concatenate([ref[:slots] for ref in sent], axis=0)
    dy = jnp.concatenate([ref[slots:] for ref in sent], axis=0)
    columns = jnp.concatenate([ref[...] for ref in acts], axis=0).T
    copies = []
    start = 0
    for values, target, staged in ((x, in_hbm, in_ref), (dy, out_hbm, out_ref)):
        for at, size in cuts_of(target.shape[0]):
            here = pl.ds(at, size)
            staged[here, :] = jnp.dot(
                columns[start + at : start + at + size], values, preferred_element_type=F32
            ).astype(BF16)
            copy = pltpu.make_async_copy(
                staged.at[here, :], target.at[here, :], sems.at[len(copies)]
            )
            copy.start()
            copies.append(copy)
        start += target.shape[0]
    for copy in copies:
        copy.wait()


def tokens_kernel(units, parts, direct, capacity, assign_ref, *refs):
    out_ref, rows_ref = refs[-2:]
    pieces = refs[:-2]
    count = units * parts
    for index in range(count):
        piece = pieces[index][...] if direct else pieces[0][index]
        rows_ref[pl.ds(index * capacity, capacity), :] = piece.astype(F32)
    width, tokens = assign_ref.shape
    slices = units // min(LAYER_EXPERTS, units)
    token_at = lax.broadcasted_iota(jnp.int32, (tokens, count * capacity), 0)
    column_at = lax.broadcasted_iota(jnp.int32, (tokens, count * capacity), 1)
    selector = jnp.zeros((tokens, count * capacity), F32)
    my_unit = lax.axis_index("expert") if direct else 0
    for token in range(tokens):
        for k in range(width):
            expert = assign_ref[k, token]
            rank = jnp.int32(0)
            for earlier in range(token):
                for other in range(width):
                    rank = rank + (assign_ref[other, earlier] == expert).astype(jnp.int32)
            for piece in range(slices):
                source = expert * slices + piece
                if direct:
                    source = lax.rem(my_unit - source + units, units)
                for part in range(parts):
                    column = (source * parts + part) * capacity + rank
                    hit = (token_at == token) & (column_at == column)
                    selector = jnp.where(hit, selector + 1.0, selector)
    out_ref[...] = jnp.dot(
        selector.astype(BF16), rows_ref[...].astype(BF16), preferred_element_type=F32
    ).astype(BF16)


def params():
    return pltpu.CompilerParams(vmem_limit_bytes=VMEM_BYTES)


def shift_along(array, axis, step):
    size = lax.axis_size(axis)
    return lax.ppermute(array, axis, [(i, (i + step) % size) for i in range(size)])


def per_device(x_rows, dy_rows, w_in, w_out, counts, assign):
    slots, width = x_rows.shape
    hidden_units = w_out.shape[2]
    groups = lax.axis_size("dp")
    units = lax.axis_size("expert")
    parts = lax.axis_size("mp")
    capacity = slots // counts.shape[1]
    quarter = width // groups
    share = width // parts
    peers = units * parts
    direct = peers <= DIRECT_PEERS
    shape = jax.ShapeDtypeStruct

    split = pl.pallas_call(
        functools.partial(split_kernel, groups),
        out_shape=[shape((2 * slots, quarter), BF16)] * groups,
        in_specs=[ANY, ANY],
        out_specs=[ANY] * groups,
        scratch_shapes=[pltpu.SemaphoreType.DMA((2 * groups,))],
        compiler_params=params(),
        name="split_rows",
    )(x_rows, dy_rows)
    sent = [split[0]] + [shift_along(split[s], "dp", s) for s in range(1, groups)]

    w_flat = jnp.transpose(w_in[0], (1, 2, 0)).reshape(2 * hidden_units, width)
    w_down = jnp.transpose(w_out[0], (1, 0))
    if direct:
        row_shapes = [shape((capacity, share), BF16)] * peers
    else:
        row_shapes = [shape((peers, capacity, share), BF16)]
    copies = 3 + len(cuts_of(2 * hidden_units)) + len(cuts_of(hidden_units))
    acts, *row_parts = pl.pallas_call(
        functools.partial(acts_kernel, units, parts, direct),
        out_shape=[shape((slots, 3 * hidden_units), BF16)] + row_shapes,
        in_specs=[ANY] * 5,
        out_specs=[IN_VMEM] * (1 + len(row_shapes)),
        scratch_shapes=[
            pltpu.VMEM(x_rows.shape, BF16),
            pltpu.VMEM(dy_rows.shape, BF16),
            pltpu.VMEM(w_flat.shape, BF16),
            pltpu.VMEM(w_down.shape, BF16),
            pltpu.SMEM(counts.shape, jnp.int32),
            pltpu.VMEM((slots, width), F32),
            pltpu.SemaphoreType.DMA((copies,)),
        ],
        compiler_params=params(),
        name="acts_and_rows",
    )(x_rows, dy_rows, w_flat, w_down, counts)

    acts_all = [acts] + [shift_along(acts, "dp", s) for s in range(1, groups)]
    if direct:
        incoming = []
        for unit in range(units):
            for part in range(parts):
                piece = row_parts[unit * parts + part]
                if unit or part:
                    pairs = [
                        (e * parts + m, (e + unit) % units * parts + (m + part) % parts)
                        for e in range(units)
                        for m in range(parts)
                    ]
                    piece = lax.ppermute(piece, ("expert", "mp"), pairs)
                incoming.append(piece)
    else:
        incoming = [lax.all_to_all(row_parts[0], ("expert", "mp"), 0, 0, tiled=True)]

    grad_in, grad_out = pl.pallas_call(
        functools.partial(weights_kernel, groups),
        out_shape=[
            shape((2 * hidden_units, quarter), BF16),
            shape((hidden_units, quarter), BF16),
        ],
        in_specs=[IN_VMEM] * (2 * groups),
        out_specs=[ANY, ANY],
        scratch_shapes=[
            pltpu.VMEM((2 * hidden_units, quarter), BF16),
            pltpu.VMEM((hidden_units, quarter), BF16),
            pltpu.SemaphoreType.DMA((len(cuts_of(2 * hidden_units)) + len(cuts_of(hidden_units)),)),
        ],
        compiler_params=params(),
        name="weight_grads",
    )(*sent, *acts_all)

    grad_tokens = pl.pallas_call(
        functools.partial(tokens_kernel, units, parts, direct, capacity),
        out_shape=shape((assign.shape[0], share), BF16),
        in_specs=[IN_SMEM] + [IN_VMEM] * len(incoming),
        out_specs=IN_VMEM,
        scratch_shapes=[pltpu.VMEM((peers * capacity, share), F32)],
        compiler_params=params(),
        name="token_grads",
    )(assign.T, *incoming)

    grad_w_in = grad_in.reshape(2, hidden_units, quarter).transpose(2, 0, 1)[None]
    grad_w_out = grad_out.transpose(1, 0)[None]
    return (grad_w_in, grad_w_out, grad_tokens)


def solution(mesh):
    return jax.shard_map(
        per_device,
        mesh=mesh,
        in_specs=(
            P(("dp", "expert"), None),
            P(("dp", "expert"), None),
            P("expert", None, None, "mp"),
            P("expert", None, "mp"),
            P(("dp", "expert"), None),
            P(("dp", "expert"), None),
        ),
        out_specs=(
            P("expert", "dp", None, "mp"),
            P("expert", "dp", "mp"),
            P(("dp", "expert"), "mp"),
        ),
        check_vma=False,
    )
```

time: 48.5 us -> 38.8 us (0.80)
  matrix products: 10.4 us -> 0 us
  Pallas kernels: 0 us -> 9.43 us
  waiting for transfers between devices: 16.2 us -> 8.71 us
  other arithmetic: 4.67 us -> 0 us
  starting transfers between devices: 13.4 us -> 15.8 us
  local copies, waits for them, and re-layouts: 2.62 us -> 4.02 us
    all_to_all x3 -> x0, waiting for transfers between devices: 16.2 us -> none  [the longest x1 6.96 us: per_device(): lax.all_to_all(both, 'dp', split_axis=1, concat_axis=0, tiled=True)]
    ppermute x0 -> x13, starting transfers between devices: none -> 15.8 us  [the longest x6 8.28 us: shift_along(): lax.ppermute(array, axis, [(i, (i + step) % size) for i in range(size)])]
    all_to_all x3 -> x0, starting transfers between devices: 13.4 us -> none  [the longest x1 5.17 us: per_device(): lax.all_to_all(outgoing.reshape(units * parts, capacity, share), ('expert...]
    dot_general x6 -> x0, matrix products: 10.4 us -> none  [the longest x1 3.38 us: local_grads(): lax.dot_general(x_rows, w_flat, contract_last, preferred_element_type=F32)]
    pallas_call x0 -> x4, Pallas kernels: none -> 9.43 us  [the longest x1 6.38 us: per_device(): pl.pallas_call(functools.partial(acts_kernel, units, parts, direct), out_...]
    ppermute x0 -> x13, waiting for transfers between devices: none -> 8.71 us  [the longest x6 4.37 us: shift_along(): lax.ppermute(array, axis, [(i, (i + step) % size) for i in range(size)])]
    unnamed x9 -> x10, local copies, waits for them, and re-layouts: 0.13 us -> 4.02 us
    reduce_sum x3 -> x0, other arithmetic: 1.71 us -> none  [the longest x1 1.45 us: per_device(): live_mask = (slot_index < jnp.sum(per_source)).astype(F32)[:, None]]
  transfers between devices with their start and end apart: 3 -> 13, of which waited for: 3 -> 5; matrix products, arithmetic and copies ran while one was open for 5% -> 0% of each run, Pallas kernels for 0% -> 4%
where the time goes in v2:
time: 38.8 us; the launch traced here: 38.6 us
  starting transfers between devices  15.8 us (41%)
  Pallas kernels  9.43 us (24%)
  waiting for transfers between devices  8.71 us (22%)
  local copies, waits for them, and re-layouts  4.02 us (10%)
  between operations  0.7 us (2%)
    ppermute x6, starting transfers between devices, shift_along(): lax.ppermute(array, axis, [(i, (i + step) % size) for i in range(size)])  8.28 us
    ppermute x7, starting transfers between devices, per_device(): piece = lax.ppermute(piece, ('expert', 'mp'), pairs)  7.47 us
    pallas_call x1, Pallas kernels, per_device(): pl.pallas_call(functools.partial(acts_kernel, units, parts, direct), out_...  6.38 us
    ppermute x6, waiting for transfers between devices, shift_along(): lax.ppermute(array, axis, [(i, (i + step) % size) for i in range(size)])  4.37 us
    ppermute x7, waiting for transfers between devices, per_device(): piece = lax.ppermute(piece, ('expert', 'mp'), pairs)  4.34 us
    unnamed x10, local copies, waits for them, and re-layouts  4.02 us
    pallas_call x1, Pallas kernels, per_device(): pl.pallas_call(functools.partial(weights_kernel, groups), out_shape=[shap...  1.49 us
    pallas_call x1, Pallas kernels, per_device(): pl.pallas_call(functools.partial(tokens_kernel, units, parts, direct, cap...  1.34 us
  transfers between devices with their start and end apart: 13, of which 5 were waited for; matrix products, arithmetic and copies ran while one was open for 0% of the time, Pallas kernels for 4%

profile of v2, /device:TPU:0, one launch (start us, length us, event | category | flops | bytes accessed | tf_op | source)
XLA Modules:
  0.0 38.6 jit_solution(13777093076389950243)
XLA Ops:
  0.6 0.0 copy-start.3
  0.6 0.0 copy-start
  0.7 1.6 %copy-done = bf16[1,3072,336]{1,2,0:T(8,128)(2,1)S(1)} copy-done((bf16[1,3072,336]{1,2,0:T(8,128)(2,1)S(1)}, bf16[1,3072,336]{1,2,0:T(8,128)(2,1)}, u32[]{:S(2)}) %copy-start) | copy-done | bytes 2064408
  2.2 0.0 copy-start.1
  2.2 0.9 %copy-done.1 = bf16[16,3072]{1,0:T(8,128)(2,1)S(1)} copy-done((bf16[16,3072]{1,0:T(8,128)(2,1)S(1)}, bf16[16,3072]{1,0:T(8,128)(2,1)}, u32[]{:S(2)}) %copy-start.1) | copy-done | bytes 98328
  3.1 0.0 copy-start.2
  3.1 0.9 %copy-done.2 = bf16[16,3072]{1,0:T(8,128)(2,1)S(1)} copy-done((bf16[16,3072]{1,0:T(8,128)(2,1)S(1)}, bf16[16,3072]{1,0:T(8,128)(2,1)}, u32[]{:S(2)}) %copy-start.2) | copy-done | bytes 98328
  4.0 0.0 copy-start.4
  4.0 0.7 %copy-done.4 = s32[1,4]{1,0:T(1,128)S(1)} copy-done((s32[1,4]{1,0:T(1,128)S(1)}, s32[1,4]{1,0:T(1,128)}, u32[]{:S(2)}) %copy-start.4) | copy-done | bytes 40
  4.7 6.4 %acts_and_rows.1 = (bf16[16,1008]{1,0:T(8,128)(2,1)S(1)}, bf16[4,1536]{1,0:T(4,128)(2,1)S(1)}, bf16[4,1536]{1,0:T(4,128)(2,1)S(1)}, bf16[4,1536]{1,0:T(4,128)(2,...) custom-call(bf16[16,3072]{1,0:T(8,128)(2,1)S(1)} %copy-done.1, ...), custom_call_target="tpu_custom_call" | custom-call | tf_op jit(solution)/shard_map/acts_and_rows/pallas_call | solution.py:237
  11.1 3.0 %collective-permute-start.6 = (bf16[4,1536]{1,0:T(4,128)(2,1)S(1)}, bf16[4,1536]{1,0:T(4,128)(2,1)S(1)}, u32[]{:S(2)}, u32[]{:S(2)}) collective-permute-start(bf16[4,1536]{1,0:T(4,128)(2,1)S(1)} %get-tuple-element.26), channel_id=1, source_target_pairs={{0,1},{1,0},{2,3},{3,2},{4,5},{5,4},{6,7},{7,6},{8,9},{9,8},{10,11... | collective-permute-start | bytes 36872 | tf_op jit(solution)/shard_map/ppermute | solution.py:267
  14.1 0.0 collective-permute-start.7
  14.1 3.6 %collective-permute-start.5 = (bf16[16,1008]{1,0:T(8,128)(2,1)S(1)}, bf16[16,1008]{1,0:T(8,128)(2,1)S(1)}, u32[]{:S(2)}, u32[]{:S(2)}) collective-permute-start(bf16[16,1008]{1,0:T(8,128)(2,1)S(1)} %get-tuple-element.22.refs_4_), channel_id=1, source_target_pairs={{0,24},{8,0},{16,8},{24,16},{1,25},{9,1},{17,9},{25,17},{2,26},{10... | collective-permute-start | bytes 96776 | tf_op jit(solution)/shard_map/ppermute | solution.py:203
  17.7 1.4 %collective-permute-start.8 = (bf16[4,1536]{1,0:T(4,128)(2,1)S(1)}, bf16[4,1536]{1,0:T(4,128)(2,1)S(1)}, u32[]{:S(2)}, u32[]{:S(2)}) collective-permute-start(bf16[4,1536]{1,0:T(4,128)(2,1)S(1)} %get-tuple-element.28), channel_id=1, source_target_pairs={{0,3},{1,2},{2,5},{3,4},{4,7},{5,6},{6,1},{7,0},{8,11},{9,10},{10,... | collective-permute-start | bytes 36872 | tf_op jit(solution)/shard_map/ppermute | solution.py:267
  19.1 0.5 %collective-permute-start.9 = (bf16[4,1536]{1,0:T(4,128)(2,1)S(1)}, bf16[4,1536]{1,0:T(4,128)(2,1)S(1)}, u32[]{:S(2)}, u32[]{:S(2)}) collective-permute-start(bf16[4,1536]{1,0:T(4,128)(2,1)S(1)} %get-tuple-element.29), channel_id=1, source_target_pairs={{0,4},{1,5},{2,6},{3,7},{4,0},{5,1},{6,2},{7,3},{8,12},{9,13},{10,... | collective-permute-start | bytes 36872 | tf_op jit(solution)/shard_map/ppermute | solution.py:267
  19.7 0.0 collective-permute-done.6.refs_1_
  19.7 2.4 %collective-permute-start.10 = (bf16[4,1536]{1,0:T(4,128)(2,1)S(1)}, bf16[4,1536]{1,0:T(4,128)(2,1)S(1)}, u32[]{:S(2)}, u32[]{:S(2)}) collective-permute-start(bf16[4,1536]{1,0:T(4,128)(2,1)S(1)} %get-tuple-element.30), channel_id=1, source_target_pairs={{0,5},{1,4},{2,7},{3,6},{4,1},{5,0},{6,3},{7,2},{8,13},{9,12},{10,... | collective-permute-start | bytes 36872 | tf_op jit(solution)/shard_map/ppermute | solution.py:267
  22.1 0.0 collective-permute-done.7.refs_2_
  22.1 0.0 collective-permute-start.11
  22.1 0.2 split_rows.1
  22.4 0.0 collective-permute-done.8.refs_3_
  22.4 0.1 collective-permute-start
  22.4 0.4 %collective-permute-done.9.refs_4_ = bf16[4,1536]{1,0:T(4,128)(2,1)S(1)} collective-permute-done((bf16[4,1536]{1,0:T(4,128)(2,1)S(1)}, bf16[4,1536]{1,0:T(4,128)(2,1)S(1)}, u32[]{:S(2)}, u32[]{:S(2)}) %collective-permute-start.9) | collective-permute-done | bytes 12320 | tf_op jit(solution)/shard_map/ppermute | solution.py:267
  22.8 0.6 %collective-permute-start.1 = (bf16[32,768]{1,0:T(8,128)(2,1)S(1)}, bf16[32,768]{1,0:T(8,128)(2,1)S(1)}, u32[]{:S(2)}, u32[]{:S(2)}) collective-permute-start(bf16[32,768]{1,0:T(8,128)(2,1)S(1)} %get-tuple-element.20), channel_id=1, source_target_pairs={{0,16},{8,24},{16,0},{24,8},{1,17},{9,25},{17,1},{25,9},{2,18},{10... | collective-permute-start | bytes 147464 | tf_op jit(solution)/shard_map/ppermute | solution.py:203
  23.4 0.8 %collective-permute-done.10.refs_5_ = bf16[4,1536]{1,0:T(4,128)(2,1)S(1)} collective-permute-done((bf16[4,1536]{1,0:T(4,128)(2,1)S(1)}, bf16[4,1536]{1,0:T(4,128)(2,1)S(1)}, u32[]{:S(2)}, u32[]{:S(2)}) %collective-permute-start.10) | collective-permute-done | bytes 12320 | tf_op jit(solution)/shard_map/ppermute | solution.py:267
  24.3 2.0 %collective-permute-start.2 = (bf16[32,768]{1,0:T(8,128)(2,1)S(1)}, bf16[32,768]{1,0:T(8,128)(2,1)S(1)}, u32[]{:S(2)}, u32[]{:S(2)}) collective-permute-start(bf16[32,768]{1,0:T(8,128)(2,1)S(1)} %get-tuple-element.21), channel_id=1, source_target_pairs={{0,24},{8,0},{16,8},{24,16},{1,25},{9,1},{17,9},{25,17},{2,26},{10... | collective-permute-start | bytes 147464 | tf_op jit(solution)/shard_map/ppermute | solution.py:203
  26.3 0.0 collective-permute-done.11.refs_6_
  26.3 0.0 collective-permute-start.12
  26.3 3.1 %collective-permute-done.12.refs_7_ = bf16[4,1536]{1,0:T(4,128)(2,1)S(1)} collective-permute-done((bf16[4,1536]{1,0:T(4,128)(2,1)S(1)}, bf16[4,1536]{1,0:T(4,128)(2,1)S(1)}, u32[]{:S(2)}, u32[]{:S(2)}) %collective-permute-start.12) | collective-permute-done | bytes 12320 | tf_op jit(solution)/shard_map/ppermute | solution.py:267
  29.4 2.0 %collective-permute-start.4 = (bf16[16,1008]{1,0:T(8,128)(2,1)S(1)}, bf16[16,1008]{1,0:T(8,128)(2,1)S(1)}, u32[]{:S(2)}, u32[]{:S(2)}) collective-permute-start(bf16[16,1008]{1,0:T(8,128)(2,1)S(1)} %get-tuple-element.22.refs_4_), channel_id=1, source_target_pairs={{0,16},{8,24},{16,0},{24,8},{1,17},{9,25},{17,1},{25,9},{2,18},{10... | collective-permute-start | bytes 96776 | tf_op jit(solution)/shard_map/ppermute | solution.py:203
  31.4 0.0 collective-permute-done.5.refs_7_
  31.4 0.0 collective-permute-start.3
  31.4 0.0 copy-done.3
  31.4 1.3 %token_grads.1 = bf16[4,1536]{1,0:T(4,128)(2,1)} custom-call(s32[2,4]{1,0:T(2,128)S(1)} %bitcast.18, bf16[4,1536]{1,0:T(4,128)(2,1)S(1)} %get-tuple-element.25.refs_0_, bf16[4,1536]{1,0:T(4,128)(2,1)S(1)} %collective-permute-done.6.refs_1_, bf16[4,1536]{1,0:T(4,128)(2,1)S(1)} %collective-permute-done.7.refs_2_, ...), custom_call_target="tpu_custom_call" | custom-call | tf_op jit(solution)/shard_map/token_grads/pallas_call | solution.py:289
  32.8 2.4 %collective-permute-done.4.refs_6_ = bf16[16,1008]{1,0:T(8,128)(2,1)S(1)} collective-permute-done((bf16[16,1008]{1,0:T(8,128)(2,1)S(1)}, bf16[16,1008]{1,0:T(8,128)(2,1)S(1)}, u32[]{:S(2)}, u32[]{:S(2)}) %collective-permute-start.4) | collective-permute-done | bytes 32288 | tf_op jit(solution)/shard_map/ppermute | solution.py:203
  35.2 2.0 %collective-permute-done.3.refs_5_ = bf16[16,1008]{1,0:T(8,128)(2,1)S(1)} collective-permute-done((bf16[16,1008]{1,0:T(8,128)(2,1)S(1)}, bf16[16,1008]{1,0:T(8,128)(2,1)S(1)}, u32[]{:S(2)}, u32[]{:S(2)}) %collective-permute-start.3) | collective-permute-done | bytes 32288 | tf_op jit(solution)/shard_map/ppermute | solution.py:203
  37.1 0.0 collective-permute-done.refs_1_
  37.1 0.0 collective-permute-done.1.refs_2_
  37.1 0.0 collective-permute-done.2.refs_3_
  37.1 1.5 %weight_grads.1 = (bf16[672,768]{1,0:T(8,128)(2,1)}, bf16[336,768]{1,0:T(8,128)(2,1)}) custom-call(bf16[32,768]{1,0:T(8,128)(2,1)S(1)} %get-tuple-element.18.refs_0_, bf16[32,768]{1,0:T(8,128)(2,1)S(1)} %collective-permute-done.refs_1_, bf16[32,768]{1,0:T(8,128)(2,1)S(1)} %collective-permute-done.1.refs_2_, ...), custom_call_target="tpu_custom_call" | custom-call | tf_op jit(solution)/shard_map/weight_grads/pallas_call | solution.py:272
Async XLA Ops:
  0.6 30.8 %copy-start.3 = (s32[4,2]{0,1:T(2,128)S(1)}, s32[4,2]{0,1:T(2,128)}, u32[]{:S(2)}) copy-start(s32[4,2]{0,1:T(2,128)} %param.11) | copy-start | bytes 100
  0.6 1.6 %copy-start = (bf16[1,3072,336]{1,2,0:T(8,128)(2,1)S(1)}, bf16[1,3072,336]{1,2,0:T(8,128)(2,1)}, u32[]{:S(2)}) copy-start(bf16[1,3072,336]{1,2,0:T(8,128)(2,1)} %param.9) | copy-start | bytes 6193156
  2.2 0.9 %copy-start.1 = (bf16[16,3072]{1,0:T(8,128)(2,1)S(1)}, bf16[16,3072]{1,0:T(8,128)(2,1)}, u32[]{:S(2)}) copy-start(bf16[16,3072]{1,0:T(8,128)(2,1)} %refs_0_.1) | copy-start | bytes 294916
  3.1 0.9 %copy-start.2 = (bf16[16,3072]{1,0:T(8,128)(2,1)S(1)}, bf16[16,3072]{1,0:T(8,128)(2,1)}, u32[]{:S(2)}) copy-start(bf16[16,3072]{1,0:T(8,128)(2,1)} %refs_1_.1) | copy-start | bytes 294916
  4.0 0.7 %copy-start.4 = (s32[1,4]{1,0:T(1,128)S(1)}, s32[1,4]{1,0:T(1,128)}, u32[]{:S(2)}) copy-start(s32[1,4]{1,0:T(1,128)} %refs_4_.1) | copy-start | bytes 52
  11.1 8.6 %collective-permute-start.6 = (bf16[4,1536]{1,0:T(4,128)(2,1)S(1)}, bf16[4,1536]{1,0:T(4,128)(2,1)S(1)}, u32[]{:S(2)}, u32[]{:S(2)}) collective-permute-start(bf16[4,1536]{1,0:T(4,128)(2,1)S(1)} %get-tuple-element.26), channel_id=1, source_target_pairs={{0,1},{1,0},{2,3},{3,2},{4,5},{5,4},{6,7},{7,6},{8,9},{9,8},{10,11... | collective-permute-start | bytes 36872 | tf_op jit(solution)/shard_map/ppermute | solution.py:267
  14.1 8.0 %collective-permute-start.7 = (bf16[4,1536]{1,0:T(4,128)(2,1)S(1)}, bf16[4,1536]{1,0:T(4,128)(2,1)S(1)}, u32[]{:S(2)}, u32[]{:S(2)}) collective-permute-start(bf16[4,1536]{1,0:T(4,128)(2,1)S(1)} %get-tuple-element.27), channel_id=1, source_target_pairs={{0,2},{1,3},{2,4},{3,5},{4,6},{5,7},{6,0},{7,1},{8,10},{9,11},{10,... | collective-permute-start | bytes 36872 | tf_op jit(solution)/shard_map/ppermute | solution.py:267
  14.1 17.3 %collective-permute-start.5 = (bf16[16,1008]{1,0:T(8,128)(2,1)S(1)}, bf16[16,1008]{1,0:T(8,128)(2,1)S(1)}, u32[]{:S(2)}, u32[]{:S(2)}) collective-permute-start(bf16[16,1008]{1,0:T(8,128)(2,1)S(1)} %get-tuple-element.22.refs_4_), channel_id=1, source_target_pairs={{0,24},{8,0},{16,8},{24,16},{1,25},{9,1},{17,9},{25,17},{2,26},{10... | collective-permute-start | bytes 96776 | tf_op jit(solution)/shard_map/ppermute | solution.py:203
  17.7 4.7 %collective-permute-start.8 = (bf16[4,1536]{1,0:T(4,128)(2,1)S(1)}, bf16[4,1536]{1,0:T(4,128)(2,1)S(1)}, u32[]{:S(2)}, u32[]{:S(2)}) collective-permute-start(bf16[4,1536]{1,0:T(4,128)(2,1)S(1)} %get-tuple-element.28), channel_id=1, source_target_pairs={{0,3},{1,2},{2,5},{3,4},{4,7},{5,6},{6,1},{7,0},{8,11},{9,10},{10,... | collective-permute-start | bytes 36872 | tf_op jit(solution)/shard_map/ppermute | solution.py:267
  19.1 3.7 %collective-permute-start.9 = (bf16[4,1536]{1,0:T(4,128)(2,1)S(1)}, bf16[4,1536]{1,0:T(4,128)(2,1)S(1)}, u32[]{:S(2)}, u32[]{:S(2)}) collective-permute-start(bf16[4,1536]{1,0:T(4,128)(2,1)S(1)} %get-tuple-element.29), channel_id=1, source_target_pairs={{0,4},{1,5},{2,6},{3,7},{4,0},{5,1},{6,2},{7,3},{8,12},{9,13},{10,... | collective-permute-start | bytes 36872 | tf_op jit(solution)/shard_map/ppermute | solution.py:267
  19.7 4.6 %collective-permute-start.10 = (bf16[4,1536]{1,0:T(4,128)(2,1)S(1)}, bf16[4,1536]{1,0:T(4,128)(2,1)S(1)}, u32[]{:S(2)}, u32[]{:S(2)}) collective-permute-start(bf16[4,1536]{1,0:T(4,128)(2,1)S(1)} %get-tuple-element.30), channel_id=1, source_target_pairs={{0,5},{1,4},{2,7},{3,6},{4,1},{5,0},{6,3},{7,2},{8,13},{9,12},{10,... | collective-permute-start | bytes 36872 | tf_op jit(solution)/shard_map/ppermute | solution.py:267
  22.1 4.2 %collective-permute-start.11 = (bf16[4,1536]{1,0:T(4,128)(2,1)S(1)}, bf16[4,1536]{1,0:T(4,128)(2,1)S(1)}, u32[]{:S(2)}, u32[]{:S(2)}) collective-permute-start(bf16[4,1536]{1,0:T(4,128)(2,1)S(1)} %get-tuple-element.31), channel_id=1, source_target_pairs={{0,6},{1,7},{2,0},{3,1},{4,2},{5,3},{6,4},{7,5},{8,14},{9,15},{10,... | collective-permute-start | bytes 36872 | tf_op jit(solution)/shard_map/ppermute | solution.py:267
  22.4 14.8 %collective-permute-start = (bf16[32,768]{1,0:T(8,128)(2,1)S(1)}, bf16[32,768]{1,0:T(8,128)(2,1)S(1)}, u32[]{:S(2)}, u32[]{:S(2)}) collective-permute-start(bf16[32,768]{1,0:T(8,128)(2,1)S(1)} %get-tuple-element.19), channel_id=1, source_target_pairs={{0,8},{8,16},{16,24},{24,0},{1,9},{9,17},{17,25},{25,1},{2,10},{10... | collective-permute-start | bytes 147464 | tf_op jit(solution)/shard_map/ppermute | solution.py:203
  22.8 14.3 %collective-permute-start.1 = (bf16[32,768]{1,0:T(8,128)(2,1)S(1)}, bf16[32,768]{1,0:T(8,128)(2,1)S(1)}, u32[]{:S(2)}, u32[]{:S(2)}) collective-permute-start(bf16[32,768]{1,0:T(8,128)(2,1)S(1)} %get-tuple-element.20), channel_id=1, source_target_pairs={{0,16},{8,24},{16,0},{24,8},{1,17},{9,25},{17,1},{25,9},{2,18},{10... | collective-permute-start | bytes 147464 | tf_op jit(solution)/shard_map/ppermute | solution.py:203
  24.3 12.9 %collective-permute-start.2 = (bf16[32,768]{1,0:T(8,128)(2,1)S(1)}, bf16[32,768]{1,0:T(8,128)(2,1)S(1)}, u32[]{:S(2)}, u32[]{:S(2)}) collective-permute-start(bf16[32,768]{1,0:T(8,128)(2,1)S(1)} %get-tuple-element.21), channel_id=1, source_target_pairs={{0,24},{8,0},{16,8},{24,16},{1,25},{9,1},{17,9},{25,17},{2,26},{10... | collective-permute-start | bytes 147464 | tf_op jit(solution)/shard_map/ppermute | solution.py:203
  26.3 3.1 %collective-permute-start.12 = (bf16[4,1536]{1,0:T(4,128)(2,1)S(1)}, bf16[4,1536]{1,0:T(4,128)(2,1)S(1)}, u32[]{:S(2)}, u32[]{:S(2)}) collective-permute-start(bf16[4,1536]{1,0:T(4,128)(2,1)S(1)} %get-tuple-element.32), channel_id=1, source_target_pairs={{0,7},{1,6},{2,1},{3,0},{4,3},{5,2},{6,5},{7,4},{8,15},{9,14},{10,... | collective-permute-start | bytes 36872 | tf_op jit(solution)/shard_map/ppermute | solution.py:267
  29.4 5.7 %collective-permute-start.4 = (bf16[16,1008]{1,0:T(8,128)(2,1)S(1)}, bf16[16,1008]{1,0:T(8,128)(2,1)S(1)}, u32[]{:S(2)}, u32[]{:S(2)}) collective-permute-start(bf16[16,1008]{1,0:T(8,128)(2,1)S(1)} %get-tuple-element.22.refs_4_), channel_id=1, source_target_pairs={{0,16},{8,24},{16,0},{24,8},{1,17},{9,25},{17,1},{25,9},{2,18},{10... | collective-permute-start | bytes 96776 | tf_op jit(solution)/shard_map/ppermute | solution.py:203
  31.4 5.7 %collective-permute-start.3 = (bf16[16,1008]{1,0:T(8,128)(2,1)S(1)}, bf16[16,1008]{1,0:T(8,128)(2,1)S(1)}, u32[]{:S(2)}, u32[]{:S(2)}) collective-permute-start(bf16[16,1008]{1,0:T(8,128)(2,1)S(1)} %get-tuple-element.22.refs_4_), channel_id=1, source_target_pairs={{0,8},{8,16},{16,24},{24,0},{1,9},{9,17},{17,25},{25,1},{2,10},{10... | collective-permute-start | bytes 96776 | tf_op jit(solution)/shard_map/ppermute | solution.py:203

commit v3 on v2

v3 whole, which is shorter than its diff:
```python
import functools

import jax
import jax.numpy as jnp
from jax import lax
from jax.experimental import pallas as pl
from jax.experimental.pallas import tpu as pltpu
from jax.sharding import PartitionSpec as P

LAYER_EXPERTS = 16
BF16 = jnp.bfloat16
F32 = jnp.float32
VMEM_BYTES = 48 * 1024 * 1024
CONTRACT_LAST = (((1,), (1,)), ((), ()))

ANY = pl.BlockSpec(memory_space=pl.ANY)
IN_HBM = pl.BlockSpec(memory_space=pltpu.HBM)
IN_VMEM = pl.BlockSpec(memory_space=pltpu.VMEM)
IN_SMEM = pl.BlockSpec(memory_space=pltpu.SMEM)


def shape(dims, dtype=BF16):
    return jax.ShapeDtypeStruct(dims, dtype)


def params():
    return pltpu.CompilerParams(vmem_limit_bytes=VMEM_BYTES)


def bits_of(size):
    return size.bit_length() - 1


def cuts_of(rows, most=256, unit=16):
    pieces = -(-rows // most)
    size = -(-rows // pieces)
    size = -(-size // unit) * unit
    return [(at, min(size, rows - at)) for at in range(0, rows, size)]


def column_start(me, bits, step, width, flipped):
    place = lax.shift_right_logical(me, jnp.int32(bits - 1 - step))
    if flipped:
        place = place ^ 1
    return place * (width // 2 ** (step + 1))


def lanes(start, size):
    return pl.ds(pl.multiple_of(start, 128), size)


def split_kernel(bits, x_ref, dy_ref, *rest):
    outs, sems = rest[: bits + 1], rest[bits + 1]
    rows, width = x_ref.shape
    me = lax.axis_index("dp")
    copies = []
    for step in range(bits + 1):
        own = step == bits
        last = min(step, bits - 1)
        start = column_start(me, bits, last, width, not own)
        size = width // 2 ** (last + 1)
        for half, ref in enumerate((x_ref, dy_ref)):
            copy = pltpu.make_async_copy(
                ref.at[:, lanes(start, size)],
                outs[step].at[pl.ds(half * rows, rows), :],
                sems.at[2 * step + half],
            )
            copy.start()
            copies.append(copy)
    for copy in copies:
        copy.wait()


def acts_kernel(parts, *refs):
    x_hbm, dy_hbm, w_in_hbm, w_out_hbm, counts_hbm = refs[:5]
    acts_ref, keep_ref, send_ref = refs[5:8]
    x_ref, dy_ref, w_in_ref, w_out_ref, counts_ref, rows_ref, sems = refs[8:]

    in_cuts = cuts_of(w_in_ref.shape[0])
    out_cuts = cuts_of(w_out_ref.shape[0])
    plan = [(x_hbm, x_ref)]
    plan += [(w_in_hbm.at[pl.ds(a, n), :], w_in_ref.at[pl.ds(a, n), :]) for a, n in in_cuts]
    plan += [(dy_hbm, dy_ref)]
    plan += [(w_out_hbm.at[pl.ds(a, n), :], w_out_ref.at[pl.ds(a, n), :]) for a, n in out_cuts]
    plan += [(counts_hbm, counts_ref)]
    copies = [pltpu.make_async_copy(s, d, sems.at[i]) for i, (s, d) in enumerate(plan)]
    for copy in copies:
        copy.start()
    copies = iter(copies)

    next(copies).wait()
    x = x_ref[...]
    pre = []
    for at, size in in_cuts:
        next(copies).wait()
        pre.append(
            lax.dot_general(
                x, w_in_ref[pl.ds(at, size), :], CONTRACT_LAST, preferred_element_type=F32
            )
        )
    pre = jnp.concatenate(pre, axis=1)
    next(copies).wait()
    dy = dy_ref[...]
    grad_hidden = []
    for at, size in out_cuts:
        next(copies).wait()
        grad_hidden.append(
            lax.dot_general(
                dy, w_out_ref[pl.ds(at, size), :], CONTRACT_LAST, preferred_element_type=F32
            )
        )
    grad_hidden = jnp.concatenate(grad_hidden, axis=1)

    next(copies).wait()
    slots = x_ref.shape[0]
    owners = counts_ref.shape[1]
    capacity = slots // owners
    my_unit = lax.axis_index("expert")
    row_at = lax.broadcasted_iota(jnp.int32, (slots, slots), 0)
    slot_at = lax.broadcasted_iota(jnp.int32, (slots, slots), 1)
    pick = jnp.zeros((slots, slots), F32)
    total = jnp.int32(0)
    for owner in range(owners):
        held = counts_ref[0, owner]
        first = (my_unit ^ owner) * capacity
        hit = (row_at >= first) & (row_at < first + held) & (slot_at - row_at == total - first)
        pick = jnp.where(hit, 1.0, pick)
        total = total + held

    units_here = w_out_ref.shape[0]
    gate_pre, up_pre = pre[:, :units_here], pre[:, units_here:]
    live = lax.broadcasted_iota(jnp.int32, gate_pre.shape, 0) < total
    live_mask = jnp.where(live, 1.0, 0.0)
    sigmoid_gate = jax.nn.sigmoid(gate_pre)
    hidden = live_mask * gate_pre * sigmoid_gate * up_pre
    grad_gate = (
        live_mask * grad_hidden * up_pre * sigmoid_gate * (1.0 + gate_pre * (1.0 - sigmoid_gate))
    )
    grad_up = live_mask * grad_hidden * gate_pre * sigmoid_gate
    grad_pre = jnp.concatenate([grad_gate, grad_up], axis=1).astype(BF16)
    acts_ref[...] = jnp.concatenate([grad_gate, grad_up, hidden], axis=1).astype(BF16)

    picked = jnp.dot(pick.astype(BF16), grad_pre, preferred_element_type=F32).astype(BF16)
    width = w_in_ref.shape[1]
    for at, size in cuts_of(width, 512, 128):
        rows_ref[:, pl.ds(at, size)] = jnp.dot(
            picked, w_in_ref[:, pl.ds(at, size)], preferred_element_type=F32
        )
    my_part = lax.axis_index("mp")
    bits = bits_of(parts)
    keep_ref[...] = rows_ref[:, lanes(column_start(my_part, bits, 0, width, False), width // 2)]
    send_ref[...] = rows_ref[
        :, lanes(column_start(my_part, bits, 0, width, True), width // 2)
    ].astype(BF16)


def sum_task(bits, step, width):
    def body(ins, outs):
        keep_ref, recv_ref = ins
        total = keep_ref[...].astype(F32) + recv_ref[...].astype(F32)
        if step + 1 < bits:
            me = lax.axis_index("mp")
            base = column_start(me, bits, step, width, False)
            size = width // 2 ** (step + 2)
            is_high = column_start(me, bits, step + 1, width, False) - base > 0
            low, high = total[:, :size], total[:, size:]
            outs[0][...] = jnp.where(is_high, high, low)
            outs[1][...] = jnp.where(is_high, low, high).astype(BF16)
        else:
            half = total.shape[0] // 2
            outs[0][...] = total[:half]
            outs[1][...] = total[half:].astype(BF16)

    return body


def deal_task(blocks, block):
    def body(ins, outs):
        keep, recv = ins[0][...].astype(F32), ins[1][...].astype(F32)
        joined = []
        for at in range(blocks):
            joined += [keep[at * block : (at + 1) * block], recv[at * block : (at + 1) * block]]
        outs[0][...] = jnp.concatenate(joined[:blocks], axis=0)
        outs[1][...] = jnp.concatenate(joined[blocks:], axis=0).astype(BF16)

    return body


def stack_task(ins, outs):
    at = 0
    for ref in ins:
        outs[0][pl.ds(at, ref.shape[0]), :] = ref[...]
        at += ref.shape[0]


def columns_task(bits, step, width):
    def body(ins, outs):
        me = lax.axis_index("dp")
        size = width // 2 ** (step + 1)
        start = column_start(me, bits, step, width, True)
        rows = ins[0].shape[0]
        outs[0][pl.ds(0, rows), :] = ins[0][...]
        at = rows
        for past, ref in enumerate(ins[1:]):
            base = column_start(me, bits, past, width, False)
            outs[0][pl.ds(at, ref.shape[0]), :] = ref[:, lanes(start - base, size)]
            at += ref.shape[0]

    return body


def run_tasks(tasks, name):
    ins = [array for _, arrays, _ in tasks for array in arrays]
    outs = [out for _, _, out_shapes in tasks for out in out_shapes]

    def kernel(*refs):
        in_at, out_at = 0, len(ins)
        for body, arrays, out_shapes in tasks:
            body(
                refs[in_at : in_at + len(arrays)],
                refs[out_at : out_at + len(out_shapes)],
            )
            in_at += len(arrays)
            out_at += len(out_shapes)

    results = iter(
        pl.pallas_call(
            kernel,
            out_shape=outs,
            in_specs=[IN_VMEM] * len(ins),
            out_specs=[IN_VMEM] * len(outs),
            compiler_params=params(),
            name=name,
        )(*ins)
    )
    return [[next(results) for _ in out_shapes] for _, _, out_shapes in tasks]


def weights_kernel(bits, width, *refs):
    count = 1 + bits
    sent, acts = refs[:count], refs[count : 2 * count]
    in_hbm, out_hbm, in_ref, out_ref, sems = refs[2 * count :]
    slots = acts[0].shape[0]
    me = lax.axis_index("dp")
    quarter = width // 2**bits
    x, dy = [], []
    for index, ref in enumerate(sent):
        if index == 0:
            block = ref[...]
        else:
            base = column_start(me, bits, index - 1, width, False)
            block = ref[:, lanes(me * quarter - base, quarter)]
        for at in range(0, block.shape[0], 2 * slots):
            x.append(block[at : at + slots])
            dy.append(block[at + slots : at + 2 * slots])
    x, dy = jnp.concatenate(x, axis=0), jnp.concatenate(dy, axis=0)
    columns = jnp.concatenate([ref[...] for ref in acts], axis=0).T
    copies = []
    start = 0
    for values, target, staged in ((x, in_hbm, in_ref), (dy, out_hbm, out_ref)):
        for at, size in cuts_of(target.shape[0]):
            here = pl.ds(at, size)
            staged[here, :] = jnp.dot(
                columns[start + at : start + at + size], values, preferred_element_type=F32
            ).astype(BF16)
            copy = pltpu.make_async_copy(
                staged.at[here, :], target.at[here, :], sems.at[len(copies)]
            )
            copy.start()
            copies.append(copy)
        start += target.shape[0]
    for copy in copies:
        copy.wait()


def tokens_kernel(units, capacity, assign_ref, keep_ref, recv_ref, out_ref):
    columns = units * capacity
    bits = bits_of(units)
    width, tokens = assign_ref.shape
    slices = units // min(LAYER_EXPERTS, units)
    token_at = lax.broadcasted_iota(jnp.int32, (tokens, columns), 0)
    column_at = lax.broadcasted_iota(jnp.int32, (tokens, columns), 1)
    selector = jnp.zeros((tokens, columns), F32)
    my_unit = lax.axis_index("expert")
    for token in range(tokens):
        for k in range(width):
            expert = assign_ref[k, token]
            rank = jnp.int32(0)
            for earlier in range(token):
                for other in range(width):
                    rank = rank + (assign_ref[other, earlier] == expert).astype(jnp.int32)
            for piece in range(slices):
                apart = (expert * slices + piece) ^ my_unit
                place = jnp.int32(0)
                for bit in range(bits):
                    place = place * 2 + (lax.shift_right_logical(apart, jnp.int32(bit)) & 1)
                hit = (token_at == token) & (column_at == place * capacity + rank)
                selector = jnp.where(hit, selector + 1.0, selector)
    rows = jnp.concatenate([keep_ref[...].astype(F32), recv_ref[...].astype(F32)], axis=0)
    out_ref[...] = jnp.dot(
        selector.astype(BF16), rows.astype(BF16), preferred_element_type=F32
    ).astype(BF16)


def swap(array, axis, bit):
    return lax.ppermute(array, axis, [(i, i ^ bit) for i in range(lax.axis_size(axis))])


def per_device(x_rows, dy_rows, w_in, w_out, counts, assign):
    slots, width = x_rows.shape
    hidden_units = w_out.shape[2]
    groups = lax.axis_size("dp")
    units = lax.axis_size("expert")
    parts = lax.axis_size("mp")
    owners = counts.shape[1]
    capacity = slots // owners
    quarter = width // groups
    share = width // parts
    dp_bits, unit_bits, part_bits = bits_of(groups), bits_of(units), bits_of(parts)

    split = pl.pallas_call(
        functools.partial(split_kernel, dp_bits),
        out_shape=[shape((2 * slots, width // 2 ** (i + 1))) for i in range(dp_bits)]
        + [shape((2 * slots, quarter))],
        in_specs=[IN_HBM, IN_HBM],
        out_specs=[ANY] * (dp_bits + 1),
        scratch_shapes=[pltpu.SemaphoreType.DMA((2 * dp_bits + 2,))],
        compiler_params=params(),
        cost_estimate=pl.CostEstimate(flops=0, bytes_accessed=2**19, transcendentals=0),
        name="split_rows",
    )(x_rows, dy_rows)
    sent = [split[dp_bits], swap(split[0], "dp", groups // 2)]

    w_flat = jnp.transpose(w_in[0], (1, 2, 0)).reshape(2 * hidden_units, width)
    w_down = jnp.transpose(w_out[0], (1, 0))
    copies = 3 + len(cuts_of(2 * hidden_units)) + len(cuts_of(hidden_units))
    acts, keep, send = pl.pallas_call(
        functools.partial(acts_kernel, parts),
        out_shape=[
            shape((slots, 3 * hidden_units)),
            shape((slots, width // 2), F32),
            shape((slots, width // 2)),
        ],
        in_specs=[IN_HBM] * 5,
        out_specs=[IN_VMEM] * 3,
        scratch_shapes=[
            pltpu.VMEM(x_rows.shape, BF16),
            pltpu.VMEM(dy_rows.shape, BF16),
            pltpu.VMEM(w_flat.shape, BF16),
            pltpu.VMEM(w_down.shape, BF16),
            pltpu.SMEM(counts.shape, jnp.int32),
            pltpu.VMEM((slots, width), F32),
            pltpu.SemaphoreType.DMA((copies,)),
        ],
        compiler_params=params(),
        cost_estimate=pl.CostEstimate(
            flops=2 * 256 * width * 5 * hidden_units,
            bytes_accessed=6 * hidden_units * width,
            transcendentals=0,
        ),
        name="acts_and_rows",
    )(x_rows, dy_rows, w_flat, w_down, counts)

    acts_all = [acts]
    swaps = [("mp", parts >> (i + 1)) for i in range(part_bits)]
    swaps += [("expert", units >> (i + 1)) for i in range(unit_bits)]
    rows_held = slots
    for step in range(max(len(swaps), dp_bits)):
        tasks = []
        if step > 0:
            if step < len(swaps):
                if step < part_bits:
                    body = sum_task(part_bits, step - 1, width)
                    out = (slots, width >> (step + 1))
                elif step == part_bits:
                    body = sum_task(part_bits, step - 1, width)
                    out = (slots // 2, share)
                else:
                    past = step - part_bits
                    body = deal_task(owners >> past, capacity << (past - 1))
                    out = (slots // 2, share)
                tasks.append((body, [keep, recv], [shape(out, F32), shape(out)]))
            if step < dp_bits:
                tasks.append((stack_task, acts_all, [shape((slots << step, 3 * hidden_units))]))
                tasks.append(
                    (
                        columns_task(dp_bits, step, width),
                        [split[step]] + sent[1:],
                        [shape((2 * slots << step, width >> (step + 1)))],
                    )
                )
            results = run_tasks(tasks, "merge%d" % step)
            if step < len(swaps):
                keep, send = results[0]
        if step < len(swaps):
            recv = swap(send, *swaps[step])
        if step < dp_bits:
            bit = groups >> (step + 1)
            acts_all.append(swap(acts if step == 0 else results[-2][0], "dp", bit))
            if step > 0:
                sent.append(swap(results[-1][0], "dp", bit))

    grad_in, grad_out = pl.pallas_call(
        functools.partial(weights_kernel, dp_bits, width),
        out_shape=[shape((2 * hidden_units, quarter)), shape((hidden_units, quarter))],
        in_specs=[IN_VMEM] * (2 + 2 * dp_bits),
        out_specs=[ANY, ANY],
        scratch_shapes=[
            pltpu.VMEM((2 * hidden_units, quarter), BF16),
            pltpu.VMEM((hidden_units, quarter), BF16),
            pltpu.SemaphoreType.DMA((len(cuts_of(2 * hidden_units)) + len(cuts_of(hidden_units)),)),
        ],
        compiler_params=params(),
        cost_estimate=pl.CostEstimate(
            flops=2 * 256 * quarter * 3 * hidden_units,
            bytes_accessed=6 * hidden_units * quarter,
            transcendentals=0,
        ),
        name="weight_grads",
    )(*sent, *acts_all)

    grad_tokens = pl.pallas_call(
        functools.partial(tokens_kernel, units, capacity),
        out_shape=shape((assign.shape[0], share)),
        in_specs=[IN_SMEM, IN_VMEM, IN_VMEM],
        out_specs=IN_VMEM,
        compiler_params=params(),
        name="token_grads",
    )(assign.T, keep, recv)

    grad_w_in = grad_in.reshape(2, hidden_units, quarter).transpose(2, 0, 1)[None]
    grad_w_out = grad_out.transpose(1, 0)[None]
    return (grad_w_in, grad_w_out, grad_tokens)


def solution(mesh):
    return jax.shard_map(
        per_device,
        mesh=mesh,
        in_specs=(
            P(("dp", "expert"), None),
            P(("dp", "expert"), None),
            P("expert", None, None, "mp"),
            P("expert", None, "mp"),
            P(("dp", "expert"), None),
            P(("dp", "expert"), None),
        ),
        out_specs=(
            P("expert", "dp", None, "mp"),
            P("expert", "dp", "mp"),
            P(("dp", "expert"), "mp"),
        ),
        check_vma=False,
    )
```

time: 38.8 us -> 32.1 us (0.83)
  starting transfers between devices: 15.8 us -> 9.68 us
  waiting for transfers between devices: 8.71 us -> 8.01 us
    ppermute x13 -> x7, starting transfers between devices: 15.8 us -> 9.68 us  [swap(): lax.ppermute(array, axis, [(i, i ^ bit) for i in range(lax.axis_size(axis...]
    ppermute x13 -> x7, waiting for transfers between devices: 8.71 us -> 8.01 us  [swap(): lax.ppermute(array, axis, [(i, i ^ bit) for i in range(lax.axis_size(axis...]
    pallas_call x4 -> x6, Pallas kernels: 9.43 us -> 9.45 us  [the longest x1 6.43 us: per_device(): pl.pallas_call(functools.partial(acts_kernel, parts), out_shape=[shape((s...]
  transfers between devices with their start and end apart: 13 -> 7, of which waited for: 5 -> 3; matrix products, arithmetic and copies ran while one was open for 0% -> 0% of each run, Pallas kernels for 4% -> 24%
where the time goes in v3:
time: 32.1 us; the launch traced here: 31.8 us
  starting transfers between devices  9.68 us (30%)
  Pallas kernels  9.45 us (29%)
  waiting for transfers between devices  8.01 us (25%)
  local copies, waits for them, and re-layouts  4.02 us (13%)
  between operations  0.68 us (2%)
    ppermute x7, starting transfers between devices, swap(): lax.ppermute(array, axis, [(i, i ^ bit) for i in range(lax.axis_size(axis...  9.68 us
    ppermute x7, waiting for transfers between devices, swap(): lax.ppermute(array, axis, [(i, i ^ bit) for i in range(lax.axis_size(axis...  8.01 us
    pallas_call x1, Pallas kernels, per_device(): pl.pallas_call(functools.partial(acts_kernel, parts), out_shape=[shape((s...  6.43 us
    unnamed x10, local copies, waits for them, and re-layouts  4.02 us
    pallas_call x1, Pallas kernels, per_device(): pl.pallas_call(functools.partial(weights_kernel, dp_bits, width), out_sha...  1.48 us
    pallas_call x1, Pallas kernels, per_device(): pl.pallas_call(functools.partial(tokens_kernel, units, capacity), out_sha...  1.32 us
  transfers between devices with their start and end apart: 7, of which 3 were waited for; matrix products, arithmetic and copies ran while one was open for 0% of the time, Pallas kernels for 24%

profile of v3, /device:TPU:0, one launch (start us, length us, event | category | flops | bytes accessed | tf_op | source)
XLA Modules:
  0.0 31.8 jit_solution(9097615874640467749)
XLA Ops:
  0.6 0.0 copy-start
  0.6 0.9 %copy-done = bf16[16,3072]{1,0:T(8,128)(2,1)S(1)} copy-done((bf16[16,3072]{1,0:T(8,128)(2,1)S(1)}, bf16[16,3072]{1,0:T(8,128)(2,1)}, u32[]{:S(2)}) %copy-start) | copy-done | bytes 98328
  1.5 0.0 copy-start.1
  1.5 0.9 %copy-done.1 = bf16[16,3072]{1,0:T(8,128)(2,1)S(1)} copy-done((bf16[16,3072]{1,0:T(8,128)(2,1)S(1)}, bf16[16,3072]{1,0:T(8,128)(2,1)}, u32[]{:S(2)}) %copy-start.1) | copy-done | bytes 98328
  2.4 0.2 split_rows.1
  2.6 4.1 %collective-permute-start = (bf16[32,1536]{1,0:T(8,128)(2,1)S(1)}, bf16[32,1536]{1,0:T(8,128)(2,1)S(1)}, u32[]{:S(2)}, u32[]{:S(2)}) collective-permute-start(bf16[32,1536]{1,0:T(8,128)(2,1)S(1)} %get-tuple-element.18), channel_id=1, source_target_pairs={{0,16},{8,24},{16,0},{24,8},{1,17},{9,25},{17,1},{25,9},{2,18},{10... | collective-permute-start | bytes 294920 | tf_op jit(solution)/shard_map/ppermute | solution.py:306
  6.7 0.0 copy-start.3
  6.7 1.6 %copy-done.3 = bf16[1,3072,336]{1,2,0:T(8,128)(2,1)S(1)} copy-done((bf16[1,3072,336]{1,2,0:T(8,128)(2,1)S(1)}, bf16[1,3072,336]{1,2,0:T(8,128)(2,1)}, u32[]{:S(2)}) %copy-start.3) | copy-done | bytes 2064408
  8.3 0.0 copy-start.4
  8.3 0.7 %copy-done.4 = s32[1,4]{1,0:T(1,128)S(1)} copy-done((s32[1,4]{1,0:T(1,128)S(1)}, s32[1,4]{1,0:T(1,128)}, u32[]{:S(2)}) %copy-start.4) | copy-done | bytes 40
  8.9 0.0 copy-start.2
  8.9 6.4 %acts_and_rows.1 = (bf16[16,1008]{1,0:T(8,128)(2,1)S(1)}, f32[16,1536]{1,0:T(8,128)S(1)}, bf16[16,1536]{1,0:T(8,128)(2,1)S(1)}) custom-call(bf16[16,3072]{1,0:T(8,128)(2,1)S(1)} %copy-done, bf16[16,3072]{1,0:T(8,128)(2,1)S(1)} %copy-done.1, bf16[672,3072]{1,0:T(8,128)(2,1)} %bitcast.19, bf16[336,3072]{1,0:T(8,128)(2,1)S(1)} %bitcast.18, s32[1,4]{1,0:T(1,128)S(1)} %copy-done.4), custom_call_target="tpu_custom_call" | custom-call | flops 2642411520 | bytes 6193152 | tf_op jit(solution)/shard_map/acts_and_rows/pallas_call | solution.py:337
  15.4 1.6 %collective-permute-start.1 = (bf16[16,1536]{1,0:T(8,128)(2,1)S(1)}, bf16[16,1536]{1,0:T(8,128)(2,1)S(1)}, u32[]{:S(2)}, u32[]{:S(2)}) collective-permute-start(bf16[16,1536]{1,0:T(8,128)(2,1)S(1)} %get-tuple-element.20), channel_id=1, source_target_pairs={{0,1},{1,0},{2,3},{3,2},{4,5},{5,4},{6,7},{7,6},{8,9},{9,8},{10,11... | collective-permute-start | bytes 147464 | tf_op jit(solution)/shard_map/ppermute | solution.py:306
  17.0 0.3 %collective-permute-start.2 = (bf16[16,1008]{1,0:T(8,128)(2,1)S(1)}, bf16[16,1008]{1,0:T(8,128)(2,1)S(1)}, u32[]{:S(2)}, u32[]{:S(2)}) collective-permute-start(bf16[16,1008]{1,0:T(8,128)(2,1)S(1)} %get-tuple-element.21.refs_2_.refs_3_), channel_id=1, source_target_pairs={{0,16},{8,24},{16,0},{24,8},{1,17},{9,25},{17,1},{25,9},{2,18},{10... | collective-permute-start | bytes 96776 | tf_op jit(solution)/shard_map/ppermute | solution.py:306
  17.3 4.5 %collective-permute-done.2.refs_3_.refs_4_ = bf16[16,1008]{1,0:T(8,128)(2,1)S(1)} collective-permute-done((bf16[16,1008]{1,0:T(8,128)(2,1)S(1)}, bf16[16,1008]{1,0:T(8,128)(2,1)S(1)}, u32[]{:S(2)}, u32[]{:S(2)}) %collective-permute-start.2) | collective-permute-done | bytes 32288 | tf_op jit(solution)/shard_map/ppermute | solution.py:306
  21.8 0.0 collective-permute-done.1.refs_1_
  21.8 0.0 collective-permute-done.refs_5_.refs_1_
  21.8 2.0 %collective-permute-start.3 = (bf16[64,768]{1,0:T(8,128)(2,1)S(1)}, bf16[64,768]{1,0:T(8,128)(2,1)S(1)}, u32[]{:S(2)}, u32[]{:S(2)}) collective-permute-start(bf16[64,768]{1,0:T(8,128)(2,1)S(1)} %get-tuple-element.23), channel_id=1, source_target_pairs={{0,8},{8,0},{16,24},{24,16},{1,9},{9,1},{17,25},{25,17},{2,10},{10... | collective-permute-start | bytes 294920 | tf_op jit(solution)/shard_map/ppermute | solution.py:306
  23.8 0.1 collective-permute-start.4
  23.9 1.5 %collective-permute-start.5 = (bf16[8,1536]{1,0:T(8,128)(2,1)S(1)}, bf16[8,1536]{1,0:T(8,128)(2,1)S(1)}, u32[]{:S(2)}, u32[]{:S(2)}) collective-permute-start(bf16[8,1536]{1,0:T(8,128)(2,1)S(1)} %get-tuple-element.28), channel_id=1, source_target_pairs={{0,4},{2,6},{4,0},{6,2},{1,5},{3,7},{5,1},{7,3},{8,12},{10,14},{12... | collective-permute-start | bytes 73736 | tf_op jit(solution)/shard_map/ppermute | solution.py:306
  25.4 2.3 %collective-permute-done.5.refs_1_ = bf16[8,1536]{1,0:T(8,128)(2,1)S(1)} collective-permute-done((bf16[8,1536]{1,0:T(8,128)(2,1)S(1)}, bf16[8,1536]{1,0:T(8,128)(2,1)S(1)}, u32[]{:S(2)}, u32[]{:S(2)}) %collective-permute-start.5) | collective-permute-done | bytes 24608 | tf_op jit(solution)/shard_map/ppermute | solution.py:306
  27.8 0.1 collective-permute-start.6
  27.8 1.2 %collective-permute-done.6.recv_ref = bf16[8,1536]{1,0:T(8,128)(2,1)S(1)} collective-permute-done((bf16[8,1536]{1,0:T(8,128)(2,1)S(1)}, bf16[8,1536]{1,0:T(8,128)(2,1)S(1)}, u32[]{:S(2)}, u32[]{:S(2)}) %collective-permute-start.6) | collective-permute-done | bytes 24608 | tf_op jit(solution)/shard_map/ppermute | solution.py:306
  29.0 0.0 copy-done.2
  29.0 1.3 %token_grads.1 = bf16[4,1536]{1,0:T(4,128)(2,1)} custom-call(s32[2,4]{1,0:T(2,128)S(1)} %bitcast.17, f32[8,1536]{1,0:T(8,128)S(1)} %get-tuple-element.29.keep_ref, bf16[8,1536]{1,0:T(8,128)(2,1)S(1)} %collective-permute-done.6.recv_ref), custom_call_target="tpu_custom_call" | custom-call | tf_op jit(solution)/shard_map/token_grads/pallas_call | solution.py:422
  30.3 0.0 collective-permute-done.4.refs_5_
  30.3 0.0 collective-permute-done.3.refs_2_
  30.4 1.5 %weight_grads.1 = (bf16[672,768]{1,0:T(8,128)(2,1)}, bf16[336,768]{1,0:T(8,128)(2,1)}) custom-call(bf16[32,768]{1,0:T(8,128)(2,1)S(1)} %get-tuple-element.17.refs_0_, bf16[32,1536]{1,0:T(8,128)(2,1)S(1)} %collective-permute-done.refs_5_.refs_1_, bf16[64,768]{1,0:T(8,128)(2,1)S(1)} %collective-permute-done.3.refs_2_, ...), custom_call_target="tpu_custom_call" | custom-call | flops 396361728 | bytes 1548288 | tf_op jit(solution)/shard_map/weight_grads/pallas_call | solution.py:403
  (2 shorter events, 0.0 us)
Async XLA Ops:
  0.6 0.9 %copy-start = (bf16[16,3072]{1,0:T(8,128)(2,1)S(1)}, bf16[16,3072]{1,0:T(8,128)(2,1)}, u32[]{:S(2)}) copy-start(bf16[16,3072]{1,0:T(8,128)(2,1)} %refs_0_.1) | copy-start | bytes 294916
  1.5 0.9 %copy-start.1 = (bf16[16,3072]{1,0:T(8,128)(2,1)S(1)}, bf16[16,3072]{1,0:T(8,128)(2,1)}, u32[]{:S(2)}) copy-start(bf16[16,3072]{1,0:T(8,128)(2,1)} %refs_1_.1) | copy-start | bytes 294916
  2.6 19.2 %collective-permute-start = (bf16[32,1536]{1,0:T(8,128)(2,1)S(1)}, bf16[32,1536]{1,0:T(8,128)(2,1)S(1)}, u32[]{:S(2)}, u32[]{:S(2)}) collective-permute-start(bf16[32,1536]{1,0:T(8,128)(2,1)S(1)} %get-tuple-element.18), channel_id=1, source_target_pairs={{0,16},{8,24},{16,0},{24,8},{1,17},{9,25},{17,1},{25,9},{2,18},{10... | collective-permute-start | bytes 294920 | tf_op jit(solution)/shard_map/ppermute | solution.py:306
  6.7 1.6 %copy-start.3 = (bf16[1,3072,336]{1,2,0:T(8,128)(2,1)S(1)}, bf16[1,3072,336]{1,2,0:T(8,128)(2,1)}, u32[]{:S(2)}) copy-start(bf16[1,3072,336]{1,2,0:T(8,128)(2,1)} %param.9) | copy-start | bytes 6193156
  8.3 0.7 %copy-start.4 = (s32[1,4]{1,0:T(1,128)S(1)}, s32[1,4]{1,0:T(1,128)}, u32[]{:S(2)}) copy-start(s32[1,4]{1,0:T(1,128)} %refs_4_.1) | copy-start | bytes 52
  8.9 20.1 %copy-start.2 = (s32[4,2]{0,1:T(2,128)S(1)}, s32[4,2]{0,1:T(2,128)}, u32[]{:S(2)}) copy-start(s32[4,2]{0,1:T(2,128)} %param.11) | copy-start | bytes 100
  15.4 6.4 %collective-permute-start.1 = (bf16[16,1536]{1,0:T(8,128)(2,1)S(1)}, bf16[16,1536]{1,0:T(8,128)(2,1)S(1)}, u32[]{:S(2)}, u32[]{:S(2)}) collective-permute-start(bf16[16,1536]{1,0:T(8,128)(2,1)S(1)} %get-tuple-element.20), channel_id=1, source_target_pairs={{0,1},{1,0},{2,3},{3,2},{4,5},{5,4},{6,7},{7,6},{8,9},{9,8},{10,11... | collective-permute-start | bytes 147464 | tf_op jit(solution)/shard_map/ppermute | solution.py:306
  17.0 4.8 %collective-permute-start.2 = (bf16[16,1008]{1,0:T(8,128)(2,1)S(1)}, bf16[16,1008]{1,0:T(8,128)(2,1)S(1)}, u32[]{:S(2)}, u32[]{:S(2)}) collective-permute-start(bf16[16,1008]{1,0:T(8,128)(2,1)S(1)} %get-tuple-element.21.refs_2_.refs_3_), channel_id=1, source_target_pairs={{0,16},{8,24},{16,0},{24,8},{1,17},{9,25},{17,1},{25,9},{2,18},{10... | collective-permute-start | bytes 96776 | tf_op jit(solution)/shard_map/ppermute | solution.py:306
  21.8 8.5 %collective-permute-start.3 = (bf16[64,768]{1,0:T(8,128)(2,1)S(1)}, bf16[64,768]{1,0:T(8,128)(2,1)S(1)}, u32[]{:S(2)}, u32[]{:S(2)}) collective-permute-start(bf16[64,768]{1,0:T(8,128)(2,1)S(1)} %get-tuple-element.23), channel_id=1, source_target_pairs={{0,8},{8,0},{16,24},{24,16},{1,9},{9,1},{17,25},{25,17},{2,10},{10... | collective-permute-start | bytes 294920 | tf_op jit(solution)/shard_map/ppermute | solution.py:306
  23.8 6.5 %collective-permute-start.4 = (bf16[32,1008]{1,0:T(8,128)(2,1)S(1)}, bf16[32,1008]{1,0:T(8,128)(2,1)S(1)}, u32[]{:S(2)}, u32[]{:S(2)}) collective-permute-start(bf16[32,1008]{1,0:T(8,128)(2,1)S(1)} %get-tuple-element.24), channel_id=1, source_target_pairs={{0,8},{8,0},{16,24},{24,16},{1,9},{9,1},{17,25},{25,17},{2,10},{10... | collective-permute-start | bytes 193544 | tf_op jit(solution)/shard_map/ppermute | solution.py:306
  23.9 3.8 %collective-permute-start.5 = (bf16[8,1536]{1,0:T(8,128)(2,1)S(1)}, bf16[8,1536]{1,0:T(8,128)(2,1)S(1)}, u32[]{:S(2)}, u32[]{:S(2)}) collective-permute-start(bf16[8,1536]{1,0:T(8,128)(2,1)S(1)} %get-tuple-element.28), channel_id=1, source_target_pairs={{0,4},{2,6},{4,0},{6,2},{1,5},{3,7},{5,1},{7,3},{8,12},{10,14},{12... | collective-permute-start | bytes 73736 | tf_op jit(solution)/shard_map/ppermute | solution.py:306
  27.8 1.3 %collective-permute-start.6 = (bf16[8,1536]{1,0:T(8,128)(2,1)S(1)}, bf16[8,1536]{1,0:T(8,128)(2,1)S(1)}, u32[]{:S(2)}, u32[]{:S(2)}) collective-permute-start(bf16[8,1536]{1,0:T(8,128)(2,1)S(1)} %get-tuple-element.30), channel_id=1, source_target_pairs={{0,2},{2,0},{4,6},{6,4},{1,3},{3,1},{5,7},{7,5},{8,10},{10,8},{12,... | collective-permute-start | bytes 73736 | tf_op jit(solution)/shard_map/ppermute | solution.py:306

commit v4 on v3

--- a/solution.py
+++ b/solution.py
@@ -16,7 +16,6 @@
 ANY = pl.BlockSpec(memory_space=pl.ANY)
 IN_HBM = pl.BlockSpec(memory_space=pltpu.HBM)
 IN_VMEM = pl.BlockSpec(memory_space=pltpu.VMEM)
-IN_SMEM = pl.BlockSpec(memory_space=pltpu.SMEM)
 
 
 def shape(dims, dtype=BF16):
@@ -71,51 +70,9 @@
         copy.wait()
 
 
-def acts_kernel(parts, *refs):
-    x_hbm, dy_hbm, w_in_hbm, w_out_hbm, counts_hbm = refs[:5]
-    acts_ref, keep_ref, send_ref = refs[5:8]
-    x_ref, dy_ref, w_in_ref, w_out_ref, counts_ref, rows_ref, sems = refs[8:]
-
-    in_cuts = cuts_of(w_in_ref.shape[0])
-    out_cuts = cuts_of(w_out_ref.shape[0])
-    plan = [(x_hbm, x_ref)]
-    plan += [(w_in_hbm.at[pl.ds(a, n), :], w_in_ref.at[pl.ds(a, n), :]) for a, n in in_cuts]
-    plan += [(dy_hbm, dy_ref)]
-    plan += [(w_out_hbm.at[pl.ds(a, n), :], w_out_ref.at[pl.ds(a, n), :]) for a, n in out_cuts]
-    plan += [(counts_hbm, counts_ref)]
-    copies = [pltpu.make_async_copy(s, d, sems.at[i]) for i, (s, d) in enumerate(plan)]
-    for copy in copies:
-        copy.start()
-    copies = iter(copies)
-
-    next(copies).wait()
-    x = x_ref[...]
-    pre = []
-    for at, size in in_cuts:
-        next(copies).wait()
-        pre.append(
-            lax.dot_general(
-                x, w_in_ref[pl.ds(at, size), :], CONTRACT_LAST, preferred_element_type=F32
-            )
-        )
-    pre = jnp.concatenate(pre, axis=1)
-    next(copies).wait()
-    dy = dy_ref[...]
-    grad_hidden = []
-    for at, size in out_cuts:
-        next(copies).wait()
-        grad_hidden.append(
-            lax.dot_general(
-                dy, w_out_ref[pl.ds(at, size), :], CONTRACT_LAST, preferred_element_type=F32
-            )
-        )
-    grad_hidden = jnp.concatenate(grad_hidden, axis=1)
-
-    next(copies).wait()
-    slots = x_ref.shape[0]
+def pick_matrix(counts_ref, slots, my_unit):
     owners = counts_ref.shape[1]
     capacity = slots // owners
-    my_unit = lax.axis_index("expert")
     row_at = lax.broadcasted_iota(jnp.int32, (slots, slots), 0)
     slot_at = lax.broadcasted_iota(jnp.int32, (slots, slots), 1)
     pick = jnp.zeros((slots, slots), F32)
@@ -126,32 +83,105 @@
         hit = (row_at >= first) & (row_at < first + held) & (slot_at - row_at == total - first)
         pick = jnp.where(hit, 1.0, pick)
         total = total + held
-
-    units_here = w_out_ref.shape[0]
-    gate_pre, up_pre = pre[:, :units_here], pre[:, units_here:]
-    live = lax.broadcasted_iota(jnp.int32, gate_pre.shape, 0) < total
-    live_mask = jnp.where(live, 1.0, 0.0)
-    sigmoid_gate = jax.nn.sigmoid(gate_pre)
-    hidden = live_mask * gate_pre * sigmoid_gate * up_pre
-    grad_gate = (
-        live_mask * grad_hidden * up_pre * sigmoid_gate * (1.0 + gate_pre * (1.0 - sigmoid_gate))
-    )
-    grad_up = live_mask * grad_hidden * gate_pre * sigmoid_gate
-    grad_pre = jnp.concatenate([grad_gate, grad_up], axis=1).astype(BF16)
-    acts_ref[...] = jnp.concatenate([grad_gate, grad_up, hidden], axis=1).astype(BF16)
-
-    picked = jnp.dot(pick.astype(BF16), grad_pre, preferred_element_type=F32).astype(BF16)
-    width = w_in_ref.shape[1]
-    for at, size in cuts_of(width, 512, 128):
-        rows_ref[:, pl.ds(at, size)] = jnp.dot(
-            picked, w_in_ref[:, pl.ds(at, size)], preferred_element_type=F32
+    return pick
+
+
+def token_selector(assign_ref, units, capacity, my_unit):
+    bits = bits_of(units)
+    width, tokens = assign_ref.shape
+    slices = units // min(LAYER_EXPERTS, units)
+    dims = (tokens, units * capacity)
+    token_at = lax.broadcasted_iota(jnp.int32, dims, 0)
+    column_at = lax.broadcasted_iota(jnp.int32, dims, 1)
+    selector = jnp.zeros(dims, F32)
+    for token in range(tokens):
+        for k in range(width):
+            expert = assign_ref[k, token]
+            rank = jnp.int32(0)
+            for earlier in range(token):
+                for other in range(width):
+                    rank = rank + (assign_ref[other, earlier] == expert).astype(jnp.int32)
+            for piece in range(slices):
+                apart = (expert * slices + piece) ^ my_unit
+                place = jnp.int32(0)
+                for bit in range(bits):
+                    place = place * 2 + (lax.shift_right_logical(apart, jnp.int32(bit)) & 1)
+                hit = (token_at == token) & (column_at == place * capacity + rank)
+                selector = jnp.where(hit, selector + 1.0, selector)
+    return selector
+
+
+def acts_kernel(units, parts, *refs):
+    x_hbm, dy_hbm, w_in_hbm, w_out_hbm, counts_hbm, assign_hbm = refs[:6]
+    acts_ref, keep_ref, send_ref, selector_ref = refs[6:10]
+    x_ref, dy_ref, w_in_ref, w_out_ref, counts_ref, assign_ref, rows_ref, sems = refs[10:]
+
+    hidden_units, width = w_out_ref.shape
+    cuts = cuts_of(hidden_units, 128)
+    plan = [(counts_hbm, counts_ref), (x_hbm, x_ref), (dy_hbm, dy_ref)]
+    for at, size in cuts:
+        for half in range(2):
+            plan.append(
+                (
+                    w_in_hbm.at[pl.ds(half * hidden_units + at, size), :],
+                    w_in_ref.at[pl.ds(2 * at + half * size, size), :],
+                )
+            )
+        plan.append((w_out_hbm.at[pl.ds(at, size), :], w_out_ref.at[pl.ds(at, size), :]))
+    plan.append((assign_hbm, assign_ref))
+    copies = [pltpu.make_async_copy(s, d, sems.at[i]) for i, (s, d) in enumerate(plan)]
+    for copy in copies:
+        copy.start()
+    copies = iter(copies)
+
+    slots = x_ref.shape[0]
+    capacity = slots // counts_ref.shape[1]
+    my_unit = lax.axis_index("expert")
+    next(copies).wait()
+    pick = pick_matrix(counts_ref, slots, my_unit)
+    back = pick.T.astype(BF16)
+    pick = pick.astype(BF16)
+    next(copies).wait()
+    x = jnp.dot(pick, x_ref[...], preferred_element_type=F32).astype(BF16)
+    next(copies).wait()
+    dy = jnp.dot(pick, dy_ref[...], preferred_element_type=F32).astype(BF16)
+
+    gates, ups, hiddens = [], [], []
+    for at, size in cuts:
+        next(copies).wait()
+        next(copies).wait()
+        w_both = w_in_ref.at[pl.ds(2 * at, 2 * size), :]
+        pre = lax.dot_general(x, w_both[...], CONTRACT_LAST, preferred_element_type=F32)
+        next(copies).wait()
+        grad_hidden = lax.dot_general(
+            dy, w_out_ref[pl.ds(at, size), :], CONTRACT_LAST, preferred_element_type=F32
         )
+        gate_pre, up_pre = pre[:, :size], pre[:, size:]
+        sigmoid_gate = jax.nn.sigmoid(gate_pre)
+        hidden = gate_pre * sigmoid_gate * up_pre
+        grad_gate = grad_hidden * up_pre * sigmoid_gate * (1.0 + gate_pre * (1.0 - sigmoid_gate))
+        grad_up = grad_hidden * gate_pre * sigmoid_gate
+        grad_pre = jnp.concatenate([grad_gate, grad_up], axis=1).astype(BF16)
+        for left, count in cuts_of(width, 1024, 128):
+            here = pl.ds(left, count)
+            part = jnp.dot(grad_pre, w_both[:, here], preferred_element_type=F32)
+            if at:
+                part = part + rows_ref[:, here]
+            rows_ref[:, here] = part
+        gates.append(grad_gate)
+        ups.append(grad_up)
+        hiddens.append(hidden)
+    acts = jnp.concatenate(gates + ups + hiddens, axis=1).astype(BF16)
+    acts_ref[...] = jnp.dot(back, acts, preferred_element_type=F32).astype(BF16)
+
     my_part = lax.axis_index("mp")
     bits = bits_of(parts)
     keep_ref[...] = rows_ref[:, lanes(column_start(my_part, bits, 0, width, False), width // 2)]
     send_ref[...] = rows_ref[
         :, lanes(column_start(my_part, bits, 0, width, True), width // 2)
     ].astype(BF16)
+    next(copies).wait()
+    selector_ref[...] = token_selector(assign_ref, units, capacity, my_unit)
 
 
 def sum_task(bits, step, width):
@@ -273,33 +303,15 @@
         copy.wait()
 
 
-def tokens_kernel(units, capacity, assign_ref, keep_ref, recv_ref, out_ref):
-    columns = units * capacity
-    bits = bits_of(units)
-    width, tokens = assign_ref.shape
-    slices = units // min(LAYER_EXPERTS, units)
-    token_at = lax.broadcasted_iota(jnp.int32, (tokens, columns), 0)
-    column_at = lax.broadcasted_iota(jnp.int32, (tokens, columns), 1)
-    selector = jnp.zeros((tokens, columns), F32)
-    my_unit = lax.axis_index("expert")
-    for token in range(tokens):
-        for k in range(width):
-            expert = assign_ref[k, token]
-            rank = jnp.int32(0)
-            for earlier in range(token):
-                for other in range(width):
-                    rank = rank + (assign_ref[other, earlier] == expert).astype(jnp.int32)
-            for piece in range(slices):
-                apart = (expert * slices + piece) ^ my_unit
-                place = jnp.int32(0)
-                for bit in range(bits):
-                    place = place * 2 + (lax.shift_right_logical(apart, jnp.int32(bit)) & 1)
-                hit = (token_at == token) & (column_at == place * capacity + rank)
-                selector = jnp.where(hit, selector + 1.0, selector)
+def tokens_kernel(selector_ref, keep_ref, recv_ref, out_ref):
     rows = jnp.concatenate([keep_ref[...].astype(F32), recv_ref[...].astype(F32)], axis=0)
     out_ref[...] = jnp.dot(
-        selector.astype(BF16), rows.astype(BF16), preferred_element_type=F32
+        selector_ref[...].astype(BF16), rows.astype(BF16), preferred_element_type=F32
     ).astype(BF16)
+
+
+def in_hbm(array):
+    return pltpu.with_memory_space_constraint(array, pltpu.HBM)
 
 
 def swap(array, axis, bit):
@@ -328,27 +340,29 @@
         compiler_params=params(),
         cost_estimate=pl.CostEstimate(flops=0, bytes_accessed=2**19, transcendentals=0),
         name="split_rows",
-    )(x_rows, dy_rows)
+    )(in_hbm(x_rows), in_hbm(dy_rows))
     sent = [split[dp_bits], swap(split[0], "dp", groups // 2)]
 
     w_flat = jnp.transpose(w_in[0], (1, 2, 0)).reshape(2 * hidden_units, width)
     w_down = jnp.transpose(w_out[0], (1, 0))
-    copies = 3 + len(cuts_of(2 * hidden_units)) + len(cuts_of(hidden_units))
-    acts, keep, send = pl.pallas_call(
-        functools.partial(acts_kernel, parts),
+    copies = 4 + 3 * len(cuts_of(hidden_units, 128))
+    acts, keep, send, selector = pl.pallas_call(
+        functools.partial(acts_kernel, units, parts),
         out_shape=[
             shape((slots, 3 * hidden_units)),
             shape((slots, width // 2), F32),
             shape((slots, width // 2)),
+            shape((assign.shape[0], slots), F32),
         ],
-        in_specs=[IN_HBM] * 5,
-        out_specs=[IN_VMEM] * 3,
+        in_specs=[IN_HBM] * 6,
+        out_specs=[IN_VMEM] * 4,
         scratch_shapes=[
             pltpu.VMEM(x_rows.shape, BF16),
             pltpu.VMEM(dy_rows.shape, BF16),
             pltpu.VMEM(w_flat.shape, BF16),
             pltpu.VMEM(w_down.shape, BF16),
             pltpu.SMEM(counts.shape, jnp.int32),
+            pltpu.SMEM(assign.shape[::-1], jnp.int32),
             pltpu.VMEM((slots, width), F32),
             pltpu.SemaphoreType.DMA((copies,)),
         ],
@@ -359,7 +373,7 @@
             transcendentals=0,
         ),
         name="acts_and_rows",
-    )(x_rows, dy_rows, w_flat, w_down, counts)
+    )(*map(in_hbm, (x_rows, dy_rows, w_flat, w_down, counts, assign.T)))
 
     acts_all = [acts]
     swaps = [("mp", parts >> (i + 1)) for i in range(part_bits)]
@@ -389,7 +403,8 @@
                         [shape((2 * slots << step, width >> (step + 1)))],
                     )
                 )
-            results = run_tasks(tasks, "merge%d" % step)
+            names = ["rows%d", "acts%d", "columns%d"][-len(tasks) :] if step < dp_bits else ["rows%d"]
+            results = [run_tasks([t], n % step)[0] for t, n in zip(tasks, names)]
             if step < len(swaps):
                 keep, send = results[0]
         if step < len(swaps):
@@ -420,13 +435,13 @@
     )(*sent, *acts_all)
 
     grad_tokens = pl.pallas_call(
-        functools.partial(tokens_kernel, units, capacity),
+        tokens_kernel,
         out_shape=shape((assign.shape[0], share)),
-        in_specs=[IN_SMEM, IN_VMEM, IN_VMEM],
+        in_specs=[IN_VMEM] * 3,
         out_specs=IN_VMEM,
         compiler_params=params(),
         name="token_grads",
-    )(assign.T, keep, recv)
+    )(selector, keep, recv)
 
     grad_w_in = grad_in.reshape(2, hidden_units, quarter).transpose(2, 0, 1)[None]
     grad_w_out = grad_out.transpose(1, 0)[None]

time: 32.1 us -> 28.6 us (0.89)
  local copies, waits for them, and re-layouts: 4.02 us -> 0 us
  Pallas kernels: 9.45 us -> 9.96 us
    unnamed x10 -> x0, local copies, waits for them, and re-layouts: 4.02 us -> none
    pallas_call x1, Pallas kernels: 0.17 us -> 0.9 us  [per_device(): pl.pallas_call(functools.partial(split_kernel, dp_bits), out_shape=[shape...]
  transfers between devices with their start and end apart: 7 -> 7, of which waited for: 3 -> 3; matrix products, arithmetic and copies ran while one was open for 0% -> 0% of each run, Pallas kernels for 24% -> 27%
where the time goes in v4:
time: 28.6 us; the launch traced here: 28.4 us
  Pallas kernels  9.96 us (35%)
  starting transfers between devices  9.53 us (33%)
  waiting for transfers between devices  8.24 us (29%)
  between operations  0.67 us (2%)
    ppermute x7, starting transfers between devices, swap(): lax.ppermute(array, axis, [(i, i ^ bit) for i in range(lax.axis_size(axis...  9.53 us
    ppermute x7, waiting for transfers between devices, swap(): lax.ppermute(array, axis, [(i, i ^ bit) for i in range(lax.axis_size(axis...  8.24 us
    pallas_call x1, Pallas kernels, per_device(): pl.pallas_call(functools.partial(acts_kernel, units, parts), out_shape=[s...  6.79 us
    pallas_call x1, Pallas kernels, per_device(): pl.pallas_call(functools.partial(weights_kernel, dp_bits, width), out_sha...  1.49 us
    pallas_call x1, Pallas kernels, per_device(): pl.pallas_call(functools.partial(split_kernel, dp_bits), out_shape=[shape...  0.9 us
    pallas_call x1, Pallas kernels, per_device(): pl.pallas_call(tokens_kernel, out_shape=shape((assign.shape[0], share)),...  0.73 us
  transfers between devices with their start and end apart: 7, of which 3 were waited for; matrix products, arithmetic and copies ran while one was open for 0% of the time, Pallas kernels for 27%

profile of v4, /device:TPU:0, one launch (start us, length us, event | category | flops | bytes accessed | tf_op | source)
XLA Modules:
  0.0 28.4 jit_solution(13707975076273155749)
XLA Ops:
  0.6 0.9 %split_rows.1 = (bf16[32,1536]{1,0:T(8,128)(2,1)S(1)}, bf16[32,768]{1,0:T(8,128)(2,1)S(1)}, bf16[32,768]{1,0:T(8,128)(2,1)S(1)}) custom-call(bf16[16,3072]{1,0:T(8,128)(2,1)} %refs_0_.1, bf16[16,3072]{1,0:T(8,128)(2,1)} %refs_1_.1), custom_call_target="tpu_custom_call" | custom-call | bytes 524288 | tf_op jit(solution)/shard_map/split_rows/pallas_call | solution.py:333
  1.5 4.1 %collective-permute-start = (bf16[32,1536]{1,0:T(8,128)(2,1)S(1)}, bf16[32,1536]{1,0:T(8,128)(2,1)S(1)}, u32[]{:S(2)}, u32[]{:S(2)}) collective-permute-start(bf16[32,1536]{1,0:T(8,128)(2,1)S(1)} %get-tuple-element.17), channel_id=1, source_target_pairs={{0,16},{8,24},{16,0},{24,8},{1,17},{9,25},{17,1},{25,9},{2,18},{10... | collective-permute-start | bytes 294920 | tf_op jit(solution)/shard_map/ppermute | solution.py:318
  5.6 6.8 %acts_and_rows.1 = (bf16[16,1008]{1,0:T(8,128)(2,1)S(1)}, f32[16,1536]{1,0:T(8,128)S(1)}, bf16[16,1536]{1,0:T(8,128)(2,1)S(1)}, f32[4,16]{1,0:T(4,128)S(1)}) custom-call(bf16[16,3072]{1,0:T(8,128)(2,1)} %refs_0_.1, bf16[16,3072]{1,0:T(8,128)(2,1)} %refs_1_.1, bf16[672,3072]{1,0:T(8,128)(2,1)} %bitcast.17, bf16[336,3072]{1,0:T(8,128)(2,1)} %bitcast.18, ...), custom_call_target="tpu_custom_call" | custom-call | flops 2642411520 | bytes 6193152 | tf_op jit(solution)/shard_map/acts_and_rows/pallas_call | solution.py:349
  12.4 1.6 %collective-permute-start.4 = (bf16[16,1536]{1,0:T(8,128)(2,1)S(1)}, bf16[16,1536]{1,0:T(8,128)(2,1)S(1)}, u32[]{:S(2)}, u32[]{:S(2)}) collective-permute-start(bf16[16,1536]{1,0:T(8,128)(2,1)S(1)} %get-tuple-element.24), channel_id=1, source_target_pairs={{0,1},{1,0},{2,3},{3,2},{4,5},{5,4},{6,7},{7,6},{8,9},{9,8},{10,11... | collective-permute-start | bytes 147464 | tf_op jit(solution)/shard_map/ppermute | solution.py:318
  14.0 0.0 collective-permute-done.refs_1_
  14.0 1.6 %collective-permute-start.1 = (bf16[64,768]{1,0:T(8,128)(2,1)S(1)}, bf16[64,768]{1,0:T(8,128)(2,1)S(1)}, u32[]{:S(2)}, u32[]{:S(2)}) collective-permute-start(bf16[64,768]{1,0:T(8,128)(2,1)S(1)} %columns1.1), channel_id=1, source_target_pairs={{0,8},{8,0},{16,24},{24,16},{1,9},{9,1},{17,25},{25,17},{2,10},{10... | collective-permute-start | bytes 294920 | tf_op jit(solution)/shard_map/ppermute | solution.py:318
  15.7 0.3 %collective-permute-start.2 = (bf16[16,1008]{1,0:T(8,128)(2,1)S(1)}, bf16[16,1008]{1,0:T(8,128)(2,1)S(1)}, u32[]{:S(2)}, u32[]{:S(2)}) collective-permute-start(bf16[16,1008]{1,0:T(8,128)(2,1)S(1)} %get-tuple-element.19.refs_0_.refs_3_), channel_id=1, source_target_pairs={{0,16},{8,24},{16,0},{24,8},{1,17},{9,25},{17,1},{25,9},{2,18},{10... | collective-permute-start | bytes 96776 | tf_op jit(solution)/shard_map/ppermute | solution.py:318
  16.0 4.7 %collective-permute-done.2.refs_1_.refs_4_ = bf16[16,1008]{1,0:T(8,128)(2,1)S(1)} collective-permute-done((bf16[16,1008]{1,0:T(8,128)(2,1)S(1)}, bf16[16,1008]{1,0:T(8,128)(2,1)S(1)}, u32[]{:S(2)}, u32[]{:S(2)}) %collective-permute-start.2) | collective-permute-done | bytes 32288 | tf_op jit(solution)/shard_map/ppermute | solution.py:318
  20.7 0.2 collective-permute-start.3
  21.0 0.0 collective-permute-done.4.refs_1_
  21.0 1.6 %collective-permute-start.5 = (bf16[8,1536]{1,0:T(8,128)(2,1)S(1)}, bf16[8,1536]{1,0:T(8,128)(2,1)S(1)}, u32[]{:S(2)}, u32[]{:S(2)}) collective-permute-start(bf16[8,1536]{1,0:T(8,128)(2,1)S(1)} %get-tuple-element.26), channel_id=1, source_target_pairs={{0,4},{2,6},{4,0},{6,2},{1,5},{3,7},{5,1},{7,3},{8,12},{10,14},{12... | collective-permute-start | bytes 73736 | tf_op jit(solution)/shard_map/ppermute | solution.py:318
  22.6 2.3 %collective-permute-done.5.refs_1_ = bf16[8,1536]{1,0:T(8,128)(2,1)S(1)} collective-permute-done((bf16[8,1536]{1,0:T(8,128)(2,1)S(1)}, bf16[8,1536]{1,0:T(8,128)(2,1)S(1)}, u32[]{:S(2)}, u32[]{:S(2)}) %collective-permute-start.5) | collective-permute-done | bytes 24608 | tf_op jit(solution)/shard_map/ppermute | solution.py:318
  24.9 0.1 collective-permute-start.6
  25.0 1.2 %collective-permute-done.6.recv_ref = bf16[8,1536]{1,0:T(8,128)(2,1)S(1)} collective-permute-done((bf16[8,1536]{1,0:T(8,128)(2,1)S(1)}, bf16[8,1536]{1,0:T(8,128)(2,1)S(1)}, u32[]{:S(2)}, u32[]{:S(2)}) %collective-permute-start.6) | collective-permute-done | bytes 24608 | tf_op jit(solution)/shard_map/ppermute | solution.py:318
  26.2 0.7 %token_grads.1 = bf16[4,1536]{1,0:T(4,128)(2,1)} custom-call(f32[4,16]{1,0:T(4,128)S(1)} %get-tuple-element.22.selector_ref, f32[8,1536]{1,0:T(8,128)S(1)} %get-tuple-element.27.keep_ref, bf16[8,1536]{1,0:T(8,128)(2,1)S(1)} %collective-permute-done.6.recv_ref), custom_call_target="tpu_custom_call" | custom-call | tf_op jit(solution)/shard_map/token_grads/pallas_call | solution.py:437
  26.9 0.0 collective-permute-done.3.refs_5_
  26.9 0.0 collective-permute-done.1.refs_2_
  26.9 1.5 %weight_grads.1 = (bf16[672,768]{1,0:T(8,128)(2,1)}, bf16[336,768]{1,0:T(8,128)(2,1)}) custom-call(bf16[32,768]{1,0:T(8,128)(2,1)S(1)} %get-tuple-element.16.refs_0_, bf16[32,1536]{1,0:T(8,128)(2,1)S(1)} %collective-permute-done.refs_1_, bf16[64,768]{1,0:T(8,128)(2,1)S(1)} %collective-permute-done.1.refs_2_, ...), custom_call_target="tpu_custom_call" | custom-call | flops 396361728 | bytes 1548288 | tf_op jit(solution)/shard_map/weight_grads/pallas_call | solution.py:418
  (4 shorter events, 0.0 us)
Async XLA Ops:
  1.5 12.5 %collective-permute-start = (bf16[32,1536]{1,0:T(8,128)(2,1)S(1)}, bf16[32,1536]{1,0:T(8,128)(2,1)S(1)}, u32[]{:S(2)}, u32[]{:S(2)}) collective-permute-start(bf16[32,1536]{1,0:T(8,128)(2,1)S(1)} %get-tuple-element.17), channel_id=1, source_target_pairs={{0,16},{8,24},{16,0},{24,8},{1,17},{9,25},{17,1},{25,9},{2,18},{10... | collective-permute-start | bytes 294920 | tf_op jit(solution)/shard_map/ppermute | solution.py:318
  12.4 8.5 %collective-permute-start.4 = (bf16[16,1536]{1,0:T(8,128)(2,1)S(1)}, bf16[16,1536]{1,0:T(8,128)(2,1)S(1)}, u32[]{:S(2)}, u32[]{:S(2)}) collective-permute-start(bf16[16,1536]{1,0:T(8,128)(2,1)S(1)} %get-tuple-element.24), channel_id=1, source_target_pairs={{0,1},{1,0},{2,3},{3,2},{4,5},{5,4},{6,7},{7,6},{8,9},{9,8},{10,11... | collective-permute-start | bytes 147464 | tf_op jit(solution)/shard_map/ppermute | solution.py:318
  14.0 12.9 %collective-permute-start.1 = (bf16[64,768]{1,0:T(8,128)(2,1)S(1)}, bf16[64,768]{1,0:T(8,128)(2,1)S(1)}, u32[]{:S(2)}, u32[]{:S(2)}) collective-permute-start(bf16[64,768]{1,0:T(8,128)(2,1)S(1)} %columns1.1), channel_id=1, source_target_pairs={{0,8},{8,0},{16,24},{24,16},{1,9},{9,1},{17,25},{25,17},{2,10},{10... | collective-permute-start | bytes 294920 | tf_op jit(solution)/shard_map/ppermute | solution.py:318
  15.7 5.1 %collective-permute-start.2 = (bf16[16,1008]{1,0:T(8,128)(2,1)S(1)}, bf16[16,1008]{1,0:T(8,128)(2,1)S(1)}, u32[]{:S(2)}, u32[]{:S(2)}) collective-permute-start(bf16[16,1008]{1,0:T(8,128)(2,1)S(1)} %get-tuple-element.19.refs_0_.refs_3_), channel_id=1, source_target_pairs={{0,16},{8,24},{16,0},{24,8},{1,17},{9,25},{17,1},{25,9},{2,18},{10... | collective-permute-start | bytes 96776 | tf_op jit(solution)/shard_map/ppermute | solution.py:318
  20.7 6.2 %collective-permute-start.3 = (bf16[32,1008]{1,0:T(8,128)(2,1)S(1)}, bf16[32,1008]{1,0:T(8,128)(2,1)S(1)}, u32[]{:S(2)}, u32[]{:S(2)}) collective-permute-start(bf16[32,1008]{1,0:T(8,128)(2,1)S(1)} %acts1.1), channel_id=1, source_target_pairs={{0,8},{8,0},{16,24},{24,16},{1,9},{9,1},{17,25},{25,17},{2,10},{10... | collective-permute-start | bytes 193544 | tf_op jit(solution)/shard_map/ppermute | solution.py:318
  21.0 3.9 %collective-permute-start.5 = (bf16[8,1536]{1,0:T(8,128)(2,1)S(1)}, bf16[8,1536]{1,0:T(8,128)(2,1)S(1)}, u32[]{:S(2)}, u32[]{:S(2)}) collective-permute-start(bf16[8,1536]{1,0:T(8,128)(2,1)S(1)} %get-tuple-element.26), channel_id=1, source_target_pairs={{0,4},{2,6},{4,0},{6,2},{1,5},{3,7},{5,1},{7,3},{8,12},{10,14},{12... | collective-permute-start | bytes 73736 | tf_op jit(solution)/shard_map/ppermute | solution.py:318
  24.9 1.3 %collective-permute-start.6 = (bf16[8,1536]{1,0:T(8,128)(2,1)S(1)}, bf16[8,1536]{1,0:T(8,128)(2,1)S(1)}, u32[]{:S(2)}, u32[]{:S(2)}) collective-permute-start(bf16[8,1536]{1,0:T(8,128)(2,1)S(1)} %get-tuple-element.28), channel_id=1, source_target_pairs={{0,2},{2,0},{4,6},{6,4},{1,3},{3,1},{5,7},{7,5},{8,10},{10,8},{12,... | collective-permute-start | bytes 73736 | tf_op jit(solution)/shard_map/ppermute | solution.py:318

commit v5 on v4

--- a/solution.py
+++ b/solution.py
@@ -111,66 +111,109 @@
     return selector
 
 
+def unit_cuts(hidden_units):
+    cuts = [(at, min(128, hidden_units - at)) for at in range(0, hidden_units, 128)]
+    runs = [cuts[:1]] + [cuts[i : i + 2] for i in range(1, len(cuts), 2)]
+    return cuts, runs
+
+
 def acts_kernel(units, parts, *refs):
     x_hbm, dy_hbm, w_in_hbm, w_out_hbm, counts_hbm, assign_hbm = refs[:6]
     acts_ref, keep_ref, send_ref, selector_ref = refs[6:10]
     x_ref, dy_ref, w_in_ref, w_out_ref, counts_ref, assign_ref, rows_ref, sems = refs[10:]
 
     hidden_units, width = w_out_ref.shape
-    cuts = cuts_of(hidden_units, 128)
-    plan = [(counts_hbm, counts_ref), (x_hbm, x_ref), (dy_hbm, dy_ref)]
-    for at, size in cuts:
-        for half in range(2):
-            plan.append(
-                (
-                    w_in_hbm.at[pl.ds(half * hidden_units + at, size), :],
-                    w_in_ref.at[pl.ds(2 * at + half * size, size), :],
-                )
+    cuts, runs = unit_cuts(hidden_units)
+    used = []
+
+    def begin(source, target):
+        copy = pltpu.make_async_copy(source, target, sems.at[len(used)])
+        copy.start()
+        used.append(copy)
+        return copy
+
+    counts_copy = begin(counts_hbm, counts_ref)
+    x_copy = begin(x_hbm, x_ref)
+    in_copies, out_copies = [], []
+    dy_copy = None
+    for run in runs:
+        for at, size in run:
+            in_copies.append(
+                [
+                    begin(
+                        w_in_hbm.at[pl.ds(half * hidden_units + at, size), :],
+                        w_in_ref.at[pl.ds(2 * at + half * size, size), :],
+                    )
+                    for half in range(2)
+                ]
             )
-        plan.append((w_out_hbm.at[pl.ds(at, size), :], w_out_ref.at[pl.ds(at, size), :]))
-    plan.append((assign_hbm, assign_ref))
-    copies = [pltpu.make_async_copy(s, d, sems.at[i]) for i, (s, d) in enumerate(plan)]
-    for copy in copies:
-        copy.start()
-    copies = iter(copies)
+            if at == run[0][0]:
+                if dy_copy is None:
+                    dy_copy = begin(dy_hbm, dy_ref)
+                here = pl.ds(at, sum(n for _, n in run))
+                out_copies.append(begin(w_out_hbm.at[here, :], w_out_ref.at[here, :]))
+    assign_copy = begin(assign_hbm, assign_ref)
 
     slots = x_ref.shape[0]
     capacity = slots // counts_ref.shape[1]
     my_unit = lax.axis_index("expert")
-    next(copies).wait()
+    counts_copy.wait()
     pick = pick_matrix(counts_ref, slots, my_unit)
     back = pick.T.astype(BF16)
     pick = pick.astype(BF16)
-    next(copies).wait()
+    x_copy.wait()
     x = jnp.dot(pick, x_ref[...], preferred_element_type=F32).astype(BF16)
-    next(copies).wait()
-    dy = jnp.dot(pick, dy_ref[...], preferred_element_type=F32).astype(BF16)
+    dy = None
 
     gates, ups, hiddens = [], [], []
-    for at, size in cuts:
-        next(copies).wait()
-        next(copies).wait()
-        w_both = w_in_ref.at[pl.ds(2 * at, 2 * size), :]
-        pre = lax.dot_general(x, w_both[...], CONTRACT_LAST, preferred_element_type=F32)
-        next(copies).wait()
-        grad_hidden = lax.dot_general(
-            dy, w_out_ref[pl.ds(at, size), :], CONTRACT_LAST, preferred_element_type=F32
-        )
+
+    def add_rows(at, size, pre, grad_hidden):
         gate_pre, up_pre = pre[:, :size], pre[:, size:]
         sigmoid_gate = jax.nn.sigmoid(gate_pre)
         hidden = gate_pre * sigmoid_gate * up_pre
         grad_gate = grad_hidden * up_pre * sigmoid_gate * (1.0 + gate_pre * (1.0 - sigmoid_gate))
         grad_up = grad_hidden * gate_pre * sigmoid_gate
         grad_pre = jnp.concatenate([grad_gate, grad_up], axis=1).astype(BF16)
+        gates.append(grad_gate)
+        ups.append(grad_up)
+        hiddens.append(hidden)
         for left, count in cuts_of(width, 1024, 128):
             here = pl.ds(left, count)
-            part = jnp.dot(grad_pre, w_both[:, here], preferred_element_type=F32)
+            part = jnp.dot(
+                grad_pre, w_in_ref[pl.ds(2 * at, 2 * size), here], preferred_element_type=F32
+            )
             if at:
                 part = part + rows_ref[:, here]
             rows_ref[:, here] = part
-        gates.append(grad_gate)
-        ups.append(grad_up)
-        hiddens.append(hidden)
+
+    waiting = None
+    for run, out_copy in zip(runs, out_copies):
+        grad_hidden = None
+        for at, size in run:
+            for copy in in_copies.pop(0):
+                copy.wait()
+            pre = lax.dot_general(
+                x,
+                w_in_ref[pl.ds(2 * at, 2 * size), :],
+                CONTRACT_LAST,
+                preferred_element_type=F32,
+            )
+            if grad_hidden is None:
+                if dy is None:
+                    dy_copy.wait()
+                    dy = jnp.dot(pick, dy_ref[...], preferred_element_type=F32).astype(BF16)
+                out_copy.wait()
+                start, total = at, sum(n for _, n in run)
+                grad_hidden = lax.dot_general(
+                    dy,
+                    w_out_ref[pl.ds(start, total), :],
+                    CONTRACT_LAST,
+                    preferred_element_type=F32,
+                )
+            if waiting is not None:
+                add_rows(*waiting)
+            waiting = (at, size, pre, grad_hidden[:, at - start : at - start + size])
+    add_rows(*waiting)
     acts = jnp.concatenate(gates + ups + hiddens, axis=1).astype(BF16)
     acts_ref[...] = jnp.dot(back, acts, preferred_element_type=F32).astype(BF16)
 
@@ -180,7 +223,7 @@
     send_ref[...] = rows_ref[
         :, lanes(column_start(my_part, bits, 0, width, True), width // 2)
     ].astype(BF16)
-    next(copies).wait()
+    assign_copy.wait()
     selector_ref[...] = token_selector(assign_ref, units, capacity, my_unit)
 
 
@@ -239,37 +282,27 @@
     return body
 
 
-def run_tasks(tasks, name):
-    ins = [array for _, arrays, _ in tasks for array in arrays]
-    outs = [out for _, _, out_shapes in tasks for out in out_shapes]
+def run_whole(body, ins, outs, name, after=None):
+    extra = [] if after is None else [after]
 
     def kernel(*refs):
-        in_at, out_at = 0, len(ins)
-        for body, arrays, out_shapes in tasks:
-            body(
-                refs[in_at : in_at + len(arrays)],
-                refs[out_at : out_at + len(out_shapes)],
-            )
-            in_at += len(arrays)
-            out_at += len(out_shapes)
-
-    results = iter(
-        pl.pallas_call(
-            kernel,
-            out_shape=outs,
-            in_specs=[IN_VMEM] * len(ins),
-            out_specs=[IN_VMEM] * len(outs),
-            compiler_params=params(),
-            name=name,
-        )(*ins)
-    )
-    return [[next(results) for _ in out_shapes] for _, _, out_shapes in tasks]
+        body(refs[: len(ins)], refs[len(ins) + len(extra) :])
+
+    return pl.pallas_call(
+        kernel,
+        out_shape=outs,
+        in_specs=[IN_VMEM] * (len(ins) + len(extra)),
+        out_specs=[IN_VMEM] * len(outs),
+        compiler_params=params(),
+        name=name,
+    )(*ins, *extra)
 
 
 def weights_kernel(bits, width, *refs):
     count = 1 + bits
     sent, acts = refs[:count], refs[count : 2 * count]
-    in_hbm, out_hbm, in_ref, out_ref, sems = refs[2 * count :]
+    selector_ref, keep_ref, recv_ref = refs[2 * count : 2 * count + 3]
+    in_hbm, out_hbm, tokens_hbm, in_ref, out_ref, tokens_ref, sems = refs[2 * count + 3 :]
     slots = acts[0].shape[0]
     me = lax.axis_index("dp")
     quarter = width // 2**bits
@@ -286,6 +319,12 @@
     x, dy = jnp.concatenate(x, axis=0), jnp.concatenate(dy, axis=0)
     columns = jnp.concatenate([ref[...] for ref in acts], axis=0).T
     copies = []
+
+    def begin(source, target):
+        copy = pltpu.make_async_copy(source, target, sems.at[len(copies)])
+        copy.start()
+        copies.append(copy)
+
     start = 0
     for values, target, staged in ((x, in_hbm, in_ref), (dy, out_hbm, out_ref)):
         for at, size in cuts_of(target.shape[0]):
@@ -293,21 +332,15 @@
             staged[here, :] = jnp.dot(
                 columns[start + at : start + at + size], values, preferred_element_type=F32
             ).astype(BF16)
-            copy = pltpu.make_async_copy(
-                staged.at[here, :], target.at[here, :], sems.at[len(copies)]
-            )
-            copy.start()
-            copies.append(copy)
+            begin(staged.at[here, :], target.at[here, :])
         start += target.shape[0]
+    rows = jnp.concatenate([keep_ref[...].astype(F32), recv_ref[...].astype(F32)], axis=0)
+    tokens_ref[...] = jnp.dot(
+        selector_ref[...].astype(BF16), rows.astype(BF16), preferred_element_type=F32
+    ).astype(BF16)
+    begin(tokens_ref, tokens_hbm)
     for copy in copies:
         copy.wait()
-
-
-def tokens_kernel(selector_ref, keep_ref, recv_ref, out_ref):
-    rows = jnp.concatenate([keep_ref[...].astype(F32), recv_ref[...].astype(F32)], axis=0)
-    out_ref[...] = jnp.dot(
-        selector_ref[...].astype(BF16), rows.astype(BF16), preferred_element_type=F32
-    ).astype(BF16)
 
 
 def in_hbm(array):
@@ -345,7 +378,8 @@
 
     w_flat = jnp.transpose(w_in[0], (1, 2, 0)).reshape(2 * hidden_units, width)
     w_down = jnp.transpose(w_out[0], (1, 0))
-    copies = 4 + 3 * len(cuts_of(hidden_units, 128))
+    cuts, runs = unit_cuts(hidden_units)
+    copies = 4 + 2 * len(cuts) + len(runs)
     acts, keep, send, selector = pl.pallas_call(
         functools.partial(acts_kernel, units, parts),
         out_shape=[
@@ -380,50 +414,54 @@
     swaps += [("expert", units >> (i + 1)) for i in range(unit_bits)]
     rows_held = slots
     for step in range(max(len(swaps), dp_bits)):
-        tasks = []
-        if step > 0:
-            if step < len(swaps):
-                if step < part_bits:
-                    body = sum_task(part_bits, step - 1, width)
-                    out = (slots, width >> (step + 1))
-                elif step == part_bits:
-                    body = sum_task(part_bits, step - 1, width)
-                    out = (slots // 2, share)
-                else:
-                    past = step - part_bits
-                    body = deal_task(owners >> past, capacity << (past - 1))
-                    out = (slots // 2, share)
-                tasks.append((body, [keep, recv], [shape(out, F32), shape(out)]))
-            if step < dp_bits:
-                tasks.append((stack_task, acts_all, [shape((slots << step, 3 * hidden_units))]))
-                tasks.append(
-                    (
-                        columns_task(dp_bits, step, width),
-                        [split[step]] + sent[1:],
-                        [shape((2 * slots << step, width >> (step + 1)))],
-                    )
-                )
-            names = ["rows%d", "acts%d", "columns%d"][-len(tasks) :] if step < dp_bits else ["rows%d"]
-            results = [run_tasks([t], n % step)[0] for t, n in zip(tasks, names)]
-            if step < len(swaps):
-                keep, send = results[0]
+        if 0 < step < dp_bits:
+            (columns,) = run_whole(
+                columns_task(dp_bits, step, width),
+                [split[step]] + sent[1:],
+                [shape((2 * slots << step, width >> (step + 1)))],
+                "columns%d" % step,
+                after=recv,
+            )
+            sent.append(swap(columns, "dp", groups >> (step + 1)))
+        if 0 < step < len(swaps):
+            if step <= part_bits:
+                body = sum_task(part_bits, step - 1, width)
+                out = (slots, width >> (step + 1)) if step < part_bits else (slots // 2, share)
+            else:
+                past = step - part_bits
+                body = deal_task(owners >> past, capacity << (past - 1))
+                out = (slots // 2, share)
+            keep, send = run_whole(body, [keep, recv], [shape(out, F32), shape(out)], "rows%d" % step)
         if step < len(swaps):
             recv = swap(send, *swaps[step])
         if step < dp_bits:
-            bit = groups >> (step + 1)
-            acts_all.append(swap(acts if step == 0 else results[-2][0], "dp", bit))
+            held = acts
             if step > 0:
-                sent.append(swap(results[-1][0], "dp", bit))
-
-    grad_in, grad_out = pl.pallas_call(
+                (held,) = run_whole(
+                    stack_task,
+                    acts_all,
+                    [shape((slots << step, 3 * hidden_units))],
+                    "acts%d" % step,
+                    after=keep,
+                )
+            acts_all.append(swap(held, "dp", groups >> (step + 1)))
+
+    grad_in, grad_out, grad_tokens = pl.pallas_call(
         functools.partial(weights_kernel, dp_bits, width),
-        out_shape=[shape((2 * hidden_units, quarter)), shape((hidden_units, quarter))],
-        in_specs=[IN_VMEM] * (2 + 2 * dp_bits),
-        out_specs=[ANY, ANY],
+        out_shape=[
+            shape((2 * hidden_units, quarter)),
+            shape((hidden_units, quarter)),
+            shape((assign.shape[0], share)),
+        ],
+        in_specs=[IN_VMEM] * (5 + 2 * dp_bits),
+        out_specs=[ANY] * 3,
         scratch_shapes=[
             pltpu.VMEM((2 * hidden_units, quarter), BF16),
             pltpu.VMEM((hidden_units, quarter), BF16),
-            pltpu.SemaphoreType.DMA((len(cuts_of(2 * hidden_units)) + len(cuts_of(hidden_units)),)),
+            pltpu.VMEM((assign.shape[0], share), BF16),
+            pltpu.SemaphoreType.DMA(
+                (1 + len(cuts_of(2 * hidden_units)) + len(cuts_of(hidden_units)),)
+            ),
         ],
         compiler_params=params(),
         cost_estimate=pl.CostEstimate(
@@ -431,17 +469,8 @@
             bytes_accessed=6 * hidden_units * quarter,
             transcendentals=0,
         ),
-        name="weight_grads",
-    )(*sent, *acts_all)
-
-    grad_tokens = pl.pallas_call(
-        tokens_kernel,
-        out_shape=shape((assign.shape[0], share)),
-        in_specs=[IN_VMEM] * 3,
-        out_specs=IN_VMEM,
-        compiler_params=params(),
-        name="token_grads",
-    )(selector, keep, recv)
+        name="weight_and_token_grads",
+    )(*sent, *acts_all, selector, keep, recv)
 
     grad_w_in = grad_in.reshape(2, hidden_units, quarter).transpose(2, 0, 1)[None]
     grad_w_out = grad_out.transpose(1, 0)[None]

time: 28.6 us -> 29.4 us (1.028)
  waiting for transfers between devices: 8.24 us -> 10.8 us
  Pallas kernels: 9.96 us -> 8.28 us
    ppermute x7, waiting for transfers between devices: 8.24 us -> 10.8 us  [swap(): lax.ppermute(array, axis, [(i, i ^ bit) for i in range(lax.axis_size(axis...]
    pallas_call x1, Pallas kernels: 6.79 us -> 5.85 us  [per_device(): pl.pallas_call(functools.partial(acts_kernel, units, parts), out_shape=[s...]
    pallas_call x5 -> x4, Pallas kernels: 0.77 us -> 0.04 us  [run_whole(): pl.pallas_call(kernel, out_shape=outs, in_specs=[IN_VMEM] * (len(ins) + l...]
  transfers between devices with their start and end apart: 7 -> 7, of which waited for: 3 -> 4; matrix products, arithmetic and copies ran while one was open for 0% -> 0% of each run, Pallas kernels for 27% -> 20%
where the time goes in v5:
time: 29.4 us; the launch traced here: 29.2 us
  waiting for transfers between devices  10.8 us (37%)
  starting transfers between devices  9.43 us (32%)
  Pallas kernels  8.28 us (28%)
  between operations  0.67 us (2%)
    ppermute x7, waiting for transfers between devices, swap(): lax.ppermute(array, axis, [(i, i ^ bit) for i in range(lax.axis_size(axis...  10.8 us
    ppermute x7, starting transfers between devices, swap(): lax.ppermute(array, axis, [(i, i ^ bit) for i in range(lax.axis_size(axis...  9.43 us
    pallas_call x1, Pallas kernels, per_device(): pl.pallas_call(functools.partial(acts_kernel, units, parts), out_shape=[s...  5.85 us
    pallas_call x1, Pallas kernels, per_device(): pl.pallas_call(functools.partial(weights_kernel, dp_bits, width), out_sha...  1.48 us
    pallas_call x1, Pallas kernels, per_device(): pl.pallas_call(functools.partial(split_kernel, dp_bits), out_shape=[shape...  0.9 us
  transfers between devices with their start and end apart: 7, of which 4 were waited for; matrix products, arithmetic and copies ran while one was open for 0% of the time, Pallas kernels for 20%

profile of v5, /device:TPU:0, one launch (start us, length us, event | category | flops | bytes accessed | tf_op | source)
XLA Modules:
  0.0 29.2 jit_solution(4660332893453157790)
XLA Ops:
  0.6 0.9 %split_rows.1 = (bf16[32,1536]{1,0:T(8,128)(2,1)S(1)}, bf16[32,768]{1,0:T(8,128)(2,1)S(1)}, bf16[32,768]{1,0:T(8,128)(2,1)S(1)}) custom-call(bf16[16,3072]{1,0:T(8,128)(2,1)} %refs_0_.1, bf16[16,3072]{1,0:T(8,128)(2,1)} %refs_1_.1), custom_call_target="tpu_custom_call" | custom-call | bytes 524288 | tf_op jit(solution)/shard_map/split_rows/pallas_call | solution.py:366
  1.5 4.1 %collective-permute-start = (bf16[32,1536]{1,0:T(8,128)(2,1)S(1)}, bf16[32,1536]{1,0:T(8,128)(2,1)S(1)}, u32[]{:S(2)}, u32[]{:S(2)}) collective-permute-start(bf16[32,1536]{1,0:T(8,128)(2,1)S(1)} %get-tuple-element.18), channel_id=1, source_target_pairs={{0,16},{8,24},{16,0},{24,8},{1,17},{9,25},{17,1},{25,9},{2,18},{10... | collective-permute-start | bytes 294920 | tf_op jit(solution)/shard_map/ppermute | solution.py:351
  5.6 5.9 %acts_and_rows.1 = (bf16[16,1008]{1,0:T(8,128)(2,1)S(1)}, f32[16,1536]{1,0:T(8,128)S(1)}, bf16[16,1536]{1,0:T(8,128)(2,1)S(1)}, f32[4,16]{1,0:T(4,128)S(1)}) custom-call(bf16[16,3072]{1,0:T(8,128)(2,1)} %refs_0_.1, bf16[16,3072]{1,0:T(8,128)(2,1)} %refs_1_.1, bf16[672,3072]{1,0:T(8,128)(2,1)} %bitcast.17, bf16[336,3072]{1,0:T(8,128)(2,1)} %bitcast.18, ...), custom_call_target="tpu_custom_call" | custom-call | flops 2642411520 | bytes 6193152 | tf_op jit(solution)/shard_map/acts_and_rows/pallas_call | solution.py:383
  11.5 1.6 %collective-permute-start.1 = (bf16[16,1536]{1,0:T(8,128)(2,1)S(1)}, bf16[16,1536]{1,0:T(8,128)(2,1)S(1)}, u32[]{:S(2)}, u32[]{:S(2)}) collective-permute-start(bf16[16,1536]{1,0:T(8,128)(2,1)S(1)} %get-tuple-element.20), channel_id=1, source_target_pairs={{0,1},{1,0},{2,3},{3,2},{4,5},{5,4},{6,7},{7,6},{8,9},{9,8},{10,11... | collective-permute-start | bytes 147464 | tf_op jit(solution)/shard_map/ppermute | solution.py:351
  13.1 2.6 %collective-permute-done.1.refs_2_.refs_1_ = bf16[16,1536]{1,0:T(8,128)(2,1)S(1)} collective-permute-done((bf16[16,1536]{1,0:T(8,128)(2,1)S(1)}, bf16[16,1536]{1,0:T(8,128)(2,1)S(1)}, u32[]{:S(2)}, u32[]{:S(2)}) %collective-permute-start.1) | collective-permute-done | bytes 49184 | tf_op jit(solution)/shard_map/ppermute | solution.py:351
  15.7 0.0 collective-permute-done.refs_1_
  15.7 1.6 %collective-permute-start.2 = (bf16[64,768]{1,0:T(8,128)(2,1)S(1)}, bf16[64,768]{1,0:T(8,128)(2,1)S(1)}, u32[]{:S(2)}, u32[]{:S(2)}) collective-permute-start(bf16[64,768]{1,0:T(8,128)(2,1)S(1)} %columns1.1), channel_id=1, source_target_pairs={{0,8},{8,0},{16,24},{24,16},{1,9},{9,1},{17,25},{25,17},{2,10},{10... | collective-permute-start | bytes 294920 | tf_op jit(solution)/shard_map/ppermute | solution.py:351
  17.3 0.3 %collective-permute-start.3 = (bf16[16,1008]{1,0:T(8,128)(2,1)S(1)}, bf16[16,1008]{1,0:T(8,128)(2,1)S(1)}, u32[]{:S(2)}, u32[]{:S(2)}) collective-permute-start(bf16[16,1008]{1,0:T(8,128)(2,1)S(1)} %get-tuple-element.21.refs_0_.refs_3_), channel_id=1, source_target_pairs={{0,16},{8,24},{16,0},{24,8},{1,17},{9,25},{17,1},{25,9},{2,18},{10... | collective-permute-start | bytes 96776 | tf_op jit(solution)/shard_map/ppermute | solution.py:351
  17.7 4.7 %collective-permute-done.3.refs_1_.refs_4_ = bf16[16,1008]{1,0:T(8,128)(2,1)S(1)} collective-permute-done((bf16[16,1008]{1,0:T(8,128)(2,1)S(1)}, bf16[16,1008]{1,0:T(8,128)(2,1)S(1)}, u32[]{:S(2)}, u32[]{:S(2)}) %collective-permute-start.3) | collective-permute-done | bytes 32288 | tf_op jit(solution)/shard_map/ppermute | solution.py:351
  22.4 0.2 collective-permute-start.4
  22.6 1.5 %collective-permute-start.5 = (bf16[8,1536]{1,0:T(8,128)(2,1)S(1)}, bf16[8,1536]{1,0:T(8,128)(2,1)S(1)}, u32[]{:S(2)}, u32[]{:S(2)}) collective-permute-start(bf16[8,1536]{1,0:T(8,128)(2,1)S(1)} %get-tuple-element.25), channel_id=1, source_target_pairs={{0,4},{2,6},{4,0},{6,2},{1,5},{3,7},{5,1},{7,3},{8,12},{10,14},{12... | collective-permute-start | bytes 73736 | tf_op jit(solution)/shard_map/ppermute | solution.py:351
  24.1 2.3 %collective-permute-done.5.refs_1_ = bf16[8,1536]{1,0:T(8,128)(2,1)S(1)} collective-permute-done((bf16[8,1536]{1,0:T(8,128)(2,1)S(1)}, bf16[8,1536]{1,0:T(8,128)(2,1)S(1)}, u32[]{:S(2)}, u32[]{:S(2)}) %collective-permute-start.5) | collective-permute-done | bytes 24608 | tf_op jit(solution)/shard_map/ppermute | solution.py:351
  26.5 0.1 collective-permute-start.6
  26.5 1.2 %collective-permute-done.6.refs_8_ = bf16[8,1536]{1,0:T(8,128)(2,1)S(1)} collective-permute-done((bf16[8,1536]{1,0:T(8,128)(2,1)S(1)}, bf16[8,1536]{1,0:T(8,128)(2,1)S(1)}, u32[]{:S(2)}, u32[]{:S(2)}) %collective-permute-start.6) | collective-permute-done | bytes 24608 | tf_op jit(solution)/shard_map/ppermute | solution.py:351
  27.7 0.0 collective-permute-done.4.refs_5_
  27.7 0.0 collective-permute-done.2.refs_2_
  27.7 1.5 %weight_and_token_grads.1 = (bf16[672,768]{1,0:T(8,128)(2,1)}, bf16[336,768]{1,0:T(8,128)(2,1)}, bf16[4,1536]{1,0:T(4,128)(2,1)}) custom-call(bf16[32,768]{1,0:T(8,128)(2,1)S(1)} %get-tuple-element.17.refs_0_, bf16[32,1536]{1,0:T(8,128)(2,1)S(1)} %collective-permute-done.refs_1_, bf16[64,768]{1,0:T(8,128)(2,1)S(1)} %collective-permute-done.2.refs_2_, ...), custom_call_target="tpu_custom_call" | custom-call | flops 396361728 | bytes 1548288 | tf_op jit(solution)/shard_map/weight_and_token_grads/pallas_call | solution.py:449
  (4 shorter events, 0.0 us)
Async XLA Ops:
  1.5 14.1 %collective-permute-start = (bf16[32,1536]{1,0:T(8,128)(2,1)S(1)}, bf16[32,1536]{1,0:T(8,128)(2,1)S(1)}, u32[]{:S(2)}, u32[]{:S(2)}) collective-permute-start(bf16[32,1536]{1,0:T(8,128)(2,1)S(1)} %get-tuple-element.18), channel_id=1, source_target_pairs={{0,16},{8,24},{16,0},{24,8},{1,17},{9,25},{17,1},{25,9},{2,18},{10... | collective-permute-start | bytes 294920 | tf_op jit(solution)/shard_map/ppermute | solution.py:351
  11.5 4.2 %collective-permute-start.1 = (bf16[16,1536]{1,0:T(8,128)(2,1)S(1)}, bf16[16,1536]{1,0:T(8,128)(2,1)S(1)}, u32[]{:S(2)}, u32[]{:S(2)}) collective-permute-start(bf16[16,1536]{1,0:T(8,128)(2,1)S(1)} %get-tuple-element.20), channel_id=1, source_target_pairs={{0,1},{1,0},{2,3},{3,2},{4,5},{5,4},{6,7},{7,6},{8,9},{9,8},{10,11... | collective-permute-start | bytes 147464 | tf_op jit(solution)/shard_map/ppermute | solution.py:351
  15.7 12.0 %collective-permute-start.2 = (bf16[64,768]{1,0:T(8,128)(2,1)S(1)}, bf16[64,768]{1,0:T(8,128)(2,1)S(1)}, u32[]{:S(2)}, u32[]{:S(2)}) collective-permute-start(bf16[64,768]{1,0:T(8,128)(2,1)S(1)} %columns1.1), channel_id=1, source_target_pairs={{0,8},{8,0},{16,24},{24,16},{1,9},{9,1},{17,25},{25,17},{2,10},{10... | collective-permute-start | bytes 294920 | tf_op jit(solution)/shard_map/ppermute | solution.py:351
  17.3 5.1 %collective-permute-start.3 = (bf16[16,1008]{1,0:T(8,128)(2,1)S(1)}, bf16[16,1008]{1,0:T(8,128)(2,1)S(1)}, u32[]{:S(2)}, u32[]{:S(2)}) collective-permute-start(bf16[16,1008]{1,0:T(8,128)(2,1)S(1)} %get-tuple-element.21.refs_0_.refs_3_), channel_id=1, source_target_pairs={{0,16},{8,24},{16,0},{24,8},{1,17},{9,25},{17,1},{25,9},{2,18},{10... | collective-permute-start | bytes 96776 | tf_op jit(solution)/shard_map/ppermute | solution.py:351
  22.4 5.3 %collective-permute-start.4 = (bf16[32,1008]{1,0:T(8,128)(2,1)S(1)}, bf16[32,1008]{1,0:T(8,128)(2,1)S(1)}, u32[]{:S(2)}, u32[]{:S(2)}) collective-permute-start(bf16[32,1008]{1,0:T(8,128)(2,1)S(1)} %acts1.1), channel_id=1, source_target_pairs={{0,8},{8,0},{16,24},{24,16},{1,9},{9,1},{17,25},{25,17},{2,10},{10... | collective-permute-start | bytes 193544 | tf_op jit(solution)/shard_map/ppermute | solution.py:351
  22.6 3.8 %collective-permute-start.5 = (bf16[8,1536]{1,0:T(8,128)(2,1)S(1)}, bf16[8,1536]{1,0:T(8,128)(2,1)S(1)}, u32[]{:S(2)}, u32[]{:S(2)}) collective-permute-start(bf16[8,1536]{1,0:T(8,128)(2,1)S(1)} %get-tuple-element.25), channel_id=1, source_target_pairs={{0,4},{2,6},{4,0},{6,2},{1,5},{3,7},{5,1},{7,3},{8,12},{10,14},{12... | collective-permute-start | bytes 73736 | tf_op jit(solution)/shard_map/ppermute | solution.py:351
  26.5 1.3 %collective-permute-start.6 = (bf16[8,1536]{1,0:T(8,128)(2,1)S(1)}, bf16[8,1536]{1,0:T(8,128)(2,1)S(1)}, u32[]{:S(2)}, u32[]{:S(2)}) collective-permute-start(bf16[8,1536]{1,0:T(8,128)(2,1)S(1)} %get-tuple-element.27), channel_id=1, source_target_pairs={{0,2},{2,0},{4,6},{6,4},{1,3},{3,1},{5,7},{7,5},{8,10},{10,8},{12,... | collective-permute-start | bytes 73736 | tf_op jit(solution)/shard_map/ppermute | solution.py:351

commit v6 on v5

--- a/solution.py
+++ b/solution.py
@@ -35,6 +35,10 @@
     size = -(-rows // pieces)
     size = -(-size // unit) * unit
     return [(at, min(size, rows - at)) for at in range(0, rows, size)]
+
+
+def step_cuts(rows):
+    return [(at, min(256, rows - at)) for at in range(0, rows, 256)]
 
 
 def column_start(me, bits, step, width, flipped):
@@ -111,19 +115,11 @@
     return selector
 
 
-def unit_cuts(hidden_units):
-    cuts = [(at, min(128, hidden_units - at)) for at in range(0, hidden_units, 128)]
-    runs = [cuts[:1]] + [cuts[i : i + 2] for i in range(1, len(cuts), 2)]
-    return cuts, runs
-
-
-def acts_kernel(units, parts, *refs):
+def forward_kernel(units, *refs):
     x_hbm, dy_hbm, w_in_hbm, w_out_hbm, counts_hbm, assign_hbm = refs[:6]
-    acts_ref, keep_ref, send_ref, selector_ref = refs[6:10]
-    x_ref, dy_ref, w_in_ref, w_out_ref, counts_ref, assign_ref, rows_ref, sems = refs[10:]
-
-    hidden_units, width = w_out_ref.shape
-    cuts, runs = unit_cuts(hidden_units)
+    acts_ref, grad_ref, selector_ref, w_in_ref = refs[6:10]
+    x_ref, dy_ref, w_out_ref, counts_ref, assign_ref, sems = refs[10:]
+    hidden_units = w_out_ref.shape[0]
     used = []
 
     def begin(source, target):
@@ -133,25 +129,17 @@
         return copy
 
     counts_copy = begin(counts_hbm, counts_ref)
+    dy_copy = begin(dy_hbm, dy_ref)
     x_copy = begin(x_hbm, x_ref)
-    in_copies, out_copies = [], []
-    dy_copy = None
-    for run in runs:
-        for at, size in run:
-            in_copies.append(
-                [
-                    begin(
-                        w_in_hbm.at[pl.ds(half * hidden_units + at, size), :],
-                        w_in_ref.at[pl.ds(2 * at + half * size, size), :],
-                    )
-                    for half in range(2)
-                ]
-            )
-            if at == run[0][0]:
-                if dy_copy is None:
-                    dy_copy = begin(dy_hbm, dy_ref)
-                here = pl.ds(at, sum(n for _, n in run))
-                out_copies.append(begin(w_out_hbm.at[here, :], w_out_ref.at[here, :]))
+    out_cuts, cuts = step_cuts(hidden_units), step_cuts(2 * hidden_units)
+    out_copies = [
+        begin(w_out_hbm.at[pl.ds(at, size), :], w_out_ref.at[pl.ds(at, size), :])
+        for at, size in out_cuts
+    ]
+    in_copies = [
+        begin(w_in_hbm.at[pl.ds(at, size), :], w_in_ref.at[pl.ds(at, size), :])
+        for at, size in cuts
+    ]
     assign_copy = begin(assign_hbm, assign_ref)
 
     slots = x_ref.shape[0]
@@ -161,70 +149,51 @@
     pick = pick_matrix(counts_ref, slots, my_unit)
     back = pick.T.astype(BF16)
     pick = pick.astype(BF16)
+    dy_copy.wait()
+    dy = jnp.dot(pick, dy_ref[...], preferred_element_type=F32).astype(BF16)
     x_copy.wait()
     x = jnp.dot(pick, x_ref[...], preferred_element_type=F32).astype(BF16)
-    dy = None
-
-    gates, ups, hiddens = [], [], []
-
-    def add_rows(at, size, pre, grad_hidden):
-        gate_pre, up_pre = pre[:, :size], pre[:, size:]
-        sigmoid_gate = jax.nn.sigmoid(gate_pre)
-        hidden = gate_pre * sigmoid_gate * up_pre
-        grad_gate = grad_hidden * up_pre * sigmoid_gate * (1.0 + gate_pre * (1.0 - sigmoid_gate))
-        grad_up = grad_hidden * gate_pre * sigmoid_gate
-        grad_pre = jnp.concatenate([grad_gate, grad_up], axis=1).astype(BF16)
-        gates.append(grad_gate)
-        ups.append(grad_up)
-        hiddens.append(hidden)
-        for left, count in cuts_of(width, 1024, 128):
-            here = pl.ds(left, count)
-            part = jnp.dot(
-                grad_pre, w_in_ref[pl.ds(2 * at, 2 * size), here], preferred_element_type=F32
-            )
-            if at:
-                part = part + rows_ref[:, here]
-            rows_ref[:, here] = part
-
-    waiting = None
-    for run, out_copy in zip(runs, out_copies):
-        grad_hidden = None
-        for at, size in run:
-            for copy in in_copies.pop(0):
-                copy.wait()
-            pre = lax.dot_general(
-                x,
-                w_in_ref[pl.ds(2 * at, 2 * size), :],
-                CONTRACT_LAST,
-                preferred_element_type=F32,
-            )
-            if grad_hidden is None:
-                if dy is None:
-                    dy_copy.wait()
-                    dy = jnp.dot(pick, dy_ref[...], preferred_element_type=F32).astype(BF16)
-                out_copy.wait()
-                start, total = at, sum(n for _, n in run)
-                grad_hidden = lax.dot_general(
-                    dy,
-                    w_out_ref[pl.ds(start, total), :],
+
+    def product(rows, weights_ref, pieces, copies):
+        found = []
+        for (at, size), copy in zip(pieces, copies):
+            copy.wait()
+            found.append(
+                lax.dot_general(
+                    rows,
+                    weights_ref[pl.ds(at, size), :],
                     CONTRACT_LAST,
                     preferred_element_type=F32,
                 )
-            if waiting is not None:
-                add_rows(*waiting)
-            waiting = (at, size, pre, grad_hidden[:, at - start : at - start + size])
-    add_rows(*waiting)
-    acts = jnp.concatenate(gates + ups + hiddens, axis=1).astype(BF16)
+            )
+        return jnp.concatenate(found, axis=1)
+
+    grad_hidden = product(dy, w_out_ref, out_cuts, out_copies)
+    pre = product(x, w_in_ref, cuts, in_copies)
+    gate_pre, up_pre = pre[:, :hidden_units], pre[:, hidden_units:]
+    sigmoid_gate = jax.nn.sigmoid(gate_pre)
+    hidden = gate_pre * sigmoid_gate * up_pre
+    grad_gate = grad_hidden * up_pre * sigmoid_gate * (1.0 + gate_pre * (1.0 - sigmoid_gate))
+    grad_up = grad_hidden * gate_pre * sigmoid_gate
+    acts = jnp.concatenate([grad_gate, grad_up, hidden], axis=1).astype(BF16)
     acts_ref[...] = jnp.dot(back, acts, preferred_element_type=F32).astype(BF16)
-
+    grad_ref[...] = acts[:, : 2 * hidden_units]
+    assign_copy.wait()
+    selector_ref[...] = token_selector(assign_ref, units, capacity, my_unit)
+
+
+def rows_kernel(parts, grad_ref, w_in_ref, keep_ref, send_ref, rows_ref):
+    width = w_in_ref.shape[1]
+    for at, size in cuts_of(width, 1024, 128):
+        rows_ref[:, pl.ds(at, size)] = jnp.dot(
+            grad_ref[...], w_in_ref[:, pl.ds(at, size)], preferred_element_type=F32
+        )
     my_part = lax.axis_index("mp")
     bits = bits_of(parts)
     keep_ref[...] = rows_ref[:, lanes(column_start(my_part, bits, 0, width, False), width // 2)]
     send_ref[...] = rows_ref[
         :, lanes(column_start(my_part, bits, 0, width, True), width // 2)
     ].astype(BF16)
-    assign_copy.wait()
-    selector_ref[...] = token_selector(assign_ref, units, capacity, my_unit)
 
 
 def sum_task(bits, step, width):
@@ -301,8 +270,7 @@
 def weights_kernel(bits, width, *refs):
     count = 1 + bits
     sent, acts = refs[:count], refs[count : 2 * count]
-    selector_ref, keep_ref, recv_ref = refs[2 * count : 2 * count + 3]
-    in_hbm, out_hbm, tokens_hbm, in_ref, out_ref, tokens_ref, sems = refs[2 * count + 3 :]
+    in_hbm, out_hbm, in_ref, out_ref, sems = refs[2 * count :]
     slots = acts[0].shape[0]
     me = lax.axis_index("dp")
     quarter = width // 2**bits
@@ -334,13 +302,15 @@
             ).astype(BF16)
             begin(staged.at[here, :], target.at[here, :])
         start += target.shape[0]
+    for copy in copies:
+        copy.wait()
+
+
+def tokens_kernel(selector_ref, keep_ref, recv_ref, out_ref):
     rows = jnp.concatenate([keep_ref[...].astype(F32), recv_ref[...].astype(F32)], axis=0)
-    tokens_ref[...] = jnp.dot(
+    out_ref[...] = jnp.dot(
         selector_ref[...].astype(BF16), rows.astype(BF16), preferred_element_type=F32
     ).astype(BF16)
-    begin(tokens_ref, tokens_hbm)
-    for copy in copies:
-        copy.wait()
 
 
 def in_hbm(array):
@@ -378,36 +348,53 @@
 
     w_flat = jnp.transpose(w_in[0], (1, 2, 0)).reshape(2 * hidden_units, width)
     w_down = jnp.transpose(w_out[0], (1, 0))
-    cuts, runs = unit_cuts(hidden_units)
-    copies = 4 + 2 * len(cuts) + len(runs)
-    acts, keep, send, selector = pl.pallas_call(
-        functools.partial(acts_kernel, units, parts),
+    acts, grad_pre, selector, w_kept = pl.pallas_call(
+        functools.partial(forward_kernel, units),
         out_shape=[
-            shape((slots, 3 * hidden_units)),
-            shape((slots, width // 2), F32),
-            shape((slots, width // 2)),
-            shape((assign.shape[0], slots), F32),
+            pltpu.VMEM((slots, 3 * hidden_units), BF16),
+            pltpu.VMEM((slots, 2 * hidden_units), BF16),
+            pltpu.VMEM((assign.shape[0], slots), F32),
+            pltpu.VMEM(w_flat.shape, BF16),
         ],
         in_specs=[IN_HBM] * 6,
         out_specs=[IN_VMEM] * 4,
         scratch_shapes=[
             pltpu.VMEM(x_rows.shape, BF16),
             pltpu.VMEM(dy_rows.shape, BF16),
-            pltpu.VMEM(w_flat.shape, BF16),
             pltpu.VMEM(w_down.shape, BF16),
             pltpu.SMEM(counts.shape, jnp.int32),
             pltpu.SMEM(assign.shape[::-1], jnp.int32),
-            pltpu.VMEM((slots, width), F32),
-            pltpu.SemaphoreType.DMA((copies,)),
+            pltpu.SemaphoreType.DMA(
+                (4 + len(step_cuts(hidden_units)) + len(step_cuts(2 * hidden_units)),)
+            ),
         ],
         compiler_params=params(),
         cost_estimate=pl.CostEstimate(
-            flops=2 * 256 * width * 5 * hidden_units,
+            flops=2 * 256 * width * 3 * hidden_units,
             bytes_accessed=6 * hidden_units * width,
             transcendentals=0,
         ),
-        name="acts_and_rows",
-    )(*map(in_hbm, (x_rows, dy_rows, w_flat, w_down, counts, assign.T)))
+        name="forward",
+    )(
+        in_hbm(x_rows),
+        in_hbm(dy_rows),
+        in_hbm(w_flat),
+        in_hbm(w_down),
+        in_hbm(counts),
+        in_hbm(assign.T),
+    )
+    keep, send = pl.pallas_call(
+        functools.partial(rows_kernel, parts),
+        out_shape=[shape((slots, width // 2), F32), shape((slots, width // 2))],
+        in_specs=[IN_VMEM] * 2,
+        out_specs=[IN_VMEM] * 2,
+        scratch_shapes=[pltpu.VMEM((slots, width), F32)],
+        compiler_params=params(),
+        cost_estimate=pl.CostEstimate(
+            flops=2 * slots * width * 2 * hidden_units, bytes_accessed=0, transcendentals=0
+        ),
+        name="row_grads",
+    )(grad_pre, w_kept)
 
     acts_all = [acts]
     swaps = [("mp", parts >> (i + 1)) for i in range(part_bits)]
@@ -420,7 +407,7 @@
                 [split[step]] + sent[1:],
                 [shape((2 * slots << step, width >> (step + 1)))],
                 "columns%d" % step,
-                after=recv,
+                after=acts_all[-1],
             )
             sent.append(swap(columns, "dp", groups >> (step + 1)))
         if 0 < step < len(swaps):
@@ -442,25 +429,22 @@
                     acts_all,
                     [shape((slots << step, 3 * hidden_units))],
                     "acts%d" % step,
-                    after=keep,
                 )
             acts_all.append(swap(held, "dp", groups >> (step + 1)))
 
-    grad_in, grad_out, grad_tokens = pl.pallas_call(
+    grad_in, grad_out = pl.pallas_call(
         functools.partial(weights_kernel, dp_bits, width),
         out_shape=[
             shape((2 * hidden_units, quarter)),
             shape((hidden_units, quarter)),
-            shape((assign.shape[0], share)),
         ],
-        in_specs=[IN_VMEM] * (5 + 2 * dp_bits),
-        out_specs=[ANY] * 3,
+        in_specs=[IN_VMEM] * (2 + 2 * dp_bits),
+        out_specs=[ANY] * 2,
         scratch_shapes=[
             pltpu.VMEM((2 * hidden_units, quarter), BF16),
             pltpu.VMEM((hidden_units, quarter), BF16),
-            pltpu.VMEM((assign.shape[0], share), BF16),
             pltpu.SemaphoreType.DMA(
-                (1 + len(cuts_of(2 * hidden_units)) + len(cuts_of(hidden_units)),)
+                (len(cuts_of(2 * hidden_units)) + len(cuts_of(hidden_units)),)
             ),
         ],
         compiler_params=params(),
@@ -469,8 +453,17 @@
             bytes_accessed=6 * hidden_units * quarter,
             transcendentals=0,
         ),
-        name="weight_and_token_grads",
-    )(*sent, *acts_all, selector, keep, recv)
+        name="weight_grads",
+    )(*sent, *acts_all)
+
+    grad_tokens = pl.pallas_call(
+        tokens_kernel,
+        out_shape=shape((assign.shape[0], share)),
+        in_specs=[IN_VMEM] * 3,
+        out_specs=IN_VMEM,
+        compiler_params=params(),
+        name="token_grads",
+    )(selector, keep, recv)
 
     grad_w_in = grad_in.reshape(2, hidden_units, quarter).transpose(2, 0, 1)[None]
     grad_w_out = grad_out.transpose(1, 0)[None]

time: 29.4 us -> 25.9 us (0.88)
  waiting for transfers between devices: 10.8 us -> 5.75 us
  Pallas kernels: 8.28 us -> 9.51 us
  starting transfers between devices: 9.43 us -> 9.81 us
    ppermute x7, waiting for transfers between devices: 10.8 us -> 5.75 us  [swap(): lax.ppermute(array, axis, [(i, i ^ bit) for i in range(lax.axis_size(axis...]
    pallas_call x1 -> x3, Pallas kernels: 5.85 us -> 7.08 us  [the longest x1 5.69 us: per_device(): pl.pallas_call(functools.partial(forward_kernel, units), out_shape=[pltpu...]
    ppermute x7, starting transfers between devices: 9.43 us -> 9.81 us  [swap(): lax.ppermute(array, axis, [(i, i ^ bit) for i in range(lax.axis_size(axis...]
  transfers between devices with their start and end apart: 7 -> 7, of which waited for: 4 -> 3; matrix products, arithmetic and copies ran while one was open for 0% -> 0% of each run, Pallas kernels for 20% -> 28%
where the time goes in v6:
time: 25.9 us; the launch traced here: 25.7 us
  starting transfers between devices  9.81 us (38%)
  Pallas kernels  9.51 us (37%)
  waiting for transfers between devices  5.75 us (22%)
  between operations  0.68 us (3%)
    ppermute x7, starting transfers between devices, swap(): lax.ppermute(array, axis, [(i, i ^ bit) for i in range(lax.axis_size(axis...  9.81 us
    ppermute x7, waiting for transfers between devices, swap(): lax.ppermute(array, axis, [(i, i ^ bit) for i in range(lax.axis_size(axis...  5.75 us
    pallas_call x1, Pallas kernels, per_device(): pl.pallas_call(functools.partial(forward_kernel, units), out_shape=[pltpu...  5.69 us
    pallas_call x1, Pallas kernels, per_device(): pl.pallas_call(functools.partial(weights_kernel, dp_bits, width), out_sha...  1.49 us
    pallas_call x1, Pallas kernels, per_device(): pl.pallas_call(functools.partial(split_kernel, dp_bits), out_shape=[shape...  0.9 us
    pallas_call x1, Pallas kernels, per_device(): pl.pallas_call(tokens_kernel, out_shape=shape((assign.shape[0], share)),...  0.73 us
    pallas_call x1, Pallas kernels, per_device(): pl.pallas_call(functools.partial(rows_kernel, parts), out_shape=[shape((s...  0.66 us
  transfers between devices with their start and end apart: 7, of which 3 were waited for; matrix products, arithmetic and copies ran while one was open for 0% of the time, Pallas kernels for 28%

profile of v6, /device:TPU:0, one launch (start us, length us, event | category | flops | bytes accessed | tf_op | source)
XLA Modules:
  0.0 25.7 jit_solution(10943203043174188531)
XLA Ops:
  0.6 0.9 %split_rows.1 = (bf16[32,1536]{1,0:T(8,128)(2,1)S(1)}, bf16[32,768]{1,0:T(8,128)(2,1)S(1)}, bf16[32,768]{1,0:T(8,128)(2,1)S(1)}) custom-call(bf16[16,3072]{1,0:T(8,128)(2,1)} %refs_0_.1, bf16[16,3072]{1,0:T(8,128)(2,1)} %refs_1_.1), custom_call_target="tpu_custom_call" | custom-call | bytes 524288 | tf_op jit(solution)/shard_map/split_rows/pallas_call | solution.py:336
  1.5 4.1 %collective-permute-start = (bf16[32,1536]{1,0:T(8,128)(2,1)S(1)}, bf16[32,1536]{1,0:T(8,128)(2,1)S(1)}, u32[]{:S(2)}, u32[]{:S(2)}) collective-permute-start(bf16[32,1536]{1,0:T(8,128)(2,1)S(1)} %get-tuple-element.19), channel_id=1, source_target_pairs={{0,16},{8,24},{16,0},{24,8},{1,17},{9,25},{17,1},{25,9},{2,18},{10... | collective-permute-start | bytes 294920 | tf_op jit(solution)/shard_map/ppermute | solution.py:321
  5.6 5.7 %forward.1 = (bf16[16,1008]{1,0:T(8,128)(2,1)S(1)}, bf16[16,672]{1,0:T(8,128)(2,1)S(1)}, f32[4,16]{1,0:T(4,128)S(1)}, bf16[672,3072]{1,0:T(8,128)(2,1)S(1)}) custom-call(bf16[16,3072]{1,0:T(8,128)(2,1)} %refs_0_.1, bf16[16,3072]{1,0:T(8,128)(2,1)} %refs_1_.1, bf16[672,3072]{1,0:T(8,128)(2,1)} %bitcast.17, bf16[336,3072]{1,0:T(8,128)(2,1)} %bitcast.18, ...), custom_call_target="tpu_custom_call" | custom-call | flops 1585446912 | bytes 6193152 | tf_op jit(solution)/shard_map/forward/pallas_call | solution.py:351
  11.3 0.1 collective-permute-start.1
  11.4 0.7 %row_grads.1 = (f32[16,1536]{1,0:T(8,128)S(1)}, bf16[16,1536]{1,0:T(8,128)(2,1)S(1)}) custom-call(bf16[16,672]{1,0:T(8,128)(2,1)S(1)} %get-tuple-element.25.grad_ref, bf16[672,3072]{1,0:T(8,128)(2,1)S(1)} %get-tuple-element.26.w_in_ref), custom_call_target="tpu_custom_call" | custom-call | flops 66060288 | tf_op jit(solution)/shard_map/row_grads/pallas_call | solution.py:386
  12.1 1.9 %collective-permute-start.4 = (bf16[16,1536]{1,0:T(8,128)(2,1)S(1)}, bf16[16,1536]{1,0:T(8,128)(2,1)S(1)}, u32[]{:S(2)}, u32[]{:S(2)}) collective-permute-start(bf16[16,1536]{1,0:T(8,128)(2,1)S(1)} %get-tuple-element.28), channel_id=1, source_target_pairs={{0,1},{1,0},{2,3},{3,2},{4,5},{5,4},{6,7},{7,6},{8,9},{9,8},{10,11... | collective-permute-start | bytes 147464 | tf_op jit(solution)/shard_map/ppermute | solution.py:321
  14.0 2.2 %collective-permute-done.1.refs_2_.refs_1_.refs_4_ = bf16[16,1008]{1,0:T(8,128)(2,1)S(1)} collective-permute-done((bf16[16,1008]{1,0:T(8,128)(2,1)S(1)}, bf16[16,1008]{1,0:T(8,128)(2,1)S(1)}, u32[]{:S(2)}, u32[]{:S(2)}) %collective-permute-start.1) | collective-permute-done | bytes 32288 | tf_op jit(solution)/shard_map/ppermute | solution.py:321
  16.2 0.0 collective-permute-done.refs_1_
  16.2 1.6 %collective-permute-start.2 = (bf16[64,768]{1,0:T(8,128)(2,1)S(1)}, bf16[64,768]{1,0:T(8,128)(2,1)S(1)}, u32[]{:S(2)}, u32[]{:S(2)}) collective-permute-start(bf16[64,768]{1,0:T(8,128)(2,1)S(1)} %columns1.1), channel_id=1, source_target_pairs={{0,8},{8,0},{16,24},{24,16},{1,9},{9,1},{17,25},{25,17},{2,10},{10... | collective-permute-start | bytes 294920 | tf_op jit(solution)/shard_map/ppermute | solution.py:321
  17.9 0.4 %collective-permute-start.3 = (bf16[32,1008]{1,0:T(8,128)(2,1)S(1)}, bf16[32,1008]{1,0:T(8,128)(2,1)S(1)}, u32[]{:S(2)}, u32[]{:S(2)}) collective-permute-start(bf16[32,1008]{1,0:T(8,128)(2,1)S(1)} %acts1.1), channel_id=1, source_target_pairs={{0,8},{8,0},{16,24},{24,16},{1,9},{9,1},{17,25},{25,17},{2,10},{10... | collective-permute-start | bytes 193544 | tf_op jit(solution)/shard_map/ppermute | solution.py:321
  18.3 0.0 collective-permute-done.4.refs_1_
  18.4 1.6 %collective-permute-start.5 = (bf16[8,1536]{1,0:T(8,128)(2,1)S(1)}, bf16[8,1536]{1,0:T(8,128)(2,1)S(1)}, u32[]{:S(2)}, u32[]{:S(2)}) collective-permute-start(bf16[8,1536]{1,0:T(8,128)(2,1)S(1)} %get-tuple-element.30), channel_id=1, source_target_pairs={{0,4},{2,6},{4,0},{6,2},{1,5},{3,7},{5,1},{7,3},{8,12},{10,14},{12... | collective-permute-start | bytes 73736 | tf_op jit(solution)/shard_map/ppermute | solution.py:321
  19.9 2.3 %collective-permute-done.5.refs_1_ = bf16[8,1536]{1,0:T(8,128)(2,1)S(1)} collective-permute-done((bf16[8,1536]{1,0:T(8,128)(2,1)S(1)}, bf16[8,1536]{1,0:T(8,128)(2,1)S(1)}, u32[]{:S(2)}, u32[]{:S(2)}) %collective-permute-start.5) | collective-permute-done | bytes 24608 | tf_op jit(solution)/shard_map/ppermute | solution.py:321
  22.3 0.1 collective-permute-start.6
  22.3 1.2 %collective-permute-done.6.recv_ref = bf16[8,1536]{1,0:T(8,128)(2,1)S(1)} collective-permute-done((bf16[8,1536]{1,0:T(8,128)(2,1)S(1)}, bf16[8,1536]{1,0:T(8,128)(2,1)S(1)}, u32[]{:S(2)}, u32[]{:S(2)}) %collective-permute-start.6) | collective-permute-done | bytes 24608 | tf_op jit(solution)/shard_map/ppermute | solution.py:321
  23.5 0.7 %token_grads.1 = bf16[4,1536]{1,0:T(4,128)(2,1)} custom-call(f32[4,16]{1,0:T(4,128)S(1)} %get-tuple-element.24.selector_ref, f32[8,1536]{1,0:T(8,128)S(1)} %get-tuple-element.31.keep_ref, bf16[8,1536]{1,0:T(8,128)(2,1)S(1)} %collective-permute-done.6.recv_ref), custom_call_target="tpu_custom_call" | custom-call | tf_op jit(solution)/shard_map/token_grads/pallas_call | solution.py:459
  24.3 0.0 collective-permute-done.3.refs_5_
  24.3 0.0 collective-permute-done.2.refs_2_
  24.3 1.5 %weight_grads.1 = (bf16[672,768]{1,0:T(8,128)(2,1)}, bf16[336,768]{1,0:T(8,128)(2,1)}) custom-call(bf16[32,768]{1,0:T(8,128)(2,1)S(1)} %get-tuple-element.18.refs_0_, bf16[32,1536]{1,0:T(8,128)(2,1)S(1)} %collective-permute-done.refs_1_, bf16[64,768]{1,0:T(8,128)(2,1)S(1)} %collective-permute-done.2.refs_2_, ...), custom_call_target="tpu_custom_call" | custom-call | flops 396361728 | bytes 1548288 | tf_op jit(solution)/shard_map/weight_grads/pallas_call | solution.py:435
  (4 shorter events, 0.0 us)
Async XLA Ops:
  1.5 14.7 %collective-permute-start = (bf16[32,1536]{1,0:T(8,128)(2,1)S(1)}, bf16[32,1536]{1,0:T(8,128)(2,1)S(1)}, u32[]{:S(2)}, u32[]{:S(2)}) collective-permute-start(bf16[32,1536]{1,0:T(8,128)(2,1)S(1)} %get-tuple-element.19), channel_id=1, source_target_pairs={{0,16},{8,24},{16,0},{24,8},{1,17},{9,25},{17,1},{25,9},{2,18},{10... | collective-permute-start | bytes 294920 | tf_op jit(solution)/shard_map/ppermute | solution.py:321
  11.3 4.9 %collective-permute-start.1 = (bf16[16,1008]{1,0:T(8,128)(2,1)S(1)}, bf16[16,1008]{1,0:T(8,128)(2,1)S(1)}, u32[]{:S(2)}, u32[]{:S(2)}) collective-permute-start(bf16[16,1008]{1,0:T(8,128)(2,1)S(1)} %get-tuple-element.21.refs_0_.refs_3_), channel_id=1, source_target_pairs={{0,16},{8,24},{16,0},{24,8},{1,17},{9,25},{17,1},{25,9},{2,18},{10... | collective-permute-start | bytes 96776 | tf_op jit(solution)/shard_map/ppermute | solution.py:321
  12.1 6.2 %collective-permute-start.4 = (bf16[16,1536]{1,0:T(8,128)(2,1)S(1)}, bf16[16,1536]{1,0:T(8,128)(2,1)S(1)}, u32[]{:S(2)}, u32[]{:S(2)}) collective-permute-start(bf16[16,1536]{1,0:T(8,128)(2,1)S(1)} %get-tuple-element.28), channel_id=1, source_target_pairs={{0,1},{1,0},{2,3},{3,2},{4,5},{5,4},{6,7},{7,6},{8,9},{9,8},{10,11... | collective-permute-start | bytes 147464 | tf_op jit(solution)/shard_map/ppermute | solution.py:321
  16.2 8.0 %collective-permute-start.2 = (bf16[64,768]{1,0:T(8,128)(2,1)S(1)}, bf16[64,768]{1,0:T(8,128)(2,1)S(1)}, u32[]{:S(2)}, u32[]{:S(2)}) collective-permute-start(bf16[64,768]{1,0:T(8,128)(2,1)S(1)} %columns1.1), channel_id=1, source_target_pairs={{0,8},{8,0},{16,24},{24,16},{1,9},{9,1},{17,25},{25,17},{2,10},{10... | collective-permute-start | bytes 294920 | tf_op jit(solution)/shard_map/ppermute | solution.py:321
  17.9 6.4 %collective-permute-start.3 = (bf16[32,1008]{1,0:T(8,128)(2,1)S(1)}, bf16[32,1008]{1,0:T(8,128)(2,1)S(1)}, u32[]{:S(2)}, u32[]{:S(2)}) collective-permute-start(bf16[32,1008]{1,0:T(8,128)(2,1)S(1)} %acts1.1), channel_id=1, source_target_pairs={{0,8},{8,0},{16,24},{24,16},{1,9},{9,1},{17,25},{25,17},{2,10},{10... | collective-permute-start | bytes 193544 | tf_op jit(solution)/shard_map/ppermute | solution.py:321
  18.4 3.9 %collective-permute-start.5 = (bf16[8,1536]{1,0:T(8,128)(2,1)S(1)}, bf16[8,1536]{1,0:T(8,128)(2,1)S(1)}, u32[]{:S(2)}, u32[]{:S(2)}) collective-permute-start(bf16[8,1536]{1,0:T(8,128)(2,1)S(1)} %get-tuple-element.30), channel_id=1, source_target_pairs={{0,4},{2,6},{4,0},{6,2},{1,5},{3,7},{5,1},{7,3},{8,12},{10,14},{12... | collective-permute-start | bytes 73736 | tf_op jit(solution)/shard_map/ppermute | solution.py:321
  22.3 1.3 %collective-permute-start.6 = (bf16[8,1536]{1,0:T(8,128)(2,1)S(1)}, bf16[8,1536]{1,0:T(8,128)(2,1)S(1)}, u32[]{:S(2)}, u32[]{:S(2)}) collective-permute-start(bf16[8,1536]{1,0:T(8,128)(2,1)S(1)} %get-tuple-element.32), channel_id=1, source_target_pairs={{0,2},{2,0},{4,6},{6,4},{1,3},{3,1},{5,7},{7,5},{8,10},{10,8},{12,... | collective-permute-start | bytes 73736 | tf_op jit(solution)/shard_map/ppermute | solution.py:321
